TPU v7x, 32 devices: a whole 2x2x4 slice. The times are simulated.
32 devices in a mesh: seq: 8 (over y, x, core), grp: 4 (over z).
Axes of the slice: x: 2, y: 2, z: 4, core: 2. Of those that a mesh axis runs over, the one named last changes fastest.
Arguments:
- tokens: bfloat16 [8192, 2048], P(('seq', 'grp')), may hold values from -6 to 6
- first_gain: bfloat16 [2048], P('seq'), may hold values from 0.5 to 1.5
- first_bias: bfloat16 [2048], P('seq'), may hold values from -1 to 1
- query_weight: bfloat16 [2048, 2048], P('seq', 'grp'), may hold values from -0.125 to 0.125
- key_weight: bfloat16 [2048, 2048], P('seq', 'grp'), may hold values from -0.125 to 0.125
- value_weight: bfloat16 [2048, 4096], P('seq', 'grp'), may hold values from -0.125 to 0.125
- gate_weight: bfloat16 [2048, 4096], P('seq', 'grp'), may hold values from -0.125 to 0.125
- group_gain: bfloat16 [512, 8], P('seq', 'grp'), may hold values from 0.5 to 1.5
- group_bias: bfloat16 [512, 8], P('seq', 'grp'), may hold values from -1 to 1
- out_weight: bfloat16 [4096, 2048], P('seq'), may hold values from -0.1875 to 0.1875
- second_gain: bfloat16 [2048], P('seq'), may hold values from 0.5 to 1.5
- second_bias: bfloat16 [2048], P('seq'), may hold values from -1 to 1
- up_weight: bfloat16 [2048, 4096], P('seq'), may hold values from -0.125 to 0.125
- up_bias: bfloat16 [4096], P('seq'), may hold values from -1 to 1
- down_weight: bfloat16 [4096, 2048], P('seq'), may hold values from -0.125 to 0.125
- down_bias: bfloat16 [2048], P('seq'), may hold values from -1 to 1
- cotangent: bfloat16 [8192, 2048], P(('seq', 'grp')), may hold values from -6 to 6
- doc_lengths: int32 [3], replicated, may hold values from 1024 to 4096, as said below
- windows: int32 [4], P('grp'), may hold values from 512 to 1024
Outputs:
- mixed: bfloat16 [8192, 2048], P(('seq', 'grp'))
- tokens_grad: bfloat16 [8192, 2048], P(('seq', 'grp'))
- first_gain_grad: float32 [2048], P('seq')
- first_bias_grad: float32 [2048], P('seq')
- query_grad: float32 [2048, 2048], P('seq', 'grp')
- key_grad: float32 [2048, 2048], P('seq', 'grp')
- value_grad: float32 [2048, 4096], P('seq', 'grp')
- gate_grad: float32 [2048, 4096], P('seq', 'grp')
- group_gain_grad: float32 [512, 8], P('seq', 'grp')
- group_bias_grad: float32 [512, 8], P('seq', 'grp')
- out_grad: float32 [4096, 2048], P('seq')
- second_gain_grad: float32 [2048], P('seq')
- second_bias_grad: float32 [2048], P('seq')
- up_grad: float32 [2048, 4096], P('seq')
- up_bias_grad: float32 [4096], P('seq')
- down_grad: float32 [4096, 2048], P('seq')
- down_bias_grad: float32 [2048], P('seq')
Inputs may be any that keep to these rules, and one draw needn't show every extreme that they name: `doc_lengths`: the 3 documents fill the 8192 tokens in order; each is 1024 tokens or more and exactly one is 4096 long.
All inputs are finite; a program needn't handle non-finite values.
Results may differ from a plain program's by a relative error of at most 0.023.
Values may be sent and summed in bfloat16 or wider, within the bound.
No kernel may reach another device: no remote copies, remote signals or barrier semaphores. Data moves between devices by JAX's collectives and lax.ppermute only.
A program may use at most 384 MiB of HBM per device.

v0:
```python
from functools import partial

import jax
import jax.numpy as jnp
from jax import lax
from jax.sharding import PartitionSpec as P

KD = 256
VD = 512
STRETCH = 512


EPSILON = 1e-05


def shifted(shard, axis, by):
    devices = lax.axis_size(axis)
    pairs = [(i, i + by) for i in range(devices) if 0 <= i + by < devices]
    return lax.ppermute(shard, axis, pairs)


def layer_norm(values, gain, bias):
    center = values - jnp.mean(values, axis=-1, keepdims=True)
    spread = jnp.mean(center * center, axis=-1, keepdims=True)
    return center * lax.rsqrt(spread + EPSILON) * gain + bias


def document_table(doc_lengths, positions):
    ends = jnp.cumsum(doc_lengths, dtype=jnp.int32)
    after = (positions[:, None] >= ends[None, :]).astype(jnp.int32)
    documents = jnp.sum(after, axis=1, dtype=jnp.int32)
    starts = jnp.sum(after * doc_lengths[None, :], axis=1, dtype=jnp.int32)
    return (documents, positions - starts)


def rotary_table(places, width):
    half = width // 2
    freqs = 10000.0 ** (-jnp.arange(half, dtype=jnp.float32) / (half - 1))
    angles = places.astype(jnp.float32)[:, None] * freqs[None, :]
    cosine = jnp.cos(angles)
    sine = jnp.sin(angles)
    return (jnp.concatenate([cosine, cosine], axis=1), jnp.concatenate([sine, sine], axis=1))


def rotate(values, cosine, sine):
    half = values.shape[-1] // 2
    turned = jnp.concatenate([-values[..., half:], values[..., :half]], axis=-1)
    return values * cosine[:, None, :] + turned * sine[:, None, :]


def decay_mask(query_pos, key_pos, query_doc, key_doc, log_decay, window):
    distance = query_pos[:, None] - key_pos[None, :]
    inside = (distance >= 0) & (query_doc[:, None] == key_doc[None, :]) & (key_pos[None, :] >= 0)
    inside = inside[None] & (distance[None] < window[:, None, None])
    steps = jnp.where(inside, distance[None], 0).astype(jnp.float32)
    return jnp.where(inside, jnp.exp(steps * log_decay[:, None, None]), 0.0)


def gate_norm(retained, gate_pre, gain, bias):
    center = retained - jnp.mean(retained, axis=-1, keepdims=True)
    spread = jnp.mean(center * center, axis=-1, keepdims=True)
    grouped = center * lax.rsqrt(spread + EPSILON) * gain.T[None] + bias.T[None]
    return jax.nn.silu(gate_pre) * grouped.reshape(retained.shape[0], -1)


def body(
    tokens,
    first_gain,
    first_bias,
    query_weight,
    key_weight,
    value_weight,
    gate_weight,
    group_gain,
    group_bias,
    out_weight,
    second_gain,
    second_bias,
    up_weight,
    up_bias,
    down_weight,
    down_bias,
    cotangent,
    doc_lengths,
    windows,
):
    (
        query_full,
        key_full,
        value_full,
        gate_full,
        group_gain_full,
        group_bias_full,
        gain_one_full,
        bias_one_full,
    ) = (
        lax.all_gather(query_weight, "seq", axis=0, tiled=True),
        lax.all_gather(key_weight, "seq", axis=0, tiled=True),
        lax.all_gather(value_weight, "seq", axis=0, tiled=True),
        lax.all_gather(gate_weight, "seq", axis=0, tiled=True),
        lax.all_gather(group_gain, "seq", axis=0, tiled=True),
        lax.all_gather(group_bias, "seq", axis=0, tiled=True),
        lax.all_gather(first_gain, "seq", axis=0, tiled=True),
        lax.all_gather(first_bias, "seq", axis=0, tiled=True),
    )
    inputs = tokens.astype(jnp.float32)
    gain_one = gain_one_full.astype(jnp.float32)
    bias_one = bias_one_full.astype(jnp.float32)
    normed = layer_norm(inputs, gain_one, bias_one).astype(jnp.bfloat16)
    gathered = lax.all_gather(normed, "grp", axis=0, tiled=True)
    rows = gathered.shape[0]
    heads = query_full.shape[1] // KD
    seq_index = lax.axis_index("seq")
    group_index = lax.axis_index("grp")
    positions = seq_index * rows + jnp.arange(rows, dtype=jnp.int32)
    documents, places = document_table(doc_lengths, positions)
    key_positions = seq_index * rows - rows + jnp.arange(2 * rows, dtype=jnp.int32)
    key_documents = document_table(doc_lengths, key_positions)[0]
    cosine, sine = rotary_table(places, KD)
    query_pre = jnp.dot(gathered, query_full, preferred_element_type=jnp.float32).reshape(
        rows, heads, KD
    )
    key_pre = jnp.dot(gathered, key_full, preferred_element_type=jnp.float32).reshape(
        rows, heads, KD
    )
    values = jnp.dot(gathered, value_full, preferred_element_type=jnp.float32).astype(jnp.bfloat16)
    values = values.reshape(rows, heads, VD)
    gate_pre = jnp.dot(gathered, gate_full, preferred_element_type=jnp.float32)
    key_scale = KD ** (-0.5)
    queries = rotate(query_pre, cosine, sine).astype(jnp.bfloat16)
    keys = (rotate(key_pre, cosine, sine) * key_scale).astype(jnp.bfloat16)
    prior_keys, prior_values = shifted((keys, values), "seq", 1)
    all_keys = jnp.concatenate([prior_keys, keys], axis=0)
    all_values = jnp.concatenate([prior_values, values], axis=0)
    head_index = (group_index * heads + jnp.arange(heads, dtype=jnp.int32)).astype(jnp.float32)
    log_decay = jnp.log1p(-jnp.exp2(-5.0 - head_index))
    window = jnp.broadcast_to(windows, (heads,))
    span = rows + STRETCH

    def block_mask(start):
        return decay_mask(
            positions[start : start + STRETCH],
            key_positions[start : start + span],
            documents[start : start + STRETCH],
            key_documents[start : start + span],
            log_decay,
            window,
        )

    pieces = []
    for start in range(0, rows, STRETCH):
        mask = block_mask(start)
        scores = jnp.einsum(
            "qhd,khd->hqk",
            queries[start : start + STRETCH],
            all_keys[start : start + span],
            preferred_element_type=jnp.float32,
        )
        weights = (scores * mask).astype(jnp.bfloat16)
        pieces.append(
            jnp.einsum(
                "hqk,khe->qhe",
                weights,
                all_values[start : start + span],
                preferred_element_type=jnp.float32,
            )
        )
    retained = jnp.concatenate(pieces, axis=0)
    group_gain_f = group_gain_full.astype(jnp.float32)
    group_bias_f = group_bias_full.astype(jnp.float32)
    heads_out = gate_norm(retained, gate_pre, group_gain_f, group_bias_f).astype(jnp.bfloat16)
    by_token = lax.all_to_all(heads_out, "grp", split_axis=0, concat_axis=1, tiled=True)
    out_full, up_full, down_full, up_bias_full, down_bias_full, gain_two_full, bias_two_full = (
        lax.all_gather(out_weight, "seq", axis=0, tiled=True),
        lax.all_gather(up_weight, "seq", axis=0, tiled=True),
        lax.all_gather(down_weight, "seq", axis=0, tiled=True),
        lax.all_gather(up_bias, "seq", axis=0, tiled=True),
        lax.all_gather(down_bias, "seq", axis=0, tiled=True),
        lax.all_gather(second_gain, "seq", axis=0, tiled=True),
        lax.all_gather(second_bias, "seq", axis=0, tiled=True),
    )
    gain_two = gain_two_full.astype(jnp.float32)
    bias_two = bias_two_full.astype(jnp.float32)
    hidden = inputs + jnp.dot(by_token, out_full, preferred_element_type=jnp.float32)
    normed_two = layer_norm(hidden, gain_two, bias_two).astype(jnp.bfloat16)
    pre_act = jnp.dot(
        normed_two, up_full, preferred_element_type=jnp.float32
    ) + up_bias_full.astype(jnp.float32)
    activated = jax.nn.gelu(pre_act, approximate=False).astype(jnp.bfloat16)
    mixed = (
        hidden
        + jnp.dot(activated, down_full, preferred_element_type=jnp.float32)
        + down_bias_full.astype(jnp.float32)
    ).astype(jnp.bfloat16)
    out_full, up_full, down_full = (
        lax.all_gather(out_weight, "seq", axis=0, tiled=True),
        lax.all_gather(up_weight, "seq", axis=0, tiled=True),
        lax.all_gather(down_weight, "seq", axis=0, tiled=True),
    )
    grad_out = cotangent.astype(jnp.float32)
    down_bias_part = jnp.sum(grad_out, axis=0)
    down_part = jnp.dot(activated.T, cotangent, preferred_element_type=jnp.float32)
    grad_act = jnp.dot(cotangent, down_full.T, preferred_element_type=jnp.float32)
    gelu_back = jax.vjp(partial(jax.nn.gelu, approximate=False), pre_act)[1]
    grad_pre = gelu_back(grad_act)[0].astype(jnp.bfloat16)
    up_bias_part = jnp.sum(grad_pre.astype(jnp.float32), axis=0)
    up_part = jnp.dot(normed_two.T, grad_pre, preferred_element_type=jnp.float32)
    grad_normed_two = jnp.dot(grad_pre, up_full.T, preferred_element_type=jnp.float32)
    second_back = jax.vjp(layer_norm, hidden, gain_two, bias_two)[1]
    hidden_part, gain_two_part, bias_two_part = second_back(grad_normed_two)
    grad_hidden = grad_out + hidden_part
    grad_attend = grad_hidden.astype(jnp.bfloat16)
    out_part = jnp.dot(by_token.T, grad_attend, preferred_element_type=jnp.float32)
    grad_by_token = jnp.dot(grad_attend, out_full.T, preferred_element_type=jnp.float32).astype(
        jnp.bfloat16
    )
    grad_heads = lax.all_to_all(grad_by_token, "grp", split_axis=1, concat_axis=0, tiled=True)
    gate_back = jax.vjp(gate_norm, retained, gate_pre, group_gain_f, group_bias_f)[1]
    grad_retained, grad_gate, group_gain_part, group_bias_part = gate_back(
        grad_heads.astype(jnp.float32)
    )
    grad_retained = grad_retained.astype(jnp.bfloat16)
    grad_gate = grad_gate.astype(jnp.bfloat16)
    key_sums = jnp.zeros((2 * rows, heads, KD), jnp.float32)
    value_sums = jnp.zeros((2 * rows, heads, VD), jnp.float32)
    query_parts = []
    for start in range(0, rows, STRETCH):
        mask = block_mask(start)
        block_queries = queries[start : start + STRETCH]
        block_keys = all_keys[start : start + span]
        block_values = all_values[start : start + span]
        block_grad = grad_retained[start : start + STRETCH]
        scores = jnp.einsum(
            "qhd,khd->hqk", block_queries, block_keys, preferred_element_type=jnp.float32
        )
        weights = (scores * mask).astype(jnp.bfloat16)
        grad_weights = jnp.einsum(
            "qhe,khe->hqk", block_grad, block_values, preferred_element_type=jnp.float32
        )
        grad_scores = (grad_weights * mask).astype(jnp.bfloat16)
        value_sums = value_sums.at[start : start + span].add(
            jnp.einsum("hqk,qhe->khe", weights, block_grad, preferred_element_type=jnp.float32)
        )
        key_sums = key_sums.at[start : start + span].add(
            jnp.einsum(
                "hqk,qhd->khd", grad_scores, block_queries, preferred_element_type=jnp.float32
            )
        )
        query_parts.append(
            jnp.einsum("hqk,khd->qhd", grad_scores, block_keys, preferred_element_type=jnp.float32)
        )
    grad_queries = jnp.concatenate(query_parts, axis=0)
    later_keys, later_values = (
        shifted(key_sums[:rows].astype(jnp.bfloat16), "seq", -1).astype(jnp.float32),
        shifted(value_sums[:rows].astype(jnp.bfloat16), "seq", -1).astype(jnp.float32),
    )
    own_keys = key_sums[rows:] + later_keys
    grad_values = (value_sums[rows:] + later_values).astype(jnp.bfloat16).reshape(rows, heads * VD)
    turn_back = jax.vjp(lambda field: rotate(field, cosine, sine), query_pre)[1]
    grad_query = turn_back(grad_queries)[0].astype(jnp.bfloat16).reshape(rows, heads * KD)
    grad_key = (turn_back(own_keys)[0] * key_scale).astype(jnp.bfloat16).reshape(rows, heads * KD)
    query_part = jnp.dot(gathered.T, grad_query, preferred_element_type=jnp.float32)
    key_part = jnp.dot(gathered.T, grad_key, preferred_element_type=jnp.float32)
    value_part = jnp.dot(gathered.T, grad_values, preferred_element_type=jnp.float32)
    gate_part = jnp.dot(gathered.T, grad_gate, preferred_element_type=jnp.float32)
    normed_part = (
        jnp.dot(grad_query, query_full.T, preferred_element_type=jnp.float32)
        + jnp.dot(grad_key, key_full.T, preferred_element_type=jnp.float32)
        + jnp.dot(grad_values, value_full.T, preferred_element_type=jnp.float32)
        + jnp.dot(grad_gate, gate_full.T, preferred_element_type=jnp.float32)
    )
    query_grad, key_grad, value_grad, gate_grad, group_gain_grad, group_bias_grad = (
        lax.psum_scatter(
            query_part.astype(jnp.bfloat16), "seq", scatter_dimension=0, tiled=True
        ).astype(jnp.float32),
        lax.psum_scatter(
            key_part.astype(jnp.bfloat16), "seq", scatter_dimension=0, tiled=True
        ).astype(jnp.float32),
        lax.psum_scatter(
            value_part.astype(jnp.bfloat16), "seq", scatter_dimension=0, tiled=True
        ).astype(jnp.float32),
        lax.psum_scatter(
            gate_part.astype(jnp.bfloat16), "seq", scatter_dimension=0, tiled=True
        ).astype(jnp.float32),
        lax.psum_scatter(
            group_gain_part.astype(jnp.bfloat16), "seq", scatter_dimension=0, tiled=True
        ).astype(jnp.float32),
        lax.psum_scatter(
            group_bias_part.astype(jnp.bfloat16), "seq", scatter_dimension=0, tiled=True
        ).astype(jnp.float32),
    )
    grad_normed = lax.psum_scatter(
        normed_part.astype(jnp.bfloat16), "grp", scatter_dimension=0, tiled=True
    ).astype(jnp.float32)
    first_back = jax.vjp(layer_norm, inputs, gain_one, bias_one)[1]
    grad_rows, gain_one_part, bias_one_part = first_back(grad_normed)
    tokens_grad = (grad_hidden + grad_rows).astype(jnp.bfloat16)
    shares = (
        lax.psum_scatter(
            out_part.astype(jnp.bfloat16), "seq", scatter_dimension=0, tiled=True
        ).astype(jnp.float32),
        lax.psum_scatter(
            up_part.astype(jnp.bfloat16), "seq", scatter_dimension=0, tiled=True
        ).astype(jnp.float32),
        lax.psum_scatter(
            down_part.astype(jnp.bfloat16), "seq", scatter_dimension=0, tiled=True
        ).astype(jnp.float32),
        lax.psum_scatter(
            up_bias_part.astype(jnp.bfloat16), "seq", scatter_dimension=0, tiled=True
        ).astype(jnp.float32),
        lax.psum_scatter(
            down_bias_part.astype(jnp.bfloat16), "seq", scatter_dimension=0, tiled=True
        ).astype(jnp.float32),
        lax.psum_scatter(
            gain_one_part.astype(jnp.bfloat16), "seq", scatter_dimension=0, tiled=True
        ).astype(jnp.float32),
        lax.psum_scatter(
            bias_one_part.astype(jnp.bfloat16), "seq", scatter_dimension=0, tiled=True
        ).astype(jnp.float32),
        lax.psum_scatter(
            gain_two_part.astype(jnp.bfloat16), "seq", scatter_dimension=0, tiled=True
        ).astype(jnp.float32),
        lax.psum_scatter(
            bias_two_part.astype(jnp.bfloat16), "seq", scatter_dimension=0, tiled=True
        ).astype(jnp.float32),
    )
    (
        out_grad,
        up_grad,
        down_grad,
        up_bias_grad,
        down_bias_grad,
        first_gain_grad,
        first_bias_grad,
        second_gain_grad,
        second_bias_grad,
    ) = (
        lax.psum(shares[0].astype(jnp.bfloat16), "grp").astype(jnp.float32),
        lax.psum(shares[1].astype(jnp.bfloat16), "grp").astype(jnp.float32),
        lax.psum(shares[2].astype(jnp.bfloat16), "grp").astype(jnp.float32),
        lax.psum(shares[3].astype(jnp.bfloat16), "grp").astype(jnp.float32),
        lax.psum(shares[4].astype(jnp.bfloat16), "grp").astype(jnp.float32),
        lax.psum(shares[5].astype(jnp.bfloat16), "grp").astype(jnp.float32),
        lax.psum(shares[6].astype(jnp.bfloat16), "grp").astype(jnp.float32),
        lax.psum(shares[7].astype(jnp.bfloat16), "grp").astype(jnp.float32),
        lax.psum(shares[8].astype(jnp.bfloat16), "grp").astype(jnp.float32),
    )
    return (
        mixed,
        tokens_grad,
        first_gain_grad,
        first_bias_grad,
        query_grad,
        key_grad,
        value_grad,
        gate_grad,
        group_gain_grad,
        group_bias_grad,
        out_grad,
        second_gain_grad,
        second_bias_grad,
        up_grad,
        up_bias_grad,
        down_grad,
        down_bias_grad,
    )


def solution(mesh):
    placed = (
        P(("seq", "grp"), None),
        P("seq"),
        P("seq"),
        P("seq", "grp"),
        P("seq", "grp"),
        P("seq", "grp"),
        P("seq", "grp"),
        P("seq", "grp"),
        P("seq", "grp"),
        P("seq", None),
        P("seq"),
        P("seq"),
        P("seq", None),
        P("seq"),
        P("seq", None),
        P("seq"),
        P(("seq", "grp"), None),
        P(),
        P("grp"),
    )
    return jax.shard_map(
        body,
        mesh=mesh,
        in_specs=placed,
        out_specs=(
            P(("seq", "grp"), None),
            P(("seq", "grp"), None),
            P("seq"),
            P("seq"),
            P("seq", "grp"),
            P("seq", "grp"),
            P("seq", "grp"),
            P("seq", "grp"),
            P("seq", "grp"),
            P("seq", "grp"),
            P("seq", None),
            P("seq"),
            P("seq"),
            P("seq", None),
            P("seq"),
            P("seq", None),
            P("seq"),
        ),
        check_vma=False,
    )
```

profile of v0, /device:TPU:0, one launch (start us, length us, event | category | flops | bytes accessed | tf_op | source)
XLA Modules:
  0.0 1536.4 jit_solution(17321597649641220600)
XLA Ops:
  8.6 10.3 all-gather.1
  19.6 8.9 all-gather
  38.3 7.8 all-gather.3
  46.1 8.7 all-gather.2
  62.6 60.9 %all-gather.17.cloned.1.call-done = bf16[1024,2048]{1,0:T(8,128)(2,1)} async-done(((bf16[256,2048]{1,0:T(8,128)(2,1)}), bf16[1024,2048]{1,0:T(8,128)(2,1)}) %all-gather.17.cloned.1.call-update) | async-done | bytes 4194320 | tf_op jit(solution)/shard_map/all_gather | solution.py:110
  123.5 6.6 fusion.74
  132.1 19.8 %all-gather.25.cloned.1.call-done = bf16[2048,512]{1,0:T(8,128)(2,1)} async-done(((bf16[256,512]{1,0:T(8,128)(2,1)}), bf16[2048,512]{1,0:T(8,128)(2,1)}) %all-gather.25.cloned.1.call-update) | async-done | bytes 2097168 | tf_op jit(solution)/shard_map/all_gather | solution.py:98
  151.9 6.6 fusion.75
  169.2 26.7 %all-gather.21.cloned.1.call-done = bf16[2048,1024]{1,0:T(8,128)(2,1)} async-done(((bf16[256,1024]{1,0:T(8,128)(2,1)}), bf16[2048,1024]{1,0:T(8,128)(2,1)}) %all-gather.21.cloned.1.call-update) | async-done | bytes 4194320 | tf_op jit(solution)/shard_map/all_gather | solution.py:99
  195.9 8.2 convolution_convert_fusion.8
  243.8 16.3 %multiply_convert_fusion.5 = (bf16[1024,1024]{1,0:T(8,128)(2,1)}, f32[1024,1024]{1,0:T(8,128)}, f32[1024,1024]{1,0:T(8,128)}) fusion(f32[1024]{0:T(1024)S(1)} %bitcast.163, f32[1024]{0:T(1024)S(1)} %bitcast.165, f32[1024,1024]{1,0:T(8,128)} %copy.191, f32[1024,1024]{1,0:T(8,128)} %copy.190, f32[512,1024]{1,0:T(8,128)} %copy.189, f32[512,1024]{1,0:T(8,128)} %copy.188, ...), kind=kOutput, calls=%fused_computation.48 | convolution fusion | flops 4306501632 | bytes 31465472 | tf_op jit(solution)/shard_map/dot_general | solution.py:128
  268.8 39.1 %all-gather.6 = bf16[8,1,512]{2,1,0:T(2,128)(2,1)S(1)} all-gather(bf16[1,1,512]{2,1,0:T(2,128)(2,1)S(1)} %reshape.569), channel_id=1, replica_groups=mesh['seq'=8,'grp'=4] {'seq'}, dimensions={0}, use_global_device_ids=true | all-gather | bytes 9216 | tf_op jit(solution)/shard_map/all_gather | solution.py:177
  307.9 8.9 all-gather.5
  316.8 7.9 all-gather.4
  324.8 9.6 all-gather.27.cloned.1.call-done
  334.4 8.9 fusion.73
  345.0 81.2 %all-gather.29.cloned.1.call-done = bf16[2048,4096]{1,0:T(8,128)(2,1)} async-done(((bf16[256,4096]{1,0:T(8,128)(2,1)}), bf16[2048,4096]{1,0:T(8,128)(2,1)}) %all-gather.29.cloned.1.call-update) | async-done | bytes 16777232 | tf_op jit(solution)/shard_map/all_gather | solution.py:175
  426.2 13.2 convolution_add_fusion
  439.4 78.6 %all-gather.31.cloned.1.call-done = bf16[4096,2048]{1,0:T(8,128)(2,1)} async-done(((bf16[512,2048]{1,0:T(8,128)(2,1)}), bf16[4096,2048]{1,0:T(8,128)(2,1)}) %all-gather.31.cloned.1.call-update) | async-done | bytes 16777232 | tf_op jit(solution)/shard_map/all_gather | solution.py:176
  517.9 20.8 %fusion.63 = (bf16[4096]{0:T(1024)(128)(2,1)}, bf16[256,4096]{1,0:T(8,128)(2,1)}, f32[256,4096]{1,0:T(8,128)}) fusion(f32[256,4096]{1,0:T(8,128)} %convolution_add_fusion, bf16[256,2048]{1,0:T(8,128)(2,1)S(1)} %copy-done.10, bf16[4096,2048]{1,0:T(8,128)(2,1)} %all-gather.31.cloned.1.call-done), kind=kOutput, calls=%fused_computation.174 | convolution fusion | flops 4371509248 | bytes 28319744 | tf_op jit(solution)/shard_map/dot_general | solution.py:203
  538.8 13.8 multiply_reduce_fusion.3
  558.1 12.1 convolution_convert_fusion.2
  570.5 16.2 %convolution_convert_fusion.1 = bf16[2048,4096]{1,0:T(8,128)(2,1)} fusion(bf16[256,4096]{1,0:T(8,128)(2,1)} %get-tuple-element.91, f32[256,2048]{1,0:T(8,128)} %copy-done.5, f32[2048]{0:T(1024)S(1)} %bitcast.161, f32[2048]{0:T(1024)S(1)} %bitcast.155, f32[256]{0:T(256)S(1)} %fusion.51, f32[256]{0:T(256)S(1)} %broadcast_multiply_fusion.1), kind=kOutput, calls=%fused_computation.1 | convolution fusion | flops 4305977344 | bytes 20989952 | tf_op jit(solution)/shard_map/dot_general | solution.py:207
  586.8 7.1 multiply_convert_fusion.4
  593.8 10.3 convolution_convert_fusion
  605.3 18.7 %convolution_convert_fusion.3 = bf16[256,4096]{1,0:T(8,128)(2,1)} fusion(bf16[256,2048]{1,0:T(8,128)(2,1)S(1)} %copy-done.18, bf16[4096,2048]{1,0:T(8,128)(2,1)} %all-gather.27.cloned.1.call-done), kind=kOutput, calls=%fused_computation.15 | convolution fusion | flops 4296015872 | bytes 19922944 | tf_op jit(solution)/shard_map/dot_general | solution.py:214
  626.0 52.9 %all_to_all.32 = bf16[256,4,1024]{2,0,1:T(8,128)(2,1)S(1)} all-to-all(bf16[256,4,1024]{2,0,1:T(8,128)(2,1)S(1)} %bitcast.137), channel_id=1, replica_groups=mesh['seq'=8,'grp'=4] {'grp'}, dimensions={1} | all-to-all | bytes 4194304 | tf_op jit(solution)/shard_map/all_to_all | solution.py:217
  730.5 6.0 convolution_convert_fusion.7
  737.9 6.6 convolution_convert_fusion.6
  744.6 8.6 convolution_convert_fusion.4
  764.2 13.2 collective-permute-done.3
  780.4 6.3 convolution_convert_fusion.5
  788.2 9.1 fusion.78
  803.0 5.7 fusion.77
  808.7 13.6 add_convert_fusion
  822.5 117.2 %reduce-scatter.29.cloned.1.call-done = bf16[512,2048]{1,0:T(8,128)(2,1)} async-done(((bf16[4096,2048]{1,0:T(8,128)(2,1)}), bf16[512,2048]{1,0:T(8,128)(2,1)}) %reduce-scatter.29.cloned.1.call-update) | async-done | bytes 2097168 | tf_op jit(solution)/shard_map/reduce_scatter | solution.py:305
  941.1 9.0 all-gather.7
  952.0 11.9 fusion.19
  964.0 12.5 reduce-scatter.31.cloned.1.call-done
  977.8 35.9 %reduce-scatter.33.cloned.1.call-done = bf16[64,2]{1,0:T(8,128)(2,1)} async-done(((bf16[512,2]{1,0:T(8,128)(2,1)}), bf16[64,2]{1,0:T(8,128)(2,1)}) %reduce-scatter.33.cloned.1.call-update) | async-done | bytes 272
  1015.1 43.0 %reduce-scatter.17.cloned.1.call-done = bf16[256,512]{1,0:T(8,128)(2,1)} async-done(((bf16[2048,512]{1,0:T(8,128)(2,1)}), bf16[256,512]{1,0:T(8,128)(2,1)}) %reduce-scatter.17.cloned.1.call-update) | async-done | bytes 262160 | tf_op jit(solution)/shard_map/reduce_scatter | solution.py:273
  1059.9 42.9 %reduce-scatter.19.cloned.1.call-done = bf16[256,512]{1,0:T(8,128)(2,1)} async-done(((bf16[2048,512]{1,0:T(8,128)(2,1)}), bf16[256,512]{1,0:T(8,128)(2,1)}) %reduce-scatter.19.cloned.1.call-update) | async-done | bytes 262160 | tf_op jit(solution)/shard_map/reduce_scatter | solution.py:276
  1104.6 53.3 %reduce-scatter.23.cloned.1.call-done = bf16[256,1024]{1,0:T(8,128)(2,1)} async-done(((bf16[2048,1024]{1,0:T(8,128)(2,1)}), bf16[256,1024]{1,0:T(8,128)(2,1)}) %reduce-scatter.23.cloned.1.call-update) | async-done | bytes 524304 | tf_op jit(solution)/shard_map/reduce_scatter | solution.py:282
  1160.1 53.4 %reduce-scatter.21.cloned.1.call-done = bf16[256,1024]{1,0:T(8,128)(2,1)} async-done(((bf16[2048,1024]{1,0:T(8,128)(2,1)}), bf16[256,1024]{1,0:T(8,128)(2,1)}) %reduce-scatter.21.cloned.1.call-update) | async-done | bytes 524304 | tf_op jit(solution)/shard_map/reduce_scatter | solution.py:279
  1215.6 77.4 %reduce-scatter.15.cloned.1.call-done = bf16[256,2048]{1,0:T(8,128)(2,1)} async-done(((bf16[1024,2048]{1,0:T(8,128)(2,1)}), bf16[256,2048]{1,0:T(8,128)(2,1)}) %reduce-scatter.15.cloned.1.call-update) | async-done | bytes 1048592 | tf_op jit(solution)/shard_map/reduce_scatter | solution.py:292
  1298.5 25.2 %all-reduce.12 = (bf16[2048]{0:T(1024)(128)(2,1)S(1)}, bf16[2048]{0:T(1024)(128)(2,1)S(1)}, bf16[2048]{0:T(1024)(128)(2,1)S(1)}, bf16[2048]{0:T(1024)(128)(2,1)S...) all-reduce(bf16[2048]{0:T(1024)(128)(2,1)S(1)} %get-tuple-element.6, ...), channel_id=3, replica_groups=mesh['seq'=8,'grp'=4] {'seq'}, use_global_device_ids=true, to_apply=%region_18.19.clone | all-reduce | flops 14336 | bytes 57344
  1324.2 11.5 all-reduce.13
  1342.6 177.5 %all-reduce.17.cloned.1.call-done = (bf16[512,2048]{1,0:T(8,128)(2,1)}, bf16[256,4096]{1,0:T(8,128)(2,1)}, bf16[512,2048]{1,0:T(8,128)(2,1)}) async-done(((bf16[512,2048]{1,0:T(8,128)(2,1)}, bf16[256,4096]{1,0:T(8,128)(2,1)}, bf16[512,2048]{1,0:T(8,128)(2,1)}), (bf16[512,2048]{1,0:T(8,128)(2,1)}, bf16[256,4096]{1,0:T(8,128)(2,1)}, bf16[512,2048]{1,0:T(8,128)(2,1)})) %all-reduce.17.cloned.1.call-update) | async-done | bytes 6291472 | tf_op jit(solution)/shard_map/psum | solution.py:338
  (347 shorter events, 199.0 us)
Async XLA Ops:
  7.2 25.6 %copy-start.3 = (bf16[256,2048]{1,0:T(8,128)(2,1)S(1)}, bf16[256,2048]{1,0:T(8,128)(2,1)}, u32[]{:S(2)}) copy-start(bf16[256,2048]{1,0:T(8,128)(2,1)} %param.27) | copy-start | bytes 3145732
  7.2 55.4 %all-gather.23.cloned.1.call-start = ((), (), s32[]{:S(2)}) async-start(), calls=%async_computation.15 | async-start | bytes 2359296 | tf_op jit(solution)/shard_map/all_gather | solution.py:97
  7.9 115.6 %all-gather.17.cloned.1.call-start = ((), (), s32[]{:S(2)}) async-start(), calls=%async_computation.12 | async-start | bytes 5242880 | tf_op jit(solution)/shard_map/all_gather | solution.py:110
  34.2 117.6 %all-gather.25.cloned.1.call-start = ((), (), s32[]{:S(2)}) async-start(), calls=%async_computation.16 | async-start | bytes 2359296 | tf_op jit(solution)/shard_map/all_gather | solution.py:98
  35.0 160.9 %all-gather.21.cloned.1.call-start = ((), (), s32[]{:S(2)}) async-start(), calls=%async_computation.14 | async-start | bytes 4718592 | tf_op jit(solution)/shard_map/all_gather | solution.py:99
  35.6 208.3 %all-gather.19.cloned.1.call-start = ((), (), s32[]{:S(2)}) async-start(), calls=%async_computation.13 | async-start | bytes 4718592 | tf_op jit(solution)/shard_map/all_gather | solution.py:100
  36.2 19.4 %copy-start.67 = (s32[3]{0:T(128)S(1)}, s32[3]{0:T(128)}, u32[]{:S(2)}) copy-start(s32[3]{0:T(128)} %param.44) | copy-start | bytes 40
  36.2 298.2 %all-gather.27.cloned.1.call-start = ((), (), s32[]{:S(2)}) async-start(), calls=%async_computation.17 | async-start | bytes 18874368 | tf_op jit(solution)/shard_map/all_gather | solution.py:174
  36.8 389.4 %all-gather.29.cloned.1.call-start = ((), (), s32[]{:S(2)}) async-start(), calls=%async_computation.18 | async-start | bytes 18874368 | tf_op jit(solution)/shard_map/all_gather | solution.py:175
  37.5 480.4 %all-gather.31.cloned.1.call-start = ((), (), s32[]{:S(2)}) async-start(), calls=%async_computation.19 | async-start | bytes 18874368 | tf_op jit(solution)/shard_map/all_gather | solution.py:176
  55.8 157.6 %copy-start.81 = (f32[2]{0:T(128)}, f32[2]{0:T(128)S(1)}, u32[]{:S(2)}) copy-start(f32[2]{0:T(128)S(1)} %negate_log-plus-one_fusion) | copy-start | bytes 28
  166.5 42.4 %copy-start.20 = (bf16[1024,2,256]{2,0,1:T(8,128)(2,1)S(1)}, bf16[1024,2,256]{2,0,1:T(8,128)(2,1)}, u32[]{:S(2)}) copy-start(bf16[1024,2,256]{2,0,1:T(8,128)(2,1)} %get-tuple-element.102) | copy-start | bytes 3145732
  166.5 42.4 %collective-permute-start.1 = (bf16[1024,2,256]{2,0,1:T(8,128)(2,1)}, bf16[1024,2,256]{2,0,1:T(8,128)(2,1)S(1)}, u32[]{:S(2)}, u32[]{:S(2)}) collective-permute-start(bf16[1024,2,256]{2,0,1:T(8,128)(2,1)} %get-tuple-element.103), channel_id=1, source_target_pairs={{0,4},{4,8},{8,12},{12,16},{16,20},{20,24},{24,28},{1,5},{5,9},{9,... | collective-permute-start | bytes 3145736 | tf_op jit(solution)/shard_map/ppermute | solution.py:19
  195.9 13.1 copy-start.25
  204.0 14.8 copy-start.71
  204.1 12.9 collective-permute-start
  264.1 43.8 %copy-start.77 = (bf16[256]{0:T(256)(128)(2,1)S(1)}, bf16[256]{0:T(256)(128)(2,1)}, u32[]{:S(2)}) copy-start(bf16[256]{0:T(256)(128)(2,1)} %param.38) | copy-start | bytes 1540
  264.1 52.7 %copy-start.78 = (bf16[256]{0:T(256)(128)(2,1)S(1)}, bf16[256]{0:T(256)(128)(2,1)}, u32[]{:S(2)}) copy-start(bf16[256]{0:T(256)(128)(2,1)} %param.37) | copy-start | bytes 1540
  264.1 60.7 %all-to-all-start = ((bf16[4,256,1024]{1,2,0:T(8,128)(2,1)}), bf16[4,256,1024]{1,2,0:T(8,128)(2,1)}, u32[]{:S(2)}, u32[]{:S(2)}) async-start(bf16[4,256,1024]{1,2,0:T(8,128)(2,1)} %copy.159), calls=%async_computation | async-start | bytes 4194304 | tf_op jit(solution)/shard_map/all_to_all | solution.py:172
  268.8 553.7 %reduce-scatter.25.cloned.1.call-start = ((), (), s32[]{:S(2)}) async-start(), calls=%async_computation.25 | async-start | bytes 18874368 | tf_op jit(solution)/shard_map/reduce_scatter | solution.py:299
  426.2 91.8 %copy-start.10 = (bf16[256,2048]{1,0:T(8,128)(2,1)S(1)}, bf16[256,2048]{1,0:T(8,128)(2,1)}, u32[]{:S(2)}) copy-start(bf16[256,2048]{1,0:T(8,128)(2,1)} %param.43) | copy-start | bytes 3145732
  555.5 14.8 copy-start.57
  570.3 252.1 %reduce-scatter.27.cloned.1.call-start = ((), (), s32[]{:S(2)}) async-start(), calls=%async_computation.26 | async-start | bytes 18874368 | tf_op jit(solution)/shard_map/reduce_scatter | solution.py:302
  586.7 352.9 %reduce-scatter.29.cloned.1.call-start = ((), (), s32[]{:S(2)}) async-start(), calls=%async_computation.27 | async-start | bytes 18874368 | tf_op jit(solution)/shard_map/reduce_scatter | solution.py:305
  604.1 372.3 %reduce-scatter.31.cloned.1.call-start = ((), (), s32[]{:S(2)}) async-start(), calls=%async_computation.28 | async-start | bytes 147456
  624.1 54.9 %copy-start.23 = (f32[1024,1024]{1,0:T(8,128)S(1)}, f32[1024,1024]{1,0:T(8,128)}, u32[]{:S(2)}) copy-start(f32[1024,1024]{1,0:T(8,128)} %get-tuple-element.124) | copy-start | bytes 12582916
  626.0 53.0 %copy-start.22 = (f32[1024,1024]{1,0:T(8,128)S(1)}, f32[1024,1024]{1,0:T(8,128)}, u32[]{:S(2)}) copy-start(f32[1024,1024]{1,0:T(8,128)} %get-tuple-element.96) | copy-start | bytes 12582916
  713.3 9.4 collective-permute-start.2
  715.4 298.3 %reduce-scatter.33.cloned.1.call-start = ((), (), s32[]{:S(2)}) async-start(), calls=%async_computation.29 | async-start | bytes 147456
  716.3 341.8 %reduce-scatter.17.cloned.1.call-start = ((), (), s32[]{:S(2)}) async-start(), calls=%async_computation.21 | async-start | bytes 2359296 | tf_op jit(solution)/shard_map/reduce_scatter | solution.py:273
  736.5 366.3 %reduce-scatter.19.cloned.1.call-start = ((), (), s32[]{:S(2)}) async-start(), calls=%async_computation.22 | async-start | bytes 2359296 | tf_op jit(solution)/shard_map/reduce_scatter | solution.py:276
  744.5 413.4 %reduce-scatter.23.cloned.1.call-start = ((), (), s32[]{:S(2)}) async-start(), calls=%async_computation.24 | async-start | bytes 4718592 | tf_op jit(solution)/shard_map/reduce_scatter | solution.py:282
  753.2 460.3 %reduce-scatter.21.cloned.1.call-start = ((), (), s32[]{:S(2)}) async-start(), calls=%async_computation.23 | async-start | bytes 4718592 | tf_op jit(solution)/shard_map/reduce_scatter | solution.py:279
  762.9 14.5 collective-permute-start.3
  786.7 506.3 %reduce-scatter.15.cloned.1.call-start = ((), (), s32[]{:S(2)}) async-start(), calls=%async_computation.20 | async-start | bytes 5242880 | tf_op jit(solution)/shard_map/reduce_scatter | solution.py:292
  822.4 697.7 %all-reduce.17.cloned.1.call-start = ((), (), s32[]{:S(2)}) async-start(), calls=%async_computation.30 | async-start | bytes 12582912 | tf_op jit(solution)/shard_map/psum | solution.py:338
  939.6 10.5 copy-start.80
  939.6 12.4 copy-start.6
  964.0 330.5 %copy-start.4 = (bf16[256,2048]{1,0:T(8,128)(2,1)S(1)}, bf16[256,2048]{1,0:T(8,128)(2,1)}, u32[]{:S(2)}) copy-start(bf16[256,2048]{1,0:T(8,128)(2,1)} %param.27) | copy-start | bytes 3145732
  964.0 330.5 %copy-start.46 = (f32[8,1,256]{2,1,0:T(1,128)S(1)}, f32[8,1,256]{2,1,0:T(1,128)}, u32[]{:S(2)}) copy-start(f32[8,1,256]{2,1,0:T(1,128)} %copy-done.45) | copy-start | bytes 24580
  964.0 330.5 %copy-start.54 = (f32[256]{0:T(256)S(1)}, f32[256]{0:T(256)}, u32[]{:S(2)}) copy-start(f32[256]{0:T(256)} %copy-done.53) | copy-start | bytes 3076
  1104.6 191.6 %copy-start.60 = (f32[256]{0:T(256)S(1)}, f32[256]{0:T(256)}, u32[]{:S(2)}) copy-start(f32[256]{0:T(256)} %copy-done.59) | copy-start | bytes 3076
  1104.6 191.6 %copy-start.56 = (f32[256]{0:T(256)S(1)}, f32[256]{0:T(256)}, u32[]{:S(2)}) copy-start(f32[256]{0:T(256)} %copy-done.55) | copy-start | bytes 3076
  1160.1 138.4 %copy-start.61 = (bf16[4096]{0:T(1024)(128)(2,1)S(1)}, bf16[4096]{0:T(1024)(128)(2,1)}, u32[]{:S(2)}) copy-start(bf16[4096]{0:T(1024)(128)(2,1)} %get-tuple-element.90) | copy-start | bytes 24580
  1160.1 138.4 %copy-start.62 = (bf16[2048]{0:T(1024)(128)(2,1)S(1)}, bf16[2048]{0:T(1024)(128)(2,1)}, u32[]{:S(2)}) copy-start(bf16[2048]{0:T(1024)(128)(2,1)} %get-tuple-element.65) | copy-start | bytes 12292
  1160.1 138.4 %copy-start.63 = (bf16[2048]{0:T(1024)(128)(2,1)S(1)}, bf16[2048]{0:T(1024)(128)(2,1)}, u32[]{:S(2)}) copy-start(bf16[2048]{0:T(1024)(128)(2,1)} %get-tuple-element.71) | copy-start | bytes 12292
  1160.1 179.0 %copy-start.8 = (f32[256,2048]{1,0:T(8,128)S(1)}, f32[256,2048]{1,0:T(8,128)}, u32[]{:S(2)}) copy-start(f32[256,2048]{1,0:T(8,128)} %copy-done.7) | copy-start | bytes 6291460
  1160.1 179.0 %copy-start.58 = (f32[256]{0:T(256)S(1)}, f32[256]{0:T(256)}, u32[]{:S(2)}) copy-start(f32[256]{0:T(256)} %copy-done.57) | copy-start | bytes 3076
  (59 other events, 196.4 us)
Sparse Core Ops, SparseCore 0:
  9.9 30.6 all-gather.22
  42.7 80.7 all-gather.16
  125.4 26.4 all-gather.24
  153.6 42.2 all-gather.20
  197.6 44.8 all-gather.18
  244.2 90.1 all-gather.26
  336.3 89.8 all-gather.28
  428.1 89.8 all-gather.30
  570.4 115.9 reduce-scatter.24
  689.8 130.0 reduce-scatter.26
  823.6 116.0 reduce-scatter.28
  943.1 33.3 reduce-scatter.30
  980.3 33.3 reduce-scatter.32
  1016.9 41.1 reduce-scatter.16
  1061.6 41.2 reduce-scatter.18
  1106.6 51.3 reduce-scatter.22
  1162.1 51.3 reduce-scatter.20
  1216.2 76.7 reduce-scatter.14
  1295.8 224.2 all-reduce.16
where the time goes:
time: 1550 us; the launch traced here: 1540 us
  waiting for transfers between devices  908 us (59%)
  matrix products  257 us (17%)
  blocking collectives  190 us (12%)
  other arithmetic  76.1 us (5%)
  local copies, waits for them, and re-layouts  73.5 us (5%)
  between operations  17.5 us (1%)
    psum x1, waiting for transfers between devices, body(): lax.psum(shares[0].astype(jnp.bfloat16), 'grp').astype(jnp.float32)  177 us
    reduce_scatter x1, waiting for transfers between devices, body(): lax.psum_scatter(down_part.astype(jnp.bfloat16), 'seq', scatter_dimension...  117 us
    all_gather x1, waiting for transfers between devices, body(): lax.all_gather(up_weight, 'seq', axis=0, tiled=True)  81.2 us
    all_gather x1, waiting for transfers between devices, body(): lax.all_gather(down_weight, 'seq', axis=0, tiled=True)  78.6 us
    reduce_scatter x1, waiting for transfers between devices, body(): lax.psum_scatter(normed_part.astype(jnp.bfloat16), 'grp', scatter_dimensi...  77.4 us
    all_gather x1, waiting for transfers between devices, body(): gathered = lax.all_gather(normed, 'grp', axis=0, tiled=True)  60.9 us
    reduce_scatter x1, waiting for transfers between devices, body(): lax.psum_scatter(value_part.astype(jnp.bfloat16), 'seq', scatter_dimensio...  53.4 us
    reduce_scatter x1, waiting for transfers between devices, body(): lax.psum_scatter(gate_part.astype(jnp.bfloat16), 'seq', scatter_dimension...  53.3 us
  transfers between devices with their start and end apart: 24, of which 16 were waited for; matrix products, arithmetic and copies ran while one was open for 21% of the time, Pallas kernels for 0%

commit v1 on v0

v1 whole, which is shorter than its diff:
```python
from functools import partial

import jax
import jax.numpy as jnp
from jax import lax
from jax.sharding import PartitionSpec as P

KD = 256
VD = 512
STRETCH = 512
EPSILON = 1e-05

F32 = jnp.float32
BF16 = jnp.bfloat16


def dot(a, b, dims=((1,), (0,))):
    return lax.dot_general(a, b, (dims, ((), ())), preferred_element_type=F32)


def flip(block, bit):
    devices = lax.axis_size("seq")
    return lax.ppermute(block, "seq", [(i, i ^ bit) for i in range(devices)])


def hop(block, by):
    devices = lax.axis_size("seq")
    return lax.ppermute(block, "seq", [(i, i + by) for i in range(devices) if 0 <= i + by < devices])


def turn(block, by):
    groups = lax.axis_size("grp")
    return lax.ppermute(block, "grp", [(i, (i + by) % groups) for i in range(groups)])


def pick(array, index, axis=0):
    return lax.dynamic_index_in_dim(array, index, axis, keepdims=False)


def cut(array, index, size, axis):
    return lax.dynamic_slice_in_dim(array, index * size, size, axis)


def put(array, block, index, axis):
    return lax.dynamic_update_slice_in_dim(array, block, index * block.shape[axis], axis)


def after(block, *others):
    return lax.optimization_barrier((block, *others))[0]


class Stages:
    def __init__(self):
        self.last = ()

    def run(self, *sends, late=(), joined=True):
        blocks = lax.optimization_barrier(tuple(b for b, _ in sends) + tuple(self.last) + tuple(late))
        came = tuple(move(block) for block, (_, move) in zip(blocks, sends))
        came = lax.optimization_barrier(came) if joined and len(came) > 1 else came
        self.last = came
        return came


def by_core(block):
    return flip(block, 1)


def by_x(block):
    return flip(block, 2)


def by_y(block):
    return flip(block, 4)


def choose(index, options):
    result = options[0]
    for i, option in enumerate(options[1:], 1):
        result = jnp.where(index == i, option, result)
    return result


def by_difference(blocks, index):
    count = len(blocks)
    return [choose(index ^ i, [blocks[d] for d in range(count)]) for i in range(count)]


def group_scatter(block, group_index):
    groups = lax.axis_size("grp")
    size = block.shape[0] // groups
    up = down = None
    for step in range(1, groups):
        goes_up = cut(block, jnp.minimum(groups - step + group_index, groups - 1), size, 0)
        goes_down = cut(block, jnp.maximum(step - groups + group_index, 0), size, 0)
        if up is not None:
            goes_up = (goes_up.astype(F32) + up.astype(F32)).astype(BF16)
            goes_down = (goes_down.astype(F32) + down.astype(F32)).astype(BF16)
        goes_up, goes_down = lax.optimization_barrier((goes_up.astype(BF16), goes_down.astype(BF16)))
        up = lax.ppermute(goes_up, "grp", [(p, p + 1) for p in range(step)])
        down = lax.ppermute(goes_down, "grp", [(groups - 1 - p, groups - 2 - p) for p in range(step)])
        up, down = lax.optimization_barrier((up, down))
    return cut(block, group_index, size, 0).astype(F32) + up.astype(F32) + down.astype(F32)


def small_sum(block):
    for axis in ("seq", "grp"):
        devices, bit = lax.axis_size(axis), 1
        while bit < devices:
            block = block + lax.ppermute(block, axis, [(i, i ^ bit) for i in range(devices)])
            bit *= 2
    return block


def layer_norm(values, gain, bias):
    center = values - jnp.mean(values, axis=-1, keepdims=True)
    spread = jnp.mean(center * center, axis=-1, keepdims=True)
    return center * lax.rsqrt(spread + EPSILON) * gain + bias


def document_table(doc_lengths, positions):
    ends = jnp.cumsum(doc_lengths, dtype=jnp.int32)
    after = (positions[:, None] >= ends[None, :]).astype(jnp.int32)
    documents = jnp.sum(after, axis=1, dtype=jnp.int32)
    starts = jnp.sum(after * doc_lengths[None, :], axis=1, dtype=jnp.int32)
    return (documents, positions - starts)


def rotary_table(places, width):
    half = width // 2
    freqs = 10000.0 ** (-jnp.arange(half, dtype=F32) / (half - 1))
    angles = places.astype(F32)[:, None] * freqs[None, :]
    return jnp.cos(angles), jnp.sin(angles)


def rotate(values, cosine, sine):
    half = values.shape[-1] // 2
    low, high = values[:, :half], values[:, half:]
    return jnp.concatenate([low * cosine - high * sine, high * cosine + low * sine], axis=1)


def rotate_back(grads, cosine, sine):
    return rotate(grads, cosine, -sine)


def decay_mask(query_pos, key_pos, query_doc, key_doc, log_decay, window):
    distance = query_pos[:, None] - key_pos[None, :]
    inside = (distance >= 0) & (query_doc[:, None] == key_doc[None, :]) & (key_pos[None, :] >= 0)
    inside = inside & (distance < window)
    steps = jnp.where(inside, distance, 0).astype(F32)
    return jnp.where(inside, jnp.exp(steps * log_decay), 0.0)


def gate_norm(retained, gate_pre, gain, bias):
    center = retained - jnp.mean(retained, axis=-1, keepdims=True)
    spread = jnp.mean(center * center, axis=-1, keepdims=True)
    grouped = center * lax.rsqrt(spread + EPSILON) * gain + bias
    return jax.nn.silu(gate_pre) * grouped
def body(
    tokens,
    first_gain,
    first_bias,
    query_weight,
    key_weight,
    value_weight,
    gate_weight,
    group_gain,
    group_bias,
    out_weight,
    second_gain,
    second_bias,
    up_weight,
    up_bias,
    down_weight,
    down_bias,
    cotangent,
    doc_lengths,
    windows,
):
    devices, groups = lax.axis_size("seq"), lax.axis_size("grp")
    seq_index, group_index = lax.axis_index("seq"), lax.axis_index("grp")
    chips, quads = devices // 2, devices // 4
    core, chip = seq_index % 2, seq_index // 2
    quarter, quad = seq_index % 4, seq_index // 4
    own_rows, width = tokens.shape
    part = width // devices
    rows = own_rows * groups
    pair_rows = 2 * rows
    ff = up_weight.shape[1]
    ff_part, ff_quarter = ff // devices, ff // 4
    small_mesh = devices == 8
    stages = Stages()

    def head_columns(j):
        return jnp.concatenate(
            [
                cut(query_weight, j, KD, 1),
                cut(key_weight, j, KD, 1),
                cut(value_weight, j, VD, 1),
                cut(gate_weight, j, VD, 1),
            ],
            axis=1,
        )

    mine = head_columns(core)
    theirs = by_core(head_columns(1 - core))
    low_rows = jnp.where(core == 0, mine, theirs)
    high_rows = jnp.where(core == 0, theirs, mine)
    columns = mine.shape[1]

    small = [first_gain, first_bias, second_gain, second_bias, down_bias, up_bias]
    small += [group_gain.T.reshape(-1), group_bias.T.reshape(-1)]
    sizes = [item.shape[0] for item in small]
    packed = lax.all_gather(after(jnp.concatenate(small)[None], theirs), "seq", axis=0, tiled=True).astype(F32)
    whole, start = [], 0
    for size in sizes:
        whole.append(packed[:, start : start + size])
        start += size
    gain_one, bias_one, gain_two, bias_two, down_bias_full, up_bias_full = (
        item.reshape(-1) for item in whole[:6]
    )
    group_gain_f, group_bias_f = (
        pick(item.reshape(devices, 2, -1), core, 1).reshape(1, VD) for item in whole[6:]
    )
    up_bias_quarter = pick(up_bias_full.reshape(quads, 4, ff_part), quarter, 1).reshape(1, ff_quarter)

    inputs = tokens.astype(F32)
    normed = layer_norm(inputs, gain_one, bias_one).astype(BF16)
    gathered = lax.all_gather(normed, "grp", axis=0, tiled=True)

    def join_chips(low, high):
        held = {0: jnp.stack([low, high])}
        for bit in range(1, devices.bit_length() - 1):
            held.update({d | (1 << (bit - 1)): flip(v, 1 << bit) for d, v in list(held.items())})
        return {d: (v[0], v[1]) for d, v in held.items()}

    def quarter_columns(q):
        return [
            lax.dynamic_slice_in_dim(up_weight, (q + 4 * m) * ff_part, ff_part, 1) for m in range(quads)
        ]

    up_sent = jnp.concatenate(quarter_columns(quarter ^ 2) + quarter_columns(quarter ^ 3), axis=1)
    if small_mesh:
        half_low = VD // 2
        out_low, out_high = out_weight[:half_low], out_weight[half_low:]
        low_x, high_y = stages.run((low_rows, by_x), (high_rows, by_y))
        high_xy, low_xy = stages.run(
            (jnp.stack([high_rows, high_y]), by_x), (jnp.stack([low_rows, low_x]), by_y)
        )
        head_held = {
            0: (low_rows, high_rows),
            1: (low_x, high_xy[0]),
            2: (low_xy[0], high_y),
            3: (low_xy[1], high_xy[1]),
        }
        two_x, down_y = stages.run((jnp.stack([up_sent, cotangent]), by_x), (down_weight, by_y))
        up_x, cotangent_x = two_x[0], two_x[1]
        gathered = after(gathered, two_x)
    else:
        head_held = join_chips(low_rows, high_rows)
        up_x = by_x(up_sent)
    head_weight = jnp.zeros((chips, 2, part, columns), BF16)
    for d, (low, high) in head_held.items():
        head_weight = put(head_weight, jnp.stack([low, high])[None], chip ^ d, 0)
    head_weight = head_weight.reshape(width, columns)

    up_core = by_core(
        jnp.stack([jnp.concatenate(quarter_columns(quarter ^ 1), axis=1), up_x[:, ff_quarter:]])
    )
    up_own = jnp.concatenate(quarter_columns(quarter), axis=1)
    up_four = jnp.stack([up_own, up_core[0], up_x[:, :ff_quarter], up_core[1]])

    beside = by_core(gathered)
    pair_normed = jnp.concatenate(
        [jnp.where(core == 0, gathered, beside), jnp.where(core == 0, beside, gathered)], axis=0
    )

    base = chip * pair_rows
    positions = base + jnp.arange(pair_rows, dtype=jnp.int32)
    documents, places = document_table(doc_lengths, positions)
    key_positions = base - rows + jnp.arange(3 * rows, dtype=jnp.int32)
    key_documents = document_table(doc_lengths, key_positions)[0]
    cosine, sine = rotary_table(places, KD)
    key_scale = KD ** (-0.5)
    key_pre = dot(pair_normed, head_weight[:, KD : 2 * KD])
    keys = (rotate(key_pre, cosine, sine) * key_scale).astype(BF16)
    values = dot(pair_normed, head_weight[:, 2 * KD : 2 * KD + VD]).astype(BF16)
    halo = jnp.concatenate([keys[rows:], values[rows:]], axis=1)
    if small_mesh:
        (halo,) = stages.run((halo, lambda v: hop(v, 2)))
    else:
        halo = hop(halo, 2)
    query_pre = dot(pair_normed, head_weight[:, :KD])
    gate_pre = dot(pair_normed, head_weight[:, 2 * KD + VD :])
    queries = rotate(query_pre, cosine, sine).astype(BF16)
    prior_keys, prior_values = halo[:, :KD], halo[:, KD:]

    def key_span(start):
        own = keys[max(start - rows, 0) : start + STRETCH]
        return own if start >= rows else jnp.concatenate([prior_keys[start:], own], axis=0)

    def value_span(start):
        own = values[max(start - rows, 0) : start + STRETCH]
        return own if start >= rows else jnp.concatenate([prior_values[start:], own], axis=0)

    head_index = (group_index * 2 + core).astype(F32)
    log_decay = jnp.log1p(-jnp.exp2(-5.0 - head_index))
    window = windows[0]
    span = rows + STRETCH

    def block_mask(start):
        return decay_mask(
            positions[start : start + STRETCH],
            key_positions[start : start + span],
            documents[start : start + STRETCH],
            key_documents[start : start + span],
            log_decay,
            window,
        )

    pieces = {}
    for start in reversed(range(0, pair_rows, STRETCH)):
        scores = dot(queries[start : start + STRETCH], key_span(start), ((1,), (1,)))
        weights = (scores * block_mask(start)).astype(BF16)
        pieces[start] = dot(weights, value_span(start))
    retained = jnp.concatenate([pieces[start] for start in sorted(pieces)], axis=0)
    heads_out = gate_norm(retained, gate_pre, group_gain_f, group_bias_f).astype(BF16)

    if small_mesh:
        out_low_x, out_high_y = stages.run((out_low, by_x), (out_high, by_y), late=(pieces[rows],))
        out_high_xy, out_low_xy = stages.run(
            (jnp.stack([out_high, out_high_y]), by_x), (jnp.stack([out_low, out_low_x]), by_y)
        )
        out_held = {
            0: (out_low, out_high),
            1: (out_low_x, out_high_xy[0]),
            2: (out_low_xy[0], out_high_y),
            3: (out_low_xy[1], out_high_xy[1]),
        }
        out_head = jnp.zeros((chips, 2, half_low, width), BF16)
        for d, (low, high) in out_held.items():
            out_head = put(out_head, jnp.stack([low, high])[None], chip ^ d, 0)
        out_head = out_head.reshape(groups * VD, width)
    else:
        out_head = lax.all_gather(out_weight, "seq", axis=0, tiled=True)
        out_head = pick(out_head.reshape(groups, 2, VD, width), core, 1).reshape(groups * VD, width)
    up_held, down_held = {0: up_four}, {0: down_weight}
    if small_mesh:
        (up_held[1],) = stages.run((up_four, by_y))
        down_held[1] = down_y
    else:
        for bit in range(2, devices.bit_length() - 1):
            for held in (up_held, down_held):
                held.update({d | (1 << (bit - 2)): flip(v, 1 << bit) for d, v in list(held.items())})
    up_quarter = jnp.zeros((devices, part, ff_quarter), BF16)
    for e, four in up_held.items():
        for d in range(4):
            up_quarter = put(up_quarter, four[d : d + 1], seq_index ^ (4 * e + d), 0)
    up_quarter = up_quarter.reshape(width, ff_quarter)
    down_quarter = jnp.concatenate(by_difference(down_held, quad), axis=0)

    def with_core(two):
        return jnp.concatenate([two, by_core(two)], axis=0)

    def quad_rows(block):
        return with_core(jnp.concatenate([block, by_x(block)], axis=0))

    def quad_sum(block):
        two = block[: 2 * own_rows] + by_core(block[2 * own_rows :].astype(BF16)).astype(F32)
        return two[:own_rows] + by_x(two[own_rows:].astype(BF16)).astype(F32)

    if small_mesh:
        quad_cotangent = with_core(jnp.concatenate([cotangent, cotangent_x], axis=0))
    else:
        quad_cotangent = quad_rows(cotangent)

    def to_tokens(block):
        parted = block.reshape(2, groups, own_rows, VD)
        result = jnp.zeros((2 * own_rows, groups * VD), BF16)
        for by in range(groups):
            sent = pick(parted, (group_index + by) % groups, 1).reshape(2 * own_rows, VD)
            result = put(result, turn(sent, by) if by else sent, (group_index - by) % groups, 1)
        return result

    def to_heads(block):
        result = jnp.zeros((2, groups, own_rows, VD), BF16)
        for by in range(groups):
            sent = cut(block, (group_index + by) % groups, VD, 1)
            came = turn(sent, by) if by else sent
            result = put(result, came.reshape(2, 1, own_rows, VD), (group_index - by) % groups, 1)
        return result.reshape(pair_rows, VD)

    def pair_sum(block, size, kind):
        mine = cut(block, core, size, 0)
        return mine + by_core(cut(block, 1 - core, size, 0).astype(kind)).astype(F32)

    def pair_rows_of(block):
        beside = by_core(block)
        return jnp.concatenate(
            [jnp.where(core == 0, block, beside), jnp.where(core == 0, beside, block)], axis=0
        )

    by_token = to_tokens(heads_out)
    hidden = inputs + pair_sum(dot(by_token, out_head), own_rows, F32)
    normed_two = layer_norm(hidden, gain_two, bias_two).astype(BF16)
    quad_normed = quad_rows(normed_two)
    pre_act = dot(quad_normed, up_quarter) + up_bias_quarter
    activated = jax.nn.gelu(pre_act, approximate=False).astype(BF16)

    grad_out = cotangent.astype(F32)
    down_bias_part = jnp.sum(grad_out, axis=0)
    grad_act = dot(quad_cotangent, down_quarter, ((1,), (1,)))
    gelu_back = jax.vjp(partial(jax.nn.gelu, approximate=False), pre_act)[1]
    grad_pre = gelu_back(grad_act)[0].astype(BF16)
    up_bias_part = jnp.sum(grad_pre.astype(F32), axis=0)
    down_part = dot(activated, quad_cotangent, ((0,), (0,))).astype(BF16).reshape(quads, ff_part, width)
    two_part = dot(grad_pre, up_quarter, ((1,), (1,)))
    if small_mesh:
        two = two_part[: 2 * own_rows] + by_core(two_part[2 * own_rows :].astype(BF16)).astype(F32)
        two_x, down_y = stages.run(
            (two[own_rows:].astype(BF16), by_x), (pick(down_part, 1 - quad), by_y), joined=False
        )
        grad_normed_two = two[:own_rows] + two_x.astype(F32)
    else:
        grad_normed_two = quad_sum(two_part)
    second_back = jax.vjp(layer_norm, hidden, gain_two, bias_two)[1]
    hidden_part, gain_two_part, bias_two_part = second_back(grad_normed_two)
    grad_hidden = grad_out + hidden_part
    grad_attend = pair_rows_of(grad_hidden.astype(BF16))
    grad_by_token = dot(grad_attend, out_head, ((1,), (1,))).astype(BF16)
    grad_heads = to_heads(grad_by_token)

    up_part = dot(quad_normed, grad_pre, ((0,), (0,))).astype(BF16).reshape(quads, 4, part, ff_quarter)
    out_part = dot(by_token, grad_attend, ((0,), (0,))).astype(BF16)

    def split_chips(parts):
        held, bit = dict(parts), 1
        while bit < chips:
            sent = {d: flip(v.astype(BF16), 2 * bit) for d, v in held.items() if d & bit}
            held = {
                d: v.astype(F32) + sent[d | bit].astype(F32) for d, v in held.items() if not d & bit
            }
            bit *= 2
        return held[0]

    def split_quads(block):
        held, bit = {d: pick(block, quad ^ d) for d in range(quads)}, 1
        while bit < quads:
            sent = {d: flip(v.astype(BF16), 4 * bit) for d, v in held.items() if d & bit}
            held = {
                d: v.astype(F32) + sent[d | bit].astype(F32) for d, v in held.items() if not d & bit
            }
            bit *= 2
        return held[0]

    def plus(mine, came):
        return mine.astype(F32) + came.astype(F32)

    def up_to_owners(up_four, up_x):
        up_core = by_core(jnp.stack([pick(up_four, quarter ^ 1), up_x[1]]))
        up_blocks = by_difference([pick(up_four, quarter), up_core[0], up_x[0], up_core[1]], quarter)
        return jnp.concatenate(
            [block[:, m * ff_part : (m + 1) * ff_part] for m in range(quads) for block in up_blocks], axis=1
        )

    def up_x_sent(up_four):
        return jnp.stack([pick(up_four, quarter ^ 2), pick(up_four, quarter ^ 3)])

    mixed_part = dot(activated, down_quarter)
    if small_mesh:
        mixed_two = plus(mixed_part[: 2 * own_rows], by_core(mixed_part[2 * own_rows :].astype(BF16)))
        down_sum = plus(pick(down_part, quad), down_y).astype(BF16)
        out_part = out_part.reshape(chips, 2, half_low, width)
        low, high = ([pick(out_part[:, i], chip ^ d) for d in range(chips)] for i in (0, 1))
        high_x, up_y = stages.run(
            (jnp.stack([high[1], high[3]]), by_x), (pick(up_part, 1 - quad), by_y), late=(grad_by_token,)
        )
        up_four = plus(pick(up_part, quad), up_y).astype(BF16)
        up_x, low_y = stages.run(
            (up_x_sent(up_four), by_x), (jnp.stack([low[2], low[3]]), by_y), late=(grad_heads,)
        )
    else:
        mixed_sum = quad_sum(mixed_part)
        down_sum = split_quads(down_part).astype(BF16)
        up_four = split_quads(up_part).astype(BF16)
        up_x = by_x(up_x_sent(up_four))
        spread = jnp.zeros((groups, 2, VD, width), BF16)
        spread = put(spread, out_part.reshape(groups, 1, VD, width), core, 1)
        out_sum = lax.psum_scatter(
            spread.reshape(groups * 2 * VD, width), "seq", scatter_dimension=0, tiled=True
        )
    up_sum = up_to_owners(up_four, up_x)
    down_sum = lax.psum(after(down_sum, grad_heads), "grp")
    gate_back = jax.vjp(gate_norm, retained, gate_pre, group_gain_f, group_bias_f)[1]
    grad_retained, grad_gate, group_gain_part, group_bias_part = gate_back(grad_heads.astype(F32))
    grad_retained = grad_retained.astype(BF16)
    grad_gate = grad_gate.astype(BF16)
    key_sums = jnp.zeros((3 * rows, KD), F32)
    value_sums = jnp.zeros((3 * rows, VD), F32)
    query_parts = []
    for start in range(0, pair_rows, STRETCH):
        mask = block_mask(start)
        block_queries = queries[start : start + STRETCH]
        block_keys, block_values = key_span(start), value_span(start)
        block_grad = grad_retained[start : start + STRETCH]
        weights = (dot(block_queries, block_keys, ((1,), (1,))) * mask).astype(BF16)
        grad_scores = (dot(block_grad, block_values, ((1,), (1,))) * mask).astype(BF16)
        value_sums = value_sums.at[start : start + span].add(dot(weights, block_grad, ((0,), (0,))))
        key_sums = key_sums.at[start : start + span].add(dot(grad_scores, block_queries, ((0,), (0,))))
        query_parts.append(dot(grad_scores, block_keys))
    grad_queries = jnp.concatenate(query_parts, axis=0)
    later = jnp.concatenate([key_sums[:rows], value_sums[:rows]], axis=1).astype(BF16)
    if small_mesh:
        (later,) = stages.run((later, lambda v: hop(v, -2)))
        low_x, high_y = stages.run(
            (plus(low[1], low_y[1]).astype(BF16), by_x), (plus(high[2], high_x[1]).astype(BF16), by_y)
        )
        low_sum = plus(plus(low[0], low_y[0]), low_x)
        high_sum = plus(plus(high[0], high_x[0]), high_y)
        out_sum = jnp.concatenate([low_sum, high_sum], axis=0)
    else:
        later = hop(later, -2)
    up_sum = lax.psum(after(up_sum, down_sum), "grp")
    out_sum = lax.psum(after(out_sum.astype(BF16), up_sum), "grp")
    down_grad, up_grad, out_grad = down_sum.astype(F32), up_sum.astype(F32), out_sum.astype(F32)

    own_keys = key_sums[rows:].at[rows:].add(later[:, :KD].astype(F32))
    grad_values = value_sums[rows:].at[rows:].add(later[:, KD:].astype(F32)).astype(BF16)
    grad_query = rotate_back(grad_queries, cosine, sine).astype(BF16)
    grad_key = (rotate_back(own_keys, cosine, sine) * key_scale).astype(BF16)
    grads = jnp.concatenate([grad_query, grad_key, grad_values, grad_gate], axis=1)

    normed_part = pair_sum(dot(grads, head_weight, ((1,), (1,))), rows, BF16)
    grad_normed = group_scatter(normed_part, group_index)
    head_part = dot(pair_normed, grads, ((0,), (0,)))
    product_part = jnp.sum(head_part * head_weight.astype(F32), axis=1)
    bias_one_part = jnp.sum(head_weight.astype(F32) * jnp.sum(grads.astype(F32), axis=0)[None], axis=1)
    gain_one_part = (product_part - bias_one * bias_one_part) / gain_one
    head_part = head_part.astype(BF16).reshape(chips, 2, part, columns)
    parts = {d: pick(head_part, chip ^ d) for d in range(chips)}
    if small_mesh:
        high_x, low_y = stages.run(
            (jnp.stack([parts[1][1], parts[3][1]]), by_x), (jnp.stack([parts[2][0], parts[3][0]]), by_y)
        )
        low_x, high_y = stages.run(
            (plus(parts[1][0], low_y[1]).astype(BF16), by_x),
            (plus(parts[2][1], high_x[1]).astype(BF16), by_y),
        )
        (mixed_x,) = stages.run((mixed_two[own_rows:].astype(BF16), by_x))
        mixed_sum = plus(mixed_two[:own_rows], mixed_x)
        low_sum = plus(plus(parts[0][0], low_y[0]), low_x)
        high_sum = plus(plus(parts[0][1], high_x[0]), high_y)
    else:
        low_sum, high_sum = split_chips(parts)
    mixed = (hidden + mixed_sum + down_bias_full).astype(BF16)
    own_head = jnp.where(core == 0, low_sum, high_sum)
    other_head = by_core(jnp.where(core == 0, high_sum, low_sum).astype(BF16)).astype(F32)
    first_head = jnp.where(core == 0, own_head, other_head)
    second_head = jnp.where(core == 0, other_head, own_head)

    def both_heads(start, size):
        return jnp.concatenate(
            [first_head[:, start : start + size], second_head[:, start : start + size]], axis=1
        )

    query_grad, key_grad = both_heads(0, KD), both_heads(KD, KD)
    value_grad, gate_grad = both_heads(2 * KD, VD), both_heads(2 * KD + VD, VD)

    up_bias_whole = put(jnp.zeros((quads, 4, ff_part), F32), up_bias_part.reshape(quads, 1, ff_part), quarter, 1)
    group_whole = jnp.zeros((groups, 2, 2, VD), F32)
    group_pair = jnp.stack([group_gain_part.reshape(-1), group_bias_part.reshape(-1)])
    group_whole = lax.dynamic_update_slice(group_whole, group_pair[None, None], (group_index, core, 0, 0))
    group_rows = group_whole.reshape(groups, 4, devices, VD // devices).transpose(2, 0, 1, 3)
    pieces = [
        item.reshape(devices, -1)
        for item in (
            gain_one_part,
            bias_one_part,
            gain_two_part,
            bias_two_part,
            down_bias_part,
            up_bias_whole,
            group_rows,
        )
    ]
    sums = small_sum(jnp.concatenate(pieces, axis=1))
    sums = pick(sums, seq_index)
    first_back = jax.vjp(lambda v: layer_norm(v, gain_one, bias_one), inputs)[1]
    tokens_grad = (grad_hidden + first_back(after(grad_normed, sums))[0]).astype(BF16)
    taken, start = [], 0
    for item in pieces:
        taken.append(sums[start : start + item.shape[1]])
        start += item.shape[1]
    first_gain_grad, first_bias_grad, second_gain_grad, second_bias_grad = taken[:4]
    down_bias_grad, up_bias_grad = taken[4:6]
    group_own = pick(taken[6].reshape(groups, 2, 2, VD // devices), group_index)
    group_gain_grad, group_bias_grad = group_own[:, 0].T, group_own[:, 1].T
    return (
        mixed,
        tokens_grad,
        first_gain_grad,
        first_bias_grad,
        query_grad,
        key_grad,
        value_grad,
        gate_grad,
        group_gain_grad,
        group_bias_grad,
        out_grad,
        second_gain_grad,
        second_bias_grad,
        up_grad,
        up_bias_grad,
        down_grad,
        down_bias_grad,
    )


def solution(mesh):
    placed = (
        P(("seq", "grp"), None),
        P("seq"),
        P("seq"),
        P("seq", "grp"),
        P("seq", "grp"),
        P("seq", "grp"),
        P("seq", "grp"),
        P("seq", "grp"),
        P("seq", "grp"),
        P("seq", None),
        P("seq"),
        P("seq"),
        P("seq", None),
        P("seq"),
        P("seq", None),
        P("seq"),
        P(("seq", "grp"), None),
        P(),
        P("grp"),
    )
    return jax.shard_map(
        body,
        mesh=mesh,
        in_specs=placed,
        out_specs=(
            P(("seq", "grp"), None),
            P(("seq", "grp"), None),
            P("seq"),
            P("seq"),
            P("seq", "grp"),
            P("seq", "grp"),
            P("seq", "grp"),
            P("seq", "grp"),
            P("seq", "grp"),
            P("seq", "grp"),
            P("seq", None),
            P("seq"),
            P("seq"),
            P("seq", None),
            P("seq"),
            P("seq", None),
            P("seq"),
        ),
        check_vma=False,
    )
```

time: 1550 us -> 999 us (0.64)
  waiting for transfers between devices: 908 us -> 416 us
  blocking collectives: 190 us -> 10.2 us
  matrix products: 257 us -> 163 us
  other arithmetic: 76.1 us -> 170 us
  starting transfers between devices: 13.9 us -> 85 us
  local copies, waits for them, and re-layouts: 73.5 us -> 128 us
    ppermute x4 -> x56, waiting for transfers between devices: 13.2 us -> 414 us  [the longest x37 238 us: flip(): return lax.ppermute(block, 'seq', [(i, i ^ bit) for i in range(devices)])]
    reduce_scatter x8 -> x0, waiting for transfers between devices: 387 us -> none  [the longest x1 117 us: body(): lax.psum_scatter(down_part.astype(jnp.bfloat16), 'seq', scatter_dimension...]
    all_gather x7 -> x0, waiting for transfers between devices: 216 us -> none  [the longest x1 81.2 us: body(): lax.all_gather(up_weight, 'seq', axis=0, tiled=True)]
    psum x1 -> x3, waiting for transfers between devices: 177 us -> 2.35 us  [the longest x1 2.35 us: body(): out_sum = lax.psum(after(out_sum.astype(BF16), up_sum), 'grp')]
    dot_general x33 -> x39, matrix products: 257 us -> 163 us  [dot(): return lax.dot_general(a, b, (dims, ((), ())), preferred_element_type=F32)]
    all_gather x8 -> x1, blocking collectives: 101 us -> 10.2 us  [body(): lax.all_gather(after(jnp.concatenate(small)[None], theirs), 'seq', axis=0...]
    ppermute x4 -> x56, starting transfers between devices: 7.55 us -> 84.8 us  [the longest x37 27.8 us: flip(): return lax.ppermute(block, 'seq', [(i, i ^ bit) for i in range(devices)])]
    all_gather x1, waiting for transfers between devices: 60.9 us -> 0.01 us  [body(): gathered = lax.all_gather(normed, 'grp', axis=0, tiled=True)]
  transfers between devices with their start and end apart: 24 -> 60, of which waited for: 16 -> 32; matrix products, arithmetic and copies ran while one was open for 21% -> 34% of each run, Pallas kernels for 0% -> 0%
where the time goes in v1:
time: 999 us; the launch traced here: 991 us
  waiting for transfers between devices  416 us (42%)
  other arithmetic  170 us (17%)
  matrix products  163 us (16%)
  local copies, waits for them, and re-layouts  128 us (13%)
  starting transfers between devices  85 us (9%)
  between operations  18 us (2%)
  blocking collectives  10.2 us (1%)
    ppermute x37, waiting for transfers between devices, flip(): return lax.ppermute(block, 'seq', [(i, i ^ bit) for i in range(devices)])  238 us
    dot_general x39, matrix products, dot(): return lax.dot_general(a, b, (dims, ((), ())), preferred_element_type=F32)  163 us
    ppermute x3, waiting for transfers between devices, group_scatter(): up = lax.ppermute(goes_up, 'grp', [(p, p + 1) for p in range(step)])  60.5 us
    unnamed x430, local copies, waits for them, and re-layouts  54.8 us
    ppermute x2, waiting for transfers between devices, hop(): lax.ppermute(block, 'seq', [(i, i + by) for i in range(devices) if 0 <= i...  53.3 us
    ppermute x6, waiting for transfers between devices, turn(): lax.ppermute(block, 'grp', [(i, (i + by) % groups) for i in range(groups)])  47.2 us
    ppermute x37, starting transfers between devices, flip(): return lax.ppermute(block, 'seq', [(i, i ^ bit) for i in range(devices)])  27.8 us
    ppermute x3, starting transfers between devices, group_scatter(): up = lax.ppermute(goes_up, 'grp', [(p, p + 1) for p in range(step)])  23.9 us
  transfers between devices with their start and end apart: 60, of which 32 were waited for; matrix products, arithmetic and copies ran while one was open for 34% of the time, Pallas kernels for 0%

profile of v1, /device:TPU:0, one launch (start us, length us, event | category | flops | bytes accessed | tf_op | source)
XLA Modules:
  0.0 991.0 jit_solution(2205438797637805085)
XLA Ops:
  15.3 10.2 %all-gather = bf16[8,1,2048]{2,1,0:T(2,128)(2,1)S(1)} all-gather(bf16[1,1,2048]{2,1,0:T(2,128)(2,1)S(1)} %bitcast.325), channel_id=1, replica_groups=mesh['seq'=8,'grp'=4] {'seq'}, dimensions={0}, use_global_device_ids=true | all-gather | bytes 36864 | tf_op jit(solution)/shard_map/all_gather | solution.py:213
  30.6 17.8 %collective-permute-done.1 = bf16[256,1536]{1,0:T(8,128)(2,1)S(1)} collective-permute-done((bf16[256,1536]{1,0:T(8,128)(2,1)S(1)}, bf16[256,1536]{1,0:T(8,128)(2,1)S(1)}, u32[]{:S(2)}, u32[]{:S(2)}) %collective-permute-start.1) | collective-permute-done | bytes 786464 | tf_op jit(solution)/shard_map/ppermute | solution.py:23
  56.7 30.9 %collective-permute-done.3 = bf16[2,256,1536]{2,1,0:T(8,128)(2,1)} collective-permute-done((bf16[2,256,1536]{2,1,0:T(8,128)(2,1)}, bf16[2,256,1536]{2,1,0:T(8,128)(2,1)}, u32[]{:S(2)}, u32[]{:S(2)}) %collective-permute-start.3) | collective-permute-done | bytes 1572896 | tf_op jit(solution)/shard_map/ppermute | solution.py:23
  90.2 44.3 %collective-permute-done.5 = bf16[2,256,2048]{2,1,0:T(8,128)(2,1)} collective-permute-done((bf16[2,256,2048]{2,1,0:T(8,128)(2,1)}, bf16[2,256,2048]{2,1,0:T(8,128)(2,1)}, u32[]{:S(2)}, u32[]{:S(2)}) %collective-permute-start.5) | collective-permute-done | bytes 2097184 | tf_op jit(solution)/shard_map/ppermute | solution.py:23
  154.4 6.6 convolution_convert_fusion.4
  166.1 4.8 fusion.130
  181.8 27.2 %collective-permute-done.8 = bf16[1024,768]{1,0:T(8,128)(2,1)S(1)} collective-permute-done((bf16[1024,768]{1,0:T(8,128)(2,1)S(1)}, bf16[1024,768]{1,0:T(8,128)(2,1)S(1)}, u32[]{:S(2)}, u32[]{:S(2)}) %collective-permute-start.8) | collective-permute-done | bytes 1572896 | tf_op jit(solution)/shard_map/ppermute | solution.py:28
  223.5 11.1 %collective-permute-done.12 = bf16[256,2048]{1,0:T(8,128)(2,1)S(1)} collective-permute-done((bf16[256,2048]{1,0:T(8,128)(2,1)S(1)}, bf16[256,2048]{1,0:T(8,128)(2,1)S(1)}, u32[]{:S(2)}, u32[]{:S(2)}) %collective-permute-start.12) | collective-permute-done | bytes 1048608 | tf_op jit(solution)/shard_map/ppermute | solution.py:23
  242.3 10.9 %multiply_convert_fusion.1 = (bf16[2048,512]{1,0:T(8,128)(2,1)S(1)}, f32[2048,512]{1,0:T(8,128)}) fusion(f32[512]{0:T(512)S(1)} %add.612, f32[512]{0:T(512)S(1)} %mul.528, f32[2048]{0:T(1024)S(1)} %fusion.166, f32[2048]{0:T(1024)S(1)} %broadcast_multiply_fusion, f32[512,512]{1,0:T(8,128)S(1)} %fusion.114, f32[512,512]{1,0:T(8,128)S(1)} %fusion.117, ...), kind=kOutput, calls=%fused_computation.58 | convolution fusion | flops 4325376000 | bytes 20992000 | tf_op jit(solution)/shard_map/dot_general | solution.py:18
  262.4 9.2 collective-permute-done.9
  272.7 18.3 %collective-permute-done.10 = bf16[512,512]{1,0:T(8,128)(2,1)S(1)} collective-permute-done((bf16[512,512]{1,0:T(8,128)(2,1)}, bf16[512,512]{1,0:T(8,128)(2,1)S(1)}, u32[]{:S(2)}, u32[]{:S(2)}) %collective-permute-start.10) | collective-permute-done | bytes 524320 | tf_op jit(solution)/shard_map/ppermute | solution.py:33
  297.2 4.6 fusion.223
  322.6 20.5 %collective-permute-done.17 = bf16[256,2048]{1,0:T(8,128)(2,1)} collective-permute-done((bf16[256,2048]{1,0:T(8,128)(2,1)}, bf16[256,2048]{1,0:T(8,128)(2,1)}, u32[]{:S(2)}, u32[]{:S(2)}) %collective-permute-start.17) | collective-permute-done | bytes 1048608 | tf_op jit(solution)/shard_map/ppermute | solution.py:23
  348.7 20.0 %collective-permute-done.20 = bf16[4,256,1024]{2,1,0:T(8,128)(2,1)} collective-permute-done((bf16[4,256,1024]{2,1,0:T(8,128)(2,1)}, bf16[4,256,1024]{2,1,0:T(8,128)(2,1)}, u32[]{:S(2)}, u32[]{:S(2)}) %collective-permute-start.20) | collective-permute-done | bytes 2097184 | tf_op jit(solution)/shard_map/ppermute | solution.py:23
  376.2 20.1 %multiply_convert_fusion = (bf16[1024,1024]{1,0:T(8,128)(2,1)}, f32[1024,1024]{1,0:T(8,128)}, f32[1024,1024]{1,0:T(8,128)}) fusion(f32[1024]{0:T(1024)S(1)} %bitcast.328, bf16[2048,1024]{1,0:T(8,128)(2,1)} %bitcast.38, bf16[512,2048]{1,0:T(8,128)(2,1)S(1)} %collective-permute-done.18, bf16[256,2048]{1,0:T(8,128)(2,1)} %collective-permute-done.17, ...), kind=kOutput, calls=%fused_computation.45 | convolution fusion | flops 4376756224 | bytes 18878464 | tf_op jit(solution)/shard_map/dot_general | solution.py:18
  397.6 10.0 %convert_reduce_fusion.1 = (f32[1024]{0:T(1024)S(1)}, bf16[1024,1024]{1,0:T(8,128)(2,1)S(1)}) fusion(f32[1024,1024]{1,0:T(8,128)} %get-tuple-element.279, bf16[512,2048]{1,0:T(8,128)(2,1)S(1)} %get-tuple-element.309, bf16[512,2048]{1,0:T(8,128)(2,1)S(1)} %get-tuple-element.308, bf16[512,2048]{1,0:T(8,128)(2,1)} %copy-done.190, ...), kind=kOutput, calls=%fused_computation.41 | convolution fusion | flops 4333763584 | bytes 18882560 | tf_op jit(solution)/shard_map/dot_general | solution.py:18
  407.6 7.3 fusion.224
  416.5 4.5 fusion.57
  427.2 4.9 convolution_convert_fusion.2
  439.3 7.9 convolution_convert_fusion.1
  452.0 10.9 %collective-permute-done.24 = bf16[256,2048]{1,0:T(8,128)(2,1)} collective-permute-done((bf16[256,2048]{1,0:T(8,128)(2,1)}, bf16[256,2048]{1,0:T(8,128)(2,1)}, u32[]{:S(2)}, u32[]{:S(2)}) %collective-permute-start.24) | collective-permute-done | bytes 1048608 | tf_op jit(solution)/shard_map/ppermute | solution.py:23
  475.9 22.3 %collective-permute-done.29 = bf16[512,2048]{1,0:T(8,128)(2,1)} collective-permute-done((bf16[512,2048]{1,0:T(8,128)(2,1)}, bf16[512,2048]{1,0:T(8,128)(2,1)}, u32[]{:S(2)}, u32[]{:S(2)}) %collective-permute-start.29) | collective-permute-done | bytes 2097184 | tf_op jit(solution)/shard_map/ppermute | solution.py:23
  498.2 4.4 fusion.4
  502.8 8.6 convolution_convert_fusion.3
  511.5 4.8 convolution_convert_fusion
  516.5 11.7 %collective-permute-start.26 = (bf16[512,512]{1,0:T(8,128)(2,1)S(1)}, bf16[512,512]{1,0:T(8,128)(2,1)S(1)}, u32[]{:S(2)}, u32[]{:S(2)}) collective-permute-start(bf16[512,512]{1,0:T(8,128)(2,1)S(1)} %get-tuple-element.321), channel_id=1, source_target_pairs={{0,1},{1,2},{2,3},{3,0},{4,5},{5,6},{6,7},{7,4},{8,9},{9,10},{10,1... | collective-permute-start | bytes 1572872 | tf_op jit(solution)/shard_map/ppermute | solution.py:33
  543.2 19.0 %collective-permute-done.27 = bf16[512,512]{1,0:T(8,128)(2,1)S(1)} collective-permute-done((bf16[512,512]{1,0:T(8,128)(2,1)S(1)}, bf16[512,512]{1,0:T(8,128)(2,1)S(1)}, u32[]{:S(2)}, u32[]{:S(2)}) %collective-permute-start.27) | collective-permute-done | bytes 524320 | tf_op jit(solution)/shard_map/ppermute | solution.py:33
  564.1 6.0 multiply_reduce_fusion.2
  612.3 5.4 fusion.148
  617.7 5.4 fusion.147
  623.1 11.7 %collective-permute-done.32 = bf16[2,256,1024]{2,1,0:T(8,128)(2,1)S(1)} collective-permute-done((bf16[2,256,1024]{2,1,0:T(8,128)(2,1)S(1)}, bf16[2,256,1024]{2,1,0:T(8,128)(2,1)S(1)}, u32[]{:S(2)}, u32[]{:S(2)}) %collective-permute-start.32) | collective-permute-done | bytes 1048608 | tf_op jit(solution)/shard_map/ppermute | solution.py:23
  634.8 19.9 %collective-permute-done.33 = bf16[2,256,2048]{2,1,0:T(8,128)(2,1)S(1)} collective-permute-done((bf16[2,256,2048]{2,1,0:T(8,128)(2,1)S(1)}, bf16[2,256,2048]{2,1,0:T(8,128)(2,1)S(1)}, u32[]{:S(2)}, u32[]{:S(2)}) %collective-permute-start.33) | collective-permute-done | bytes 2097184 | tf_op jit(solution)/shard_map/ppermute | solution.py:23
  662.1 4.3 convert_element_type.484
  679.5 26.1 %collective-permute-done.34 = bf16[1024,768]{1,0:T(8,128)(2,1)} collective-permute-done((bf16[1024,768]{1,0:T(8,128)(2,1)}, bf16[1024,768]{1,0:T(8,128)(2,1)}, u32[]{:S(2)}, u32[]{:S(2)}) %collective-permute-start.34) | collective-permute-done | bytes 1572896 | tf_op jit(solution)/shard_map/ppermute | solution.py:28
  710.2 7.4 fusion.124
  723.7 6.0 fusion.84
  729.7 17.7 %fusion.225 = f32[2048,2048]{1,0:T(8,128)} fusion(bf16[2048,1536]{1,0:T(8,128)(2,1)} %fusion.84, bf16[2048,1536]{1,0:T(8,128)(2,1)S(1)} %bitcast.279), kind=kOutput, calls=%fused_computation.509 | convolution fusion | flops 12884901888 | bytes 29360128 | tf_op jit(solution)/shard_map/dot_general | solution.py:18
  747.4 6.0 dynamic-slice_convert_fusion
  753.4 18.7 %multiply_reduce_fusion.1 = (f32[2048]{0:T(1024)S(1)}, bf16[2048,1536]{1,0:T(8,128)(2,1)S(1)}) fusion(bf16[4,2,256,1536]{3,2,1,0:T(8,128)(2,1)S(1)} %bitcast.278, bf16[2048,1536]{1,0:T(8,128)(2,1)} %fusion.84, bf16[1024,2048]{1,0:T(8,128)(2,1)} %copy-done.56, bf16[1024,2048]{1,0:T(8,128)(2,1)} %copy-done.55), kind=kOutput, calls=%fused_computation.2 | convolution fusion | flops 12914259968 | bytes 27271168 | tf_op jit(solution)/shard_map/dot_general | solution.py:18
  789.3 25.1 %collective-permute-done.37 = bf16[2,256,1536]{2,1,0:T(8,128)(2,1)S(1)} collective-permute-done((bf16[2,256,1536]{2,1,0:T(8,128)(2,1)}, bf16[2,256,1536]{2,1,0:T(8,128)(2,1)S(1)}, u32[]{:S(2)}, u32[]{:S(2)}) %collective-permute-start.37) | collective-permute-done | bytes 1572896 | tf_op jit(solution)/shard_map/ppermute | solution.py:23
  821.0 6.0 convert_add_fusion
  831.9 14.0 %collective-permute-start.43 = (bf16[256,2048]{1,0:T(8,128)(2,1)}, bf16[256,2048]{1,0:T(8,128)(2,1)}, u32[]{:S(2)}, u32[]{:S(2)}) collective-permute-start(bf16[256,2048]{1,0:T(8,128)(2,1)} %get-tuple-element.248), channel_id=1, source_target_pairs={{0,1},{4,5},{8,9},{12,13},{16,17},{20,21},{24,25},{28,29}} | collective-permute-start | bytes 3145736 | tf_op jit(solution)/shard_map/ppermute | solution.py:99
  855.2 33.5 %collective-permute-done.43 = bf16[256,2048]{1,0:T(8,128)(2,1)} collective-permute-done((bf16[256,2048]{1,0:T(8,128)(2,1)}, bf16[256,2048]{1,0:T(8,128)(2,1)}, u32[]{:S(2)}, u32[]{:S(2)}) %collective-permute-start.43) | collective-permute-done | bytes 1048608 | tf_op jit(solution)/shard_map/ppermute | solution.py:99
  888.7 4.8 add_convert_fusion.5
  893.6 5.4 collective-permute-start.45
  913.1 9.7 collective-permute-done.45
  926.3 4.5 collective-permute-start.47
  933.8 17.3 %collective-permute-done.47 = bf16[256,2048]{1,0:T(8,128)(2,1)S(1)} collective-permute-done((bf16[256,2048]{1,0:T(8,128)(2,1)S(1)}, bf16[256,2048]{1,0:T(8,128)(2,1)S(1)}, u32[]{:S(2)}, u32[]{:S(2)}) %collective-permute-start.47) | collective-permute-done | bytes 1048608 | tf_op jit(solution)/shard_map/ppermute | solution.py:99
  (771 shorter events, 345.4 us)
Async XLA Ops:
  7.3 127.5 %all-gather.3.cloned.1.call-start = ((), (), s32[]{:S(2)}) async-start(), calls=%async_computation | async-start | bytes 5242880 | tf_op jit(solution)/shard_map/all_gather | solution.py:228
  27.1 635.1 %all-reduce.6.cloned.1.call-start = ((), (), s32[]{:S(2)}) async-start(), calls=%async_computation.1 | async-start | bytes 4194304 | tf_op jit(solution)/shard_map/psum | solution.py:492
  28.6 19.8 %collective-permute-start.1 = (bf16[256,1536]{1,0:T(8,128)(2,1)S(1)}, bf16[256,1536]{1,0:T(8,128)(2,1)S(1)}, u32[]{:S(2)}, u32[]{:S(2)}) collective-permute-start(bf16[256,1536]{1,0:T(8,128)(2,1)S(1)} %get-tuple-element.201), channel_id=1, source_target_pairs={{0,8},{4,12},{8,0},{12,4},{16,24},{20,28},{24,16},{28,20},{1,9},{5... | collective-permute-start | bytes 2359304 | tf_op jit(solution)/shard_map/ppermute | solution.py:23
  30.1 19.5 %collective-permute-start.2 = (bf16[256,1536]{1,0:T(8,128)(2,1)S(1)}, bf16[256,1536]{1,0:T(8,128)(2,1)S(1)}, u32[]{:S(2)}, u32[]{:S(2)}) collective-permute-start(bf16[256,1536]{1,0:T(8,128)(2,1)S(1)} %get-tuple-element.202), channel_id=1, source_target_pairs={{0,16},{4,20},{8,24},{12,28},{16,0},{20,4},{24,8},{28,12},{1,17},{... | collective-permute-start | bytes 2359304 | tf_op jit(solution)/shard_map/ppermute | solution.py:23
  51.6 35.9 %collective-permute-start.3 = (bf16[2,256,1536]{2,1,0:T(8,128)(2,1)}, bf16[2,256,1536]{2,1,0:T(8,128)(2,1)}, u32[]{:S(2)}, u32[]{:S(2)}) collective-permute-start(bf16[2,256,1536]{2,1,0:T(8,128)(2,1)} %get-tuple-element.205), channel_id=1, source_target_pairs={{0,8},{4,12},{8,0},{12,4},{16,24},{20,28},{24,16},{28,20},{1,9},{5... | collective-permute-start | bytes 4718600 | tf_op jit(solution)/shard_map/ppermute | solution.py:23
  52.2 36.0 %collective-permute-start.4 = (bf16[2,256,1536]{2,1,0:T(8,128)(2,1)}, bf16[2,256,1536]{2,1,0:T(8,128)(2,1)}, u32[]{:S(2)}, u32[]{:S(2)}) collective-permute-start(bf16[2,256,1536]{2,1,0:T(8,128)(2,1)} %get-tuple-element.206), channel_id=1, source_target_pairs={{0,16},{4,20},{8,24},{12,28},{16,0},{20,4},{24,8},{28,12},{1,17},{... | collective-permute-start | bytes 4718600 | tf_op jit(solution)/shard_map/ppermute | solution.py:23
  88.2 46.3 %collective-permute-start.5 = (bf16[2,256,2048]{2,1,0:T(8,128)(2,1)}, bf16[2,256,2048]{2,1,0:T(8,128)(2,1)}, u32[]{:S(2)}, u32[]{:S(2)}) collective-permute-start(bf16[2,256,2048]{2,1,0:T(8,128)(2,1)} %pad_maximum_fusion.13), channel_id=1, source_target_pairs={{0,8},{4,12},{8,0},{12,4},{16,24},{20,28},{24,16},{28,20},{1,9},{5... | collective-permute-start | bytes 6291464 | tf_op jit(solution)/shard_map/ppermute | solution.py:23
  89.3 45.5 %collective-permute-start.6 = (bf16[512,2048]{1,0:T(8,128)(2,1)S(1)}, bf16[512,2048]{1,0:T(8,128)(2,1)}, u32[]{:S(2)}, u32[]{:S(2)}) collective-permute-start(bf16[512,2048]{1,0:T(8,128)(2,1)S(1)} %copy-done.80), channel_id=1, source_target_pairs={{0,16},{4,20},{8,24},{12,28},{16,0},{20,4},{24,8},{28,12},{1,17},{... | collective-permute-start | bytes 6291464 | tf_op jit(solution)/shard_map/ppermute | solution.py:23
  171.5 37.5 %collective-permute-start.8 = (bf16[1024,768]{1,0:T(8,128)(2,1)S(1)}, bf16[1024,768]{1,0:T(8,128)(2,1)S(1)}, u32[]{:S(2)}, u32[]{:S(2)}) collective-permute-start(bf16[1024,768]{1,0:T(8,128)(2,1)S(1)} %pad_maximum_fusion.30), channel_id=1, source_target_pairs={{0,8},{4,12},{8,16},{12,20},{16,24},{20,28},{1,9},{5,13},{9,17},{1... | collective-permute-start | bytes 4718600 | tf_op jit(solution)/shard_map/ppermute | solution.py:28
  209.0 25.6 %collective-permute-start.12 = (bf16[256,2048]{1,0:T(8,128)(2,1)S(1)}, bf16[256,2048]{1,0:T(8,128)(2,1)S(1)}, u32[]{:S(2)}, u32[]{:S(2)}) collective-permute-start(bf16[256,2048]{1,0:T(8,128)(2,1)S(1)} %copy-done.100), channel_id=1, source_target_pairs={{0,8},{4,12},{8,0},{12,4},{16,24},{20,28},{24,16},{28,20},{1,9},{5... | collective-permute-start | bytes 3145736 | tf_op jit(solution)/shard_map/ppermute | solution.py:23
  211.5 24.5 %collective-permute-start.13 = (bf16[256,2048]{1,0:T(8,128)(2,1)S(1)}, bf16[256,2048]{1,0:T(8,128)(2,1)S(1)}, u32[]{:S(2)}, u32[]{:S(2)}) collective-permute-start(bf16[256,2048]{1,0:T(8,128)(2,1)S(1)} %copy-done.99), channel_id=1, source_target_pairs={{0,16},{4,20},{8,24},{12,28},{16,0},{20,4},{24,8},{28,12},{1,17},{... | collective-permute-start | bytes 3145736 | tf_op jit(solution)/shard_map/ppermute | solution.py:23
  239.2 52.0 %collective-permute-start.14 = (bf16[2,256,2048]{2,1,0:T(8,128)(2,1)}, bf16[2,256,2048]{2,1,0:T(8,128)(2,1)}, u32[]{:S(2)}, u32[]{:S(2)}) collective-permute-start(bf16[2,256,2048]{2,1,0:T(8,128)(2,1)} %pad_maximum_fusion.12), channel_id=1, source_target_pairs={{0,8},{4,12},{8,0},{12,4},{16,24},{20,28},{24,16},{28,20},{1,9},{5... | collective-permute-start | bytes 6291464 | tf_op jit(solution)/shard_map/ppermute | solution.py:23
  240.5 50.7 %collective-permute-start.15 = (bf16[2,256,2048]{2,1,0:T(8,128)(2,1)}, bf16[2,256,2048]{2,1,0:T(8,128)(2,1)}, u32[]{:S(2)}, u32[]{:S(2)}) collective-permute-start(bf16[2,256,2048]{2,1,0:T(8,128)(2,1)} %pad_maximum_fusion.9), channel_id=1, source_target_pairs={{0,16},{4,20},{8,24},{12,28},{16,0},{20,4},{24,8},{28,12},{1,17},{... | collective-permute-start | bytes 6291464 | tf_op jit(solution)/shard_map/ppermute | solution.py:23
  256.1 34.9 %collective-permute-start.10 = (bf16[512,512]{1,0:T(8,128)(2,1)}, bf16[512,512]{1,0:T(8,128)(2,1)S(1)}, u32[]{:S(2)}, u32[]{:S(2)}) collective-permute-start(bf16[512,512]{1,0:T(8,128)(2,1)} %bitcast.313), channel_id=1, source_target_pairs={{0,2},{1,3},{2,0},{3,1},{4,6},{5,7},{6,4},{7,5},{8,10},{9,11},{10,... | collective-permute-start | bytes 1572872 | tf_op jit(solution)/shard_map/ppermute | solution.py:33
  258.6 32.4 %collective-permute-start.11 = (bf16[512,512]{1,0:T(8,128)(2,1)}, bf16[512,512]{1,0:T(8,128)(2,1)S(1)}, u32[]{:S(2)}, u32[]{:S(2)}) collective-permute-start(bf16[512,512]{1,0:T(8,128)(2,1)} %bitcast.312), channel_id=1, source_target_pairs={{0,3},{1,0},{2,1},{3,2},{4,7},{5,4},{6,5},{7,6},{8,11},{9,8},{10,9... | collective-permute-start | bytes 1572872 | tf_op jit(solution)/shard_map/ppermute | solution.py:33
  317.2 25.9 %collective-permute-start.17 = (bf16[256,2048]{1,0:T(8,128)(2,1)}, bf16[256,2048]{1,0:T(8,128)(2,1)}, u32[]{:S(2)}, u32[]{:S(2)}) collective-permute-start(bf16[256,2048]{1,0:T(8,128)(2,1)} %add_convert_fusion.7), channel_id=1, source_target_pairs={{0,8},{4,12},{8,0},{12,4},{16,24},{20,28},{24,16},{28,20},{1,9},{5... | collective-permute-start | bytes 3145736 | tf_op jit(solution)/shard_map/ppermute | solution.py:23
  320.5 48.1 %collective-permute-start.20 = (bf16[4,256,1024]{2,1,0:T(8,128)(2,1)}, bf16[4,256,1024]{2,1,0:T(8,128)(2,1)}, u32[]{:S(2)}, u32[]{:S(2)}) collective-permute-start(bf16[4,256,1024]{2,1,0:T(8,128)(2,1)} %pad_maximum_fusion.15), channel_id=1, source_target_pairs={{0,16},{4,20},{8,24},{12,28},{16,0},{20,4},{24,8},{28,12},{1,17},{... | collective-permute-start | bytes 6291464 | tf_op jit(solution)/shard_map/ppermute | solution.py:23
  322.5 73.8 %collective-permute-start.22 = (bf16[512,2048]{1,0:T(8,128)(2,1)S(1)}, bf16[512,2048]{1,0:T(8,128)(2,1)S(1)}, u32[]{:S(2)}, u32[]{:S(2)}) collective-permute-start(bf16[512,2048]{1,0:T(8,128)(2,1)S(1)} %pad_maximum_fusion.16), channel_id=1, source_target_pairs={{0,4},{4,0},{8,12},{12,8},{16,20},{20,16},{24,28},{28,24},{1,5},{5... | collective-permute-start | bytes 6291464 | tf_op jit(solution)/shard_map/ppermute | solution.py:23
  344.8 31.3 %collective-permute-start.18 = (bf16[512,2048]{1,0:T(8,128)(2,1)S(1)}, bf16[512,2048]{1,0:T(8,128)(2,1)S(1)}, u32[]{:S(2)}, u32[]{:S(2)}) collective-permute-start(bf16[512,2048]{1,0:T(8,128)(2,1)S(1)} %pad_maximum_fusion.14), channel_id=1, source_target_pairs={{0,4},{4,0},{8,12},{12,8},{16,20},{20,16},{24,28},{28,24},{1,5},{5... | collective-permute-start | bytes 6291464 | tf_op jit(solution)/shard_map/ppermute | solution.py:23
  425.9 43.3 %collective-permute-start.21 = (bf16[512,2048]{1,0:T(8,128)(2,1)}, bf16[512,2048]{1,0:T(8,128)(2,1)}, u32[]{:S(2)}, u32[]{:S(2)}) collective-permute-start(bf16[512,2048]{1,0:T(8,128)(2,1)} %slice.1147), channel_id=1, source_target_pairs={{0,4},{4,0},{8,12},{12,8},{16,20},{20,16},{24,28},{28,24},{1,5},{5... | collective-permute-start | bytes 6291464 | tf_op jit(solution)/shard_map/ppermute | solution.py:23
  438.0 24.8 %collective-permute-start.24 = (bf16[256,2048]{1,0:T(8,128)(2,1)}, bf16[256,2048]{1,0:T(8,128)(2,1)}, u32[]{:S(2)}, u32[]{:S(2)}) collective-permute-start(bf16[256,2048]{1,0:T(8,128)(2,1)} %slice.1149), channel_id=1, source_target_pairs={{0,8},{4,12},{8,0},{12,4},{16,24},{20,28},{24,16},{28,20},{1,9},{5... | collective-permute-start | bytes 3145736 | tf_op jit(solution)/shard_map/ppermute | solution.py:23
  451.4 46.9 %collective-permute-start.29 = (bf16[512,2048]{1,0:T(8,128)(2,1)}, bf16[512,2048]{1,0:T(8,128)(2,1)}, u32[]{:S(2)}, u32[]{:S(2)}) collective-permute-start(bf16[512,2048]{1,0:T(8,128)(2,1)} %dynamic-slice_bitcast_fusion.1), channel_id=1, source_target_pairs={{0,16},{4,20},{8,24},{12,28},{16,0},{20,4},{24,8},{28,12},{1,17},{... | collective-permute-start | bytes 6291464 | tf_op jit(solution)/shard_map/ppermute | solution.py:23
  469.0 33.6 %collective-permute-start.25 = (bf16[256,2048]{1,0:T(8,128)(2,1)S(1)}, bf16[256,2048]{1,0:T(8,128)(2,1)S(1)}, u32[]{:S(2)}, u32[]{:S(2)}) collective-permute-start(bf16[256,2048]{1,0:T(8,128)(2,1)S(1)} %fusion.119), channel_id=1, source_target_pairs={{0,4},{4,0},{8,12},{12,8},{16,20},{20,16},{24,28},{28,24},{1,5},{5... | collective-permute-start | bytes 3145736 | tf_op jit(solution)/shard_map/ppermute | solution.py:23
  516.5 25.8 %collective-permute-start.26 = (bf16[512,512]{1,0:T(8,128)(2,1)S(1)}, bf16[512,512]{1,0:T(8,128)(2,1)S(1)}, u32[]{:S(2)}, u32[]{:S(2)}) collective-permute-start(bf16[512,512]{1,0:T(8,128)(2,1)S(1)} %get-tuple-element.321), channel_id=1, source_target_pairs={{0,1},{1,2},{2,3},{3,0},{4,5},{5,6},{6,7},{7,4},{8,9},{9,10},{10,1... | collective-permute-start | bytes 1572872 | tf_op jit(solution)/shard_map/ppermute | solution.py:33
  528.2 34.0 %collective-permute-start.27 = (bf16[512,512]{1,0:T(8,128)(2,1)S(1)}, bf16[512,512]{1,0:T(8,128)(2,1)S(1)}, u32[]{:S(2)}, u32[]{:S(2)}) collective-permute-start(bf16[512,512]{1,0:T(8,128)(2,1)S(1)} %get-tuple-element.320), channel_id=1, source_target_pairs={{0,2},{1,3},{2,0},{3,1},{4,6},{5,7},{6,4},{7,5},{8,10},{9,11},{10,... | collective-permute-start | bytes 1572872 | tf_op jit(solution)/shard_map/ppermute | solution.py:33
  530.0 33.1 %collective-permute-start.28 = (bf16[512,512]{1,0:T(8,128)(2,1)S(1)}, bf16[512,512]{1,0:T(8,128)(2,1)S(1)}, u32[]{:S(2)}, u32[]{:S(2)}) collective-permute-start(bf16[512,512]{1,0:T(8,128)(2,1)S(1)} %get-tuple-element.319), channel_id=1, source_target_pairs={{0,3},{1,0},{2,1},{3,2},{4,7},{5,4},{6,5},{7,6},{8,11},{9,8},{10,9... | collective-permute-start | bytes 1572872 | tf_op jit(solution)/shard_map/ppermute | solution.py:33
  536.6 63.4 %collective-permute-start.30 = (bf16[2,256,2048]{2,1,0:T(8,128)(2,1)}, bf16[2,256,2048]{2,1,0:T(8,128)(2,1)}, u32[]{:S(2)}, u32[]{:S(2)}) collective-permute-start(bf16[2,256,2048]{2,1,0:T(8,128)(2,1)} %pad_maximum_fusion.19), channel_id=1, source_target_pairs={{0,8},{4,12},{8,0},{12,4},{16,24},{20,28},{24,16},{28,20},{1,9},{5... | collective-permute-start | bytes 6291464 | tf_op jit(solution)/shard_map/ppermute | solution.py:23
  537.5 62.6 %collective-permute-start.31 = (bf16[4,256,1024]{2,1,0:T(8,128)(2,1)}, bf16[4,256,1024]{2,1,0:T(8,128)(2,1)}, u32[]{:S(2)}, u32[]{:S(2)}) collective-permute-start(bf16[4,256,1024]{2,1,0:T(8,128)(2,1)} %dynamic-slice_bitcast_fusion), channel_id=1, source_target_pairs={{0,16},{4,20},{8,24},{12,28},{16,0},{20,4},{24,8},{28,12},{1,17},{... | collective-permute-start | bytes 6291464 | tf_op jit(solution)/shard_map/ppermute | solution.py:23
  563.9 225.3 %all-reduce.8.cloned.1.call-start = ((), (), s32[]{:S(2)}) async-start(), calls=%async_computation.2 | async-start | bytes 4194304 | tf_op jit(solution)/shard_map/psum | solution.py:522
  607.1 47.5 %collective-permute-start.33 = (bf16[2,256,2048]{2,1,0:T(8,128)(2,1)S(1)}, bf16[2,256,2048]{2,1,0:T(8,128)(2,1)S(1)}, u32[]{:S(2)}, u32[]{:S(2)}) collective-permute-start(bf16[2,256,2048]{2,1,0:T(8,128)(2,1)S(1)} %copy-done.89), channel_id=1, source_target_pairs={{0,16},{4,20},{8,24},{12,28},{16,0},{20,4},{24,8},{28,12},{1,17},{... | collective-permute-start | bytes 6291464 | tf_op jit(solution)/shard_map/ppermute | solution.py:23
  609.9 24.9 %collective-permute-start.32 = (bf16[2,256,1024]{2,1,0:T(8,128)(2,1)S(1)}, bf16[2,256,1024]{2,1,0:T(8,128)(2,1)S(1)}, u32[]{:S(2)}, u32[]{:S(2)}) collective-permute-start(bf16[2,256,1024]{2,1,0:T(8,128)(2,1)S(1)} %pad_maximum_fusion.39), channel_id=1, source_target_pairs={{0,8},{4,12},{8,0},{12,4},{16,24},{20,28},{24,16},{28,20},{1,9},{5... | collective-permute-start | bytes 3145736 | tf_op jit(solution)/shard_map/ppermute | solution.py:23
  666.4 39.3 %collective-permute-start.34 = (bf16[1024,768]{1,0:T(8,128)(2,1)}, bf16[1024,768]{1,0:T(8,128)(2,1)}, u32[]{:S(2)}, u32[]{:S(2)}) collective-permute-start(bf16[1024,768]{1,0:T(8,128)(2,1)} %pad_maximum_fusion.33), channel_id=1, source_target_pairs={{8,0},{12,4},{16,8},{20,12},{24,16},{28,20},{9,1},{13,5},{17,9},{2... | collective-permute-start | bytes 4718600 | tf_op jit(solution)/shard_map/ppermute | solution.py:28
  679.5 226.8 %all-reduce.10.cloned.1.call-start = ((), (), s32[]{:S(2)}) async-start(), calls=%async_computation.3 | async-start | bytes 4194304 | tf_op jit(solution)/shard_map/psum | solution.py:523
  705.7 71.6 %collective-permute-start.35 = (bf16[256,2048]{1,0:T(8,128)(2,1)}, bf16[256,2048]{1,0:T(8,128)(2,1)}, u32[]{:S(2)}, u32[]{:S(2)}) collective-permute-start(bf16[256,2048]{1,0:T(8,128)(2,1)} %fusion.83), channel_id=1, source_target_pairs={{0,8},{4,12},{8,0},{12,4},{16,24},{20,28},{24,16},{28,20},{1,9},{5... | collective-permute-start | bytes 3145736 | tf_op jit(solution)/shard_map/ppermute | solution.py:23
  707.7 69.5 %collective-permute-start.36 = (bf16[256,2048]{1,0:T(8,128)(2,1)}, bf16[256,2048]{1,0:T(8,128)(2,1)}, u32[]{:S(2)}, u32[]{:S(2)}) collective-permute-start(bf16[256,2048]{1,0:T(8,128)(2,1)} %fusion.82), channel_id=1, source_target_pairs={{0,16},{4,20},{8,24},{12,28},{16,0},{20,4},{24,8},{28,12},{1,17},{... | collective-permute-start | bytes 3145736 | tf_op jit(solution)/shard_map/ppermute | solution.py:23
  753.4 67.6 %collective-permute-start.42 = (bf16[1024,2048]{1,0:T(8,128)(2,1)}, bf16[1024,2048]{1,0:T(8,128)(2,1)}, u32[]{:S(2)}, u32[]{:S(2)}) collective-permute-start(bf16[1024,2048]{1,0:T(8,128)(2,1)} %dynamic-slice_convert_fusion), channel_id=1, source_target_pairs={{0,4},{4,0},{8,12},{12,8},{16,20},{20,16},{24,28},{28,24},{1,5},{5... | collective-permute-start | bytes 12582920 | tf_op jit(solution)/shard_map/ppermute | solution.py:23
  777.2 37.1 %collective-permute-start.37 = (bf16[2,256,1536]{2,1,0:T(8,128)(2,1)}, bf16[2,256,1536]{2,1,0:T(8,128)(2,1)S(1)}, u32[]{:S(2)}, u32[]{:S(2)}) collective-permute-start(bf16[2,256,1536]{2,1,0:T(8,128)(2,1)} %pad_maximum_fusion.34), channel_id=1, source_target_pairs={{0,8},{4,12},{8,0},{12,4},{16,24},{20,28},{24,16},{28,20},{1,9},{5... | collective-permute-start | bytes 4718600 | tf_op jit(solution)/shard_map/ppermute | solution.py:23
  778.1 36.7 %collective-permute-start.38 = (bf16[2,256,1536]{2,1,0:T(8,128)(2,1)}, bf16[2,256,1536]{2,1,0:T(8,128)(2,1)S(1)}, u32[]{:S(2)}, u32[]{:S(2)}) collective-permute-start(bf16[2,256,1536]{2,1,0:T(8,128)(2,1)} %pad_maximum_fusion.35), channel_id=1, source_target_pairs={{0,16},{4,20},{8,24},{12,28},{16,0},{20,4},{24,8},{28,12},{1,17},{... | collective-permute-start | bytes 4718600 | tf_op jit(solution)/shard_map/ppermute | solution.py:23
  817.8 34.0 %collective-permute-start.39 = (bf16[256,1536]{1,0:T(8,128)(2,1)}, bf16[256,1536]{1,0:T(8,128)(2,1)}, u32[]{:S(2)}, u32[]{:S(2)}) collective-permute-start(bf16[256,1536]{1,0:T(8,128)(2,1)} %get-tuple-element.243), channel_id=1, source_target_pairs={{0,8},{4,12},{8,0},{12,4},{16,24},{20,28},{24,16},{28,20},{1,9},{5... | collective-permute-start | bytes 2359304 | tf_op jit(solution)/shard_map/ppermute | solution.py:23
  819.2 32.6 %collective-permute-start.40 = (bf16[256,1536]{1,0:T(8,128)(2,1)}, bf16[256,1536]{1,0:T(8,128)(2,1)}, u32[]{:S(2)}, u32[]{:S(2)}) collective-permute-start(bf16[256,1536]{1,0:T(8,128)(2,1)} %get-tuple-element.244), channel_id=1, source_target_pairs={{0,16},{4,20},{8,24},{12,28},{16,0},{20,4},{24,8},{28,12},{1,17},{... | collective-permute-start | bytes 2359304 | tf_op jit(solution)/shard_map/ppermute | solution.py:23
  831.9 56.9 %collective-permute-start.43 = (bf16[256,2048]{1,0:T(8,128)(2,1)}, bf16[256,2048]{1,0:T(8,128)(2,1)}, u32[]{:S(2)}, u32[]{:S(2)}) collective-permute-start(bf16[256,2048]{1,0:T(8,128)(2,1)} %get-tuple-element.248), channel_id=1, source_target_pairs={{0,1},{4,5},{8,9},{12,13},{16,17},{20,21},{24,25},{28,29}} | collective-permute-start | bytes 3145736 | tf_op jit(solution)/shard_map/ppermute | solution.py:99
  845.8 42.9 %collective-permute-start.44 = (bf16[256,2048]{1,0:T(8,128)(2,1)}, bf16[256,2048]{1,0:T(8,128)(2,1)}, u32[]{:S(2)}, u32[]{:S(2)}) collective-permute-start(bf16[256,2048]{1,0:T(8,128)(2,1)} %get-tuple-element.249), channel_id=1, source_target_pairs={{3,2},{7,6},{11,10},{15,14},{19,18},{23,22},{27,26},{31,30}} | collective-permute-start | bytes 3145736 | tf_op jit(solution)/shard_map/ppermute | solution.py:100
  855.1 55.2 %collective-permute-start.54 = (bf16[256,1536]{1,0:T(8,128)(2,1)}, bf16[256,1536]{1,0:T(8,128)(2,1)}, u32[]{:S(2)}, u32[]{:S(2)}) collective-permute-start(bf16[256,1536]{1,0:T(8,128)(2,1)} %select_convert_fusion), channel_id=1, source_target_pairs={{0,4},{4,0},{8,12},{12,8},{16,20},{20,16},{24,28},{28,24},{1,5},{5... | collective-permute-start | bytes 2359304 | tf_op jit(solution)/shard_map/ppermute | solution.py:23
  893.6 29.3 %collective-permute-start.45 = (bf16[256,2048]{1,0:T(8,128)(2,1)}, bf16[256,2048]{1,0:T(8,128)(2,1)}, u32[]{:S(2)}, u32[]{:S(2)}) collective-permute-start(bf16[256,2048]{1,0:T(8,128)(2,1)} %get-tuple-element.252), channel_id=1, source_target_pairs={{0,1},{1,2},{4,5},{5,6},{8,9},{9,10},{12,13},{13,14},{16,17},{17,1... | collective-permute-start | bytes 3145736 | tf_op jit(solution)/shard_map/ppermute | solution.py:99
  898.9 23.9 %collective-permute-start.46 = (bf16[256,2048]{1,0:T(8,128)(2,1)}, bf16[256,2048]{1,0:T(8,128)(2,1)}, u32[]{:S(2)}, u32[]{:S(2)}) collective-permute-start(bf16[256,2048]{1,0:T(8,128)(2,1)} %get-tuple-element.253), channel_id=1, source_target_pairs={{3,2},{2,1},{7,6},{6,5},{11,10},{10,9},{15,14},{14,13},{19,18},{18... | collective-permute-start | bytes 3145736 | tf_op jit(solution)/shard_map/ppermute | solution.py:100
  903.9 73.8 %collective-permute-start.41 = (bf16[256,2048]{1,0:T(8,128)(2,1)}, bf16[256,2048]{1,0:T(8,128)(2,1)}, u32[]{:S(2)}, u32[]{:S(2)}) collective-permute-start(bf16[256,2048]{1,0:T(8,128)(2,1)} %slice.1150), channel_id=1, source_target_pairs={{0,8},{4,12},{8,0},{12,4},{16,24},{20,28},{24,16},{28,20},{1,9},{5... | collective-permute-start | bytes 3145736 | tf_op jit(solution)/shard_map/ppermute | solution.py:23
  926.3 24.7 %collective-permute-start.47 = (bf16[256,2048]{1,0:T(8,128)(2,1)S(1)}, bf16[256,2048]{1,0:T(8,128)(2,1)S(1)}, u32[]{:S(2)}, u32[]{:S(2)}) collective-permute-start(bf16[256,2048]{1,0:T(8,128)(2,1)S(1)} %get-tuple-element.256), channel_id=1, source_target_pairs={{0,1},{1,2},{2,3},{4,5},{5,6},{6,7},{8,9},{9,10},{10,11},{12,13},{... | collective-permute-start | bytes 3145736 | tf_op jit(solution)/shard_map/ppermute | solution.py:99
  930.9 24.4 %collective-permute-start.48 = (bf16[256,2048]{1,0:T(8,128)(2,1)S(1)}, bf16[256,2048]{1,0:T(8,128)(2,1)S(1)}, u32[]{:S(2)}, u32[]{:S(2)}) collective-permute-start(bf16[256,2048]{1,0:T(8,128)(2,1)S(1)} %get-tuple-element.257), channel_id=1, source_target_pairs={{3,2},{2,1},{1,0},{7,6},{6,5},{5,4},{11,10},{10,9},{9,8},{15,14},{... | collective-permute-start | bytes 3145736 | tf_op jit(solution)/shard_map/ppermute | solution.py:100
  (214 other events, 2804.1 us)
Sparse Core Ops, SparseCore 0:
  27.2 81.0 all-gather.2
  564.1 95.0 all-reduce.5
  679.6 96.8 all-reduce.7
  789.4 116.8 all-reduce.9

commit v2 on v1

--- a/solution.py
+++ b/solution.py
@@ -1,13 +1,14 @@
-from functools import partial
-
 import jax
 import jax.numpy as jnp
 from jax import lax
+from jax.experimental import pallas as pl
+from jax.experimental.pallas import tpu as pltpu
 from jax.sharding import PartitionSpec as P
 
 KD = 256
 VD = 512
-STRETCH = 512
+TILE = 256
+VMEM_LIMIT = 48 * 2**20
 EPSILON = 1e-05
 
 F32 = jnp.float32
@@ -53,8 +54,9 @@
     def __init__(self):
         self.last = ()
 
-    def run(self, *sends, late=(), joined=True):
-        blocks = lax.optimization_barrier(tuple(b for b, _ in sends) + tuple(self.last) + tuple(late))
+    def run(self, *sends, late=(), chain=None, joined=True):
+        first = tuple(self.last if chain is None else chain) + tuple(late)
+        blocks = lax.optimization_barrier(tuple(b for b, _ in sends) + first)
         came = tuple(move(block) for block, (_, move) in zip(blocks, sends))
         came = lax.optimization_barrier(came) if joined and len(came) > 1 else came
         self.last = came
@@ -85,21 +87,55 @@
     return [choose(index ^ i, [blocks[d] for d in range(count)]) for i in range(count)]
 
 
-def group_scatter(block, group_index):
-    groups = lax.axis_size("grp")
-    size = block.shape[0] // groups
-    up = down = None
-    for step in range(1, groups):
-        goes_up = cut(block, jnp.minimum(groups - step + group_index, groups - 1), size, 0)
-        goes_down = cut(block, jnp.maximum(step - groups + group_index, 0), size, 0)
-        if up is not None:
-            goes_up = (goes_up.astype(F32) + up.astype(F32)).astype(BF16)
-            goes_down = (goes_down.astype(F32) + down.astype(F32)).astype(BF16)
-        goes_up, goes_down = lax.optimization_barrier((goes_up.astype(BF16), goes_down.astype(BF16)))
-        up = lax.ppermute(goes_up, "grp", [(p, p + 1) for p in range(step)])
-        down = lax.ppermute(goes_down, "grp", [(groups - 1 - p, groups - 2 - p) for p in range(step)])
-        up, down = lax.optimization_barrier((up, down))
-    return cut(block, group_index, size, 0).astype(F32) + up.astype(F32) + down.astype(F32)
+class GroupLine:
+    def __init__(self, group_index, count):
+        self.groups = lax.axis_size("grp")
+        self.index, self.count = group_index, count
+        self.pieces = {}
+        self.came = {"up": [], "down": []}
+
+    def add(self, *pieces):
+        for piece in lax.optimization_barrier(pieces):
+            self.pieces[len(self.pieces)] = (piece, piece)
+
+    def add_blocks(self, blocks):
+        blocks = lax.optimization_barrier(tuple(blocks))
+        for i in range(self.groups - 1):
+            self.pieces[self.count + i] = (blocks[self.groups - 1 - i], blocks[i])
+
+    def step(self, *late):
+        step, groups = len(self.came["up"]), self.groups
+        sends = []
+        for way, place in (("up", self.index), ("down", groups - 1 - self.index)):
+            side = 0 if way == "up" else 1
+            pairs, options = [], []
+            for p in range(groups - 1):
+                item = step - p
+                ahead = item - self.count
+                live = item in self.pieces and (ahead < 0 or p + 1 <= groups - 1 - ahead)
+                if live:
+                    pairs.append((p, p + 1) if side == 0 else (groups - 1 - p, groups - 2 - p))
+                options.append(self.pieces[item][side] if live else None)
+            known = next(option for option in options if option is not None)
+            sent = choose(place, [known if option is None else option for option in options])
+            if step:
+                sent = (sent.astype(F32) + self.came[way][-1].astype(F32)).astype(BF16)
+            sends.append((sent, pairs))
+        blocks = lax.optimization_barrier(tuple(sent for sent, _ in sends) + late)
+        for way, block, (_, pairs) in zip(("up", "down"), blocks, sends):
+            self.came[way].append(lax.ppermute(block, "grp", pairs))
+
+    def total(self, item):
+        groups = self.groups
+        piece = self.pieces[item][0]
+        zero = jnp.zeros_like(piece)
+        below = choose(self.index, [zero] + self.came["up"][item : item + groups - 1])
+        above = choose(groups - 1 - self.index, [zero] + self.came["down"][item : item + groups - 1])
+        return piece.astype(F32) + below.astype(F32) + above.astype(F32)
+
+    def last(self):
+        step = self.count + self.groups - 2
+        return self.came["up"][step].astype(F32) + self.came["down"][step].astype(F32)
 
 
 def small_sum(block):
@@ -142,19 +178,266 @@
     return rotate(grads, cosine, -sine)
 
 
-def decay_mask(query_pos, key_pos, query_doc, key_doc, log_decay, window):
-    distance = query_pos[:, None] - key_pos[None, :]
-    inside = (distance >= 0) & (query_doc[:, None] == key_doc[None, :]) & (key_pos[None, :] >= 0)
-    inside = inside & (distance < window)
-    steps = jnp.where(inside, distance, 0).astype(F32)
-    return jnp.where(inside, jnp.exp(steps * log_decay), 0.0)
-
-
-def gate_norm(retained, gate_pre, gain, bias):
-    center = retained - jnp.mean(retained, axis=-1, keepdims=True)
-    spread = jnp.mean(center * center, axis=-1, keepdims=True)
-    grouped = center * lax.rsqrt(spread + EPSILON) * gain + bias
-    return jax.nn.silu(gate_pre) * grouped
+def tile_bounds(starts_ref, window, first, rows, axis):
+    shape = (rows, 1) if axis == 0 else (1, rows)
+    position = first + lax.broadcasted_iota(jnp.int32, shape, axis)
+    earliest = jnp.maximum(position - window + 1, 0)
+    for d in range(starts_ref.shape[0]):
+        begin = starts_ref[d]
+        earliest = jnp.where(position >= begin, jnp.maximum(earliest, begin), earliest)
+    return position, earliest
+
+
+def retention_kernel(
+    place_ref,
+    starts_ref,
+    decay_ref,
+    query_ref,
+    key_low_ref,
+    key_high_ref,
+    value_low_ref,
+    value_high_ref,
+    gate_ref,
+    gain_ref,
+    bias_ref,
+    out_ref,
+    hat_ref,
+    scale_ref,
+):
+    half = key_low_ref.shape[0]
+    log_decay = decay_ref[0]
+    for tile in range(query_ref.shape[0] // TILE):
+        begin = tile * TILE
+        first = place_ref[0] + begin
+        rows = slice(begin, begin + TILE)
+        position, earliest = tile_bounds(starts_ref, place_ref[1], first, TILE, 0)
+        row_decay = jnp.exp((position - first).astype(F32) * log_decay)
+        total = jnp.zeros((TILE, VD), F32)
+        for keys, values, low, high, offset in (
+            (key_low_ref, value_low_ref, begin, half, begin - half),
+            (key_high_ref, value_high_ref, 0, begin + TILE, begin * 0),
+        ):
+            count = high - low
+            ahead = (low - begin) - (half if keys is key_low_ref else 0)
+            column = first + ahead + lax.broadcasted_iota(jnp.int32, (1, count), 1)
+            column_decay = jnp.exp((first - column).astype(F32) * log_decay)
+            scores = dot(query_ref[rows, :], keys[low:high, :], ((1,), (1,)))
+            inside = (column <= position) & (column >= earliest)
+            weights = jnp.where(inside, scores * (row_decay * column_decay), 0.0).astype(BF16)
+            total = total + dot(weights, values[low:high, :])
+        center = total - jnp.mean(total, axis=1, keepdims=True)
+        scale = lax.rsqrt(jnp.mean(center * center, axis=1, keepdims=True) + EPSILON)
+        hat = center * scale
+        gate = gate_ref[rows, :].astype(F32)
+        silu = gate / (1.0 + jnp.exp(-gate))
+        out_ref[rows, :] = (silu * (hat * gain_ref[...] + bias_ref[...])).astype(BF16)
+        hat_ref[rows, :] = hat.astype(BF16)
+        scale_ref[rows, :] = jnp.broadcast_to(scale, (TILE, 128))
+
+
+def retention_back_kernel(
+    place_ref,
+    starts_ref,
+    decay_ref,
+    query_ref,
+    key_low_ref,
+    key_high_ref,
+    value_low_ref,
+    value_high_ref,
+    gate_ref,
+    gain_ref,
+    bias_ref,
+    hat_ref,
+    scale_ref,
+    grad_ref,
+    query_grad_ref,
+    gate_grad_ref,
+    low_grad_ref,
+    high_grad_ref,
+    gain_grad_ref,
+    bias_grad_ref,
+):
+    half = key_low_ref.shape[0]
+    log_decay = decay_ref[0]
+    gain, bias = gain_ref[...], bias_ref[...]
+    gain_grad = jnp.zeros((1, VD), F32)
+    bias_grad = jnp.zeros((1, VD), F32)
+    low_grad_ref[...] = jnp.zeros_like(low_grad_ref)
+    high_grad_ref[...] = jnp.zeros_like(high_grad_ref)
+    for tile in range(query_ref.shape[0] // TILE):
+        begin = tile * TILE
+        first = place_ref[0] + begin
+        rows = slice(begin, begin + TILE)
+        hat = hat_ref[rows, :].astype(F32)
+        grad = grad_ref[rows, :].astype(F32)
+        gate = gate_ref[rows, :].astype(F32)
+        sigmoid = 1.0 / (1.0 + jnp.exp(-gate))
+        silu = gate * sigmoid
+        grouped_grad = grad * silu
+        gate_grad = grad * (hat * gain + bias) * (sigmoid + silu * (1.0 - sigmoid))
+        gate_grad_ref[rows, :] = gate_grad.astype(BF16)
+        gain_grad = gain_grad + jnp.sum(grouped_grad * hat, axis=0, keepdims=True)
+        bias_grad = bias_grad + jnp.sum(grouped_grad, axis=0, keepdims=True)
+        inner = grouped_grad * gain
+        mean = jnp.mean(inner, axis=1, keepdims=True)
+        along = jnp.mean(inner * hat, axis=1, keepdims=True)
+        kept_grad = ((inner - mean - hat * along) * scale_ref[rows, :1]).astype(BF16)
+        query = query_ref[rows, :]
+        position, earliest = tile_bounds(starts_ref, place_ref[1], first, TILE, 1)
+        row_decay = jnp.exp((position - first).astype(F32) * log_decay)
+        query_grad = jnp.zeros((TILE, KD), F32)
+        for keys, values, sums, low, high in (
+            (key_low_ref, value_low_ref, low_grad_ref, begin, half),
+            (key_high_ref, value_high_ref, high_grad_ref, 0, begin + TILE),
+        ):
+            count = high - low
+            ahead = (low - begin) - (half if keys is key_low_ref else 0)
+            column = first + ahead + lax.broadcasted_iota(jnp.int32, (count, 1), 0)
+            column_decay = jnp.exp((first - column).astype(F32) * log_decay)
+            inside = (column <= position) & (column >= earliest)
+            mask = jnp.where(inside, row_decay * column_decay, 0.0)
+            key, value = keys[low:high, :], values[low:high, :]
+            weights = (dot(key, query, ((1,), (1,))) * mask).astype(BF16)
+            scores = (dot(value, kept_grad, ((1,), (1,))) * mask).astype(BF16)
+            sums[low:high, KD:] += dot(weights, kept_grad)
+            sums[low:high, :KD] += dot(scores, query)
+            query_grad = query_grad + dot(scores, key, ((0,), (0,)))
+        query_grad_ref[rows, :] = query_grad
+    gain_grad_ref[...] = gain_grad
+    bias_grad_ref[...] = bias_grad
+
+
+def whole_spec(*shape):
+    return pl.BlockSpec(shape, lambda _: (0,) * len(shape))
+
+
+def retention_specs(rows, low, high):
+    def part(width, index):
+        return pl.BlockSpec((rows, width), lambda _: (index, 0))
+
+    smem = pl.BlockSpec(memory_space=pltpu.SMEM)
+    return [smem] * 3 + [
+        part(KD, high[1]),
+        part(KD, low),
+        part(KD, high[0]),
+        part(VD, low),
+        part(VD, high[0]),
+        part(VD, high[1]),
+        whole_spec(1, VD),
+        whole_spec(1, VD),
+    ]
+
+
+def retention(place, starts, decay, queries, keys, values, gate, gain, bias, rows, low, high):
+    cost = pl.CostEstimate(flops=rows * 1280 * 192, bytes_accessed=rows * 1024, transcendentals=0)
+    return pl.pallas_call(
+        retention_kernel,
+        out_shape=(
+            jax.ShapeDtypeStruct((rows, VD), BF16),
+            jax.ShapeDtypeStruct((rows, VD), BF16),
+            jax.ShapeDtypeStruct((rows, 128), F32),
+        ),
+        grid=(1,),
+        in_specs=retention_specs(rows, low, high),
+        out_specs=(whole_spec(rows, VD), whole_spec(rows, VD), whole_spec(rows, 128)),
+        compiler_params=pltpu.CompilerParams(vmem_limit_bytes=VMEM_LIMIT),
+        cost_estimate=cost,
+    )(place, starts, decay, queries, keys[0], keys[1], values[0], values[1], gate, gain, bias)
+
+
+def retention_back(
+    place, starts, decay, queries, keys, values, gate, gain, bias, hat, scale, grad, rows, low, high
+):
+    cost = pl.CostEstimate(flops=rows * 1280 * 448, bytes_accessed=rows * 2048, transcendentals=0)
+    part = pl.BlockSpec((rows, VD), lambda _: (high[1], 0))
+    return pl.pallas_call(
+        retention_back_kernel,
+        out_shape=(
+            jax.ShapeDtypeStruct((rows, KD), F32),
+            jax.ShapeDtypeStruct((rows, VD), BF16),
+            jax.ShapeDtypeStruct((rows, KD + VD), F32),
+            jax.ShapeDtypeStruct((rows, KD + VD), F32),
+            jax.ShapeDtypeStruct((1, VD), F32),
+            jax.ShapeDtypeStruct((1, VD), F32),
+        ),
+        grid=(1,),
+        in_specs=retention_specs(rows, low, high)
+        + [whole_spec(rows, VD), whole_spec(rows, 128), part],
+        out_specs=(
+            whole_spec(rows, KD),
+            whole_spec(rows, VD),
+            whole_spec(rows, KD + VD),
+            whole_spec(rows, KD + VD),
+            whole_spec(1, VD),
+            whole_spec(1, VD),
+        ),
+        compiler_params=pltpu.CompilerParams(vmem_limit_bytes=VMEM_LIMIT),
+        cost_estimate=cost,
+    )(place, starts, decay, queries, keys[0], keys[1], values[0], values[1], gate, gain, bias, hat, scale, grad)
+
+
+def feed_kernel(
+    normed_ref,
+    cotangent_ref,
+    up_ref,
+    down_ref,
+    bias_ref,
+    activated_ref,
+    grad_pre_ref,
+    mixed_ref,
+    grad_ref,
+    bias_grad_ref,
+):
+    up, down = up_ref[...], down_ref[...]
+    pre = dot(normed_ref[...], up) + bias_ref[...]
+    grad_act = dot(cotangent_ref[...], down, ((1,), (1,)))
+    share = 0.5 + 0.5 * lax.erf(pre * 0.7071067811865476)
+    bell = jnp.exp(-0.5 * pre * pre) * 0.3989422804014327
+    activated = (pre * share).astype(BF16)
+    grad_pre = (grad_act * (share + pre * bell)).astype(BF16)
+    activated_ref[...] = activated
+    grad_pre_ref[...] = grad_pre
+    mixed_ref[...] = dot(activated, down).astype(BF16)
+    grad_ref[...] = dot(grad_pre, up, ((1,), (1,))).astype(BF16)
+
+    @pl.when(pl.program_id(0) == 0)
+    def _():
+        bias_grad_ref[...] = jnp.zeros_like(bias_grad_ref)
+
+    bias_grad_ref[...] += jnp.sum(grad_pre.astype(F32), axis=0, keepdims=True)
+
+
+def feed(normed, cotangent, up, down, bias):
+    rows, width = normed.shape
+    hidden = up.shape[1]
+
+    def tiled(columns):
+        return pl.BlockSpec((TILE, columns), lambda i: (i, 0))
+
+    cost = pl.CostEstimate(
+        flops=rows * width * hidden, bytes_accessed=rows * width, transcendentals=0
+    )
+    return pl.pallas_call(
+        feed_kernel,
+        out_shape=(
+            jax.ShapeDtypeStruct((rows, hidden), BF16),
+            jax.ShapeDtypeStruct((rows, hidden), BF16),
+            jax.ShapeDtypeStruct((rows, width), BF16),
+            jax.ShapeDtypeStruct((rows, width), BF16),
+            jax.ShapeDtypeStruct((1, hidden), F32),
+        ),
+        grid=(rows // TILE,),
+        in_specs=[
+            tiled(width),
+            tiled(width),
+            whole_spec(*up.shape),
+            whole_spec(*down.shape),
+            whole_spec(1, hidden),
+        ],
+        out_specs=(tiled(hidden), tiled(hidden), tiled(width), tiled(width), whole_spec(1, hidden)),
+        compiler_params=pltpu.CompilerParams(vmem_limit_bytes=VMEM_LIMIT),
+        cost_estimate=cost,
+    )(normed, cotangent, up, down, bias)
 def body(
     tokens,
     first_gain,
@@ -210,7 +493,7 @@
     small = [first_gain, first_bias, second_gain, second_bias, down_bias, up_bias]
     small += [group_gain.T.reshape(-1), group_bias.T.reshape(-1)]
     sizes = [item.shape[0] for item in small]
-    packed = lax.all_gather(after(jnp.concatenate(small)[None], theirs), "seq", axis=0, tiled=True).astype(F32)
+    packed = lax.all_gather(after(jnp.concatenate(small)[None], low_rows, high_rows), "seq", axis=0, tiled=True).astype(F32)
     whole, start = [], 0
     for size in sizes:
         whole.append(packed[:, start : start + size])
@@ -227,6 +510,11 @@
     normed = layer_norm(inputs, gain_one, bias_one).astype(BF16)
     gathered = lax.all_gather(normed, "grp", axis=0, tiled=True)
 
+    base = chip * pair_rows
+    positions = base + jnp.arange(pair_rows, dtype=jnp.int32)
+    places = document_table(doc_lengths, positions)[1]
+    doc_starts = jnp.cumsum(doc_lengths, dtype=jnp.int32) - doc_lengths
+    cosine, sine = rotary_table(places, KD)
     def join_chips(low, high):
         held = {0: jnp.stack([low, high])}
         for bit in range(1, devices.bit_length() - 1):
@@ -254,7 +542,7 @@
         }
         two_x, down_y = stages.run((jnp.stack([up_sent, cotangent]), by_x), (down_weight, by_y))
         up_x, cotangent_x = two_x[0], two_x[1]
-        gathered = after(gathered, two_x)
+        gathered = after(gathered, high_xy, low_xy, cosine, sine)
     else:
         head_held = join_chips(low_rows, high_rows)
         up_x = by_x(up_sent)
@@ -274,61 +562,48 @@
         [jnp.where(core == 0, gathered, beside), jnp.where(core == 0, beside, gathered)], axis=0
     )
 
-    base = chip * pair_rows
-    positions = base + jnp.arange(pair_rows, dtype=jnp.int32)
-    documents, places = document_table(doc_lengths, positions)
-    key_positions = base - rows + jnp.arange(3 * rows, dtype=jnp.int32)
-    key_documents = document_table(doc_lengths, key_positions)[0]
-    cosine, sine = rotary_table(places, KD)
     key_scale = KD ** (-0.5)
     key_pre = dot(pair_normed, head_weight[:, KD : 2 * KD])
     keys = (rotate(key_pre, cosine, sine) * key_scale).astype(BF16)
     values = dot(pair_normed, head_weight[:, 2 * KD : 2 * KD + VD]).astype(BF16)
     halo = jnp.concatenate([keys[rows:], values[rows:]], axis=1)
     if small_mesh:
-        (halo,) = stages.run((halo, lambda v: hop(v, 2)))
+        weights_last = stages.last
+        (halo,) = stages.run((halo, lambda v: hop(v, 2)), chain=(high_xy, low_xy))
     else:
         halo = hop(halo, 2)
     query_pre = dot(pair_normed, head_weight[:, :KD])
-    gate_pre = dot(pair_normed, head_weight[:, 2 * KD + VD :])
+    gate_pre = dot(pair_normed, head_weight[:, 2 * KD + VD :]).astype(BF16)
     queries = rotate(query_pre, cosine, sine).astype(BF16)
-    prior_keys, prior_values = halo[:, :KD], halo[:, KD:]
-
-    def key_span(start):
-        own = keys[max(start - rows, 0) : start + STRETCH]
-        return own if start >= rows else jnp.concatenate([prior_keys[start:], own], axis=0)
-
-    def value_span(start):
-        own = values[max(start - rows, 0) : start + STRETCH]
-        return own if start >= rows else jnp.concatenate([prior_values[start:], own], axis=0)
-
+    halo = (halo[:, :KD], halo[:, KD:])
     head_index = (group_index * 2 + core).astype(F32)
-    log_decay = jnp.log1p(-jnp.exp2(-5.0 - head_index))
+    log_decay = jnp.log1p(-jnp.exp2(-5.0 - head_index)).reshape(1)
     window = windows[0]
-    span = rows + STRETCH
-
-    def block_mask(start):
-        return decay_mask(
-            positions[start : start + STRETCH],
-            key_positions[start : start + span],
-            documents[start : start + STRETCH],
-            key_documents[start : start + span],
-            log_decay,
-            window,
-        )
-
-    pieces = {}
-    for start in reversed(range(0, pair_rows, STRETCH)):
-        scores = dot(queries[start : start + STRETCH], key_span(start), ((1,), (1,)))
-        weights = (scores * block_mask(start)).astype(BF16)
-        pieces[start] = dot(weights, value_span(start))
-    retained = jnp.concatenate([pieces[start] for start in sorted(pieces)], axis=0)
-    heads_out = gate_norm(retained, gate_pre, group_gain_f, group_bias_f).astype(BF16)
+
+    shared = (doc_starts, log_decay, queries)
+    late_rows, early_rows = (0, (1, 1)), (0, (0, 0))
+    late_place = jnp.stack([base + rows, window])
+    early_place = jnp.stack([base, window])
+    late_keys, late_values = (keys, keys), (values, values)
+    early_keys, early_values = (halo[0], keys), (halo[1], values)
+    gated = (gate_pre, group_gain_f, group_bias_f)
+    late_out, late_hat, late_scale = retention(
+        late_place, *shared, late_keys, late_values, *gated, rows, *late_rows
+    )
+    early_out, early_hat, early_scale = retention(
+        early_place, *shared, early_keys, early_values, *gated, rows, *early_rows
+    )
 
     if small_mesh:
-        out_low_x, out_high_y = stages.run((out_low, by_x), (out_high, by_y), late=(pieces[rows],))
-        out_high_xy, out_low_xy = stages.run(
-            (jnp.stack([out_high, out_high_y]), by_x), (jnp.stack([out_low, out_low_x]), by_y)
+        out_low_x, out_high_y = stages.run(
+            (out_low, by_x), (out_high, by_y), chain=weights_last, late=(gate_pre,)
+        )
+        out_high_xy, out_low_xy, up_y = stages.run(
+            (jnp.stack([out_high, out_high_y]), by_x),
+            (jnp.stack([out_low, out_low_x]), by_y),
+            (up_four, by_y),
+            chain=(),
+            joined=False,
         )
         out_held = {
             0: (out_low, out_high),
@@ -345,7 +620,7 @@
         out_head = pick(out_head.reshape(groups, 2, VD, width), core, 1).reshape(groups * VD, width)
     up_held, down_held = {0: up_four}, {0: down_weight}
     if small_mesh:
-        (up_held[1],) = stages.run((up_four, by_y))
+        up_held[1] = up_y
         down_held[1] = down_y
     else:
         for bit in range(2, devices.bit_length() - 1):
@@ -361,33 +636,22 @@
     def with_core(two):
         return jnp.concatenate([two, by_core(two)], axis=0)
 
-    def quad_rows(block):
-        return with_core(jnp.concatenate([block, by_x(block)], axis=0))
-
-    def quad_sum(block):
-        two = block[: 2 * own_rows] + by_core(block[2 * own_rows :].astype(BF16)).astype(F32)
-        return two[:own_rows] + by_x(two[own_rows:].astype(BF16)).astype(F32)
-
-    if small_mesh:
-        quad_cotangent = with_core(jnp.concatenate([cotangent, cotangent_x], axis=0))
-    else:
-        quad_cotangent = quad_rows(cotangent)
-
-    def to_tokens(block):
-        parted = block.reshape(2, groups, own_rows, VD)
-        result = jnp.zeros((2 * own_rows, groups * VD), BF16)
-        for by in range(groups):
-            sent = pick(parted, (group_index + by) % groups, 1).reshape(2 * own_rows, VD)
-            result = put(result, turn(sent, by) if by else sent, (group_index - by) % groups, 1)
-        return result
+    if not small_mesh:
+        cotangent_x = by_x(cotangent)
+    near_cotangent, far_cotangent = with_core(cotangent), with_core(cotangent_x)
+
+    def exchange(blocks):
+        return lax.all_to_all(blocks, "grp", split_axis=0, concat_axis=0, tiled=True)
+
+    def to_tokens(early, late):
+        parted = [item.reshape(groups, own_rows, VD) for item in (early, late)]
+        came = exchange(jnp.concatenate(parted, axis=1))
+        return jnp.concatenate(list(came), axis=1)
 
     def to_heads(block):
-        result = jnp.zeros((2, groups, own_rows, VD), BF16)
-        for by in range(groups):
-            sent = cut(block, (group_index + by) % groups, VD, 1)
-            came = turn(sent, by) if by else sent
-            result = put(result, came.reshape(2, 1, own_rows, VD), (group_index - by) % groups, 1)
-        return result.reshape(pair_rows, VD)
+        sent = jnp.stack([block[:, i * VD : (i + 1) * VD] for i in range(groups)])
+        came = exchange(sent).reshape(groups, 2, own_rows, VD)
+        return jnp.concatenate([came[:, 0].reshape(rows, VD), came[:, 1].reshape(rows, VD)])
 
     def pair_sum(block, size, kind):
         mine = cut(block, core, size, 0)
@@ -399,29 +663,33 @@
             [jnp.where(core == 0, block, beside), jnp.where(core == 0, beside, block)], axis=0
         )
 
-    by_token = to_tokens(heads_out)
+    by_token = to_tokens(early_out, late_out)
     hidden = inputs + pair_sum(dot(by_token, out_head), own_rows, F32)
     normed_two = layer_norm(hidden, gain_two, bias_two).astype(BF16)
-    quad_normed = quad_rows(normed_two)
-    pre_act = dot(quad_normed, up_quarter) + up_bias_quarter
-    activated = jax.nn.gelu(pre_act, approximate=False).astype(BF16)
-
+    normed_x = by_x(normed_two)
+    near_normed, far_normed = with_core(normed_two), with_core(normed_x)
+    weights = (up_quarter, down_quarter, up_bias_quarter)
+    near_activated, near_grad_pre, near_mixed, near_grad, near_bias = feed(near_normed, near_cotangent, *weights)
+    far_activated, far_grad_pre, far_mixed, far_grad, far_bias = feed(far_normed, far_cotangent, *weights)
+    up_bias_part = near_bias + far_bias
     grad_out = cotangent.astype(F32)
     down_bias_part = jnp.sum(grad_out, axis=0)
-    grad_act = dot(quad_cotangent, down_quarter, ((1,), (1,)))
-    gelu_back = jax.vjp(partial(jax.nn.gelu, approximate=False), pre_act)[1]
-    grad_pre = gelu_back(grad_act)[0].astype(BF16)
-    up_bias_part = jnp.sum(grad_pre.astype(F32), axis=0)
+
+    def plus(mine, came):
+        return mine.astype(F32) + came.astype(F32)
+
+    def pair_part(block):
+        return plus(block[:own_rows], by_core(block[own_rows:]))
+
+    far_grad = pair_part(far_grad).astype(BF16)
+    activated = jnp.concatenate([near_activated, far_activated])
+    quad_cotangent = jnp.concatenate([near_cotangent, far_cotangent])
     down_part = dot(activated, quad_cotangent, ((0,), (0,))).astype(BF16).reshape(quads, ff_part, width)
-    two_part = dot(grad_pre, up_quarter, ((1,), (1,)))
     if small_mesh:
-        two = two_part[: 2 * own_rows] + by_core(two_part[2 * own_rows :].astype(BF16)).astype(F32)
-        two_x, down_y = stages.run(
-            (two[own_rows:].astype(BF16), by_x), (pick(down_part, 1 - quad), by_y), joined=False
-        )
-        grad_normed_two = two[:own_rows] + two_x.astype(F32)
+        grad_x, down_y = stages.run((far_grad, by_x), (pick(down_part, 1 - quad), by_y), chain=(), joined=False)
     else:
-        grad_normed_two = quad_sum(two_part)
+        grad_x = by_x(far_grad)
+    grad_normed_two = plus(pair_part(near_grad), grad_x)
     second_back = jax.vjp(layer_norm, hidden, gain_two, bias_two)[1]
     hidden_part, gain_two_part, bias_two_part = second_back(grad_normed_two)
     grad_hidden = grad_out + hidden_part
@@ -429,7 +697,9 @@
     grad_by_token = dot(grad_attend, out_head, ((1,), (1,))).astype(BF16)
     grad_heads = to_heads(grad_by_token)
 
-    up_part = dot(quad_normed, grad_pre, ((0,), (0,))).astype(BF16).reshape(quads, 4, part, ff_quarter)
+    quad_normed = jnp.concatenate([near_normed, far_normed])
+    quad_grad_pre = jnp.concatenate([near_grad_pre, far_grad_pre])
+    up_part = dot(quad_normed, quad_grad_pre, ((0,), (0,))).astype(BF16).reshape(quads, 4, part, ff_quarter)
     out_part = dot(by_token, grad_attend, ((0,), (0,))).astype(BF16)
 
     def split_chips(parts):
@@ -452,9 +722,6 @@
             bit *= 2
         return held[0]
 
-    def plus(mine, came):
-        return mine.astype(F32) + came.astype(F32)
-
     def up_to_owners(up_four, up_x):
         up_core = by_core(jnp.stack([pick(up_four, quarter ^ 1), up_x[1]]))
         up_blocks = by_difference([pick(up_four, quarter), up_core[0], up_x[0], up_core[1]], quarter)
@@ -465,93 +732,123 @@
     def up_x_sent(up_four):
         return jnp.stack([pick(up_four, quarter ^ 2), pick(up_four, quarter ^ 3)])
 
-    mixed_part = dot(activated, down_quarter)
+    mixed_sent = pair_part(far_mixed).astype(BF16)
     if small_mesh:
-        mixed_two = plus(mixed_part[: 2 * own_rows], by_core(mixed_part[2 * own_rows :].astype(BF16)))
         down_sum = plus(pick(down_part, quad), down_y).astype(BF16)
         out_part = out_part.reshape(chips, 2, half_low, width)
         low, high = ([pick(out_part[:, i], chip ^ d) for d in range(chips)] for i in (0, 1))
-        high_x, up_y = stages.run(
-            (jnp.stack([high[1], high[3]]), by_x), (pick(up_part, 1 - quad), by_y), late=(grad_by_token,)
-        )
-        up_four = plus(pick(up_part, quad), up_y).astype(BF16)
-        up_x, low_y = stages.run(
-            (up_x_sent(up_four), by_x), (jnp.stack([low[2], low[3]]), by_y), late=(grad_heads,)
-        )
+        high_x, low_y = stages.run(
+            (jnp.stack([high[1], high[3]]), by_x),
+            (jnp.stack([low[2], low[3]]), by_y),
+            chain=(grad_by_token,),
+        )
+        low_x, high_y = stages.run(
+            (plus(low[1], low_y[1]).astype(BF16), by_x),
+            (plus(high[2], high_x[1]).astype(BF16), by_y),
+            late=(grad_heads,),
+        )
+        low_sum = plus(plus(low[0], low_y[0]), low_x).astype(BF16)
+        high_sum = plus(plus(high[0], high_x[0]), high_y).astype(BF16)
     else:
-        mixed_sum = quad_sum(mixed_part)
+        mixed_x = by_x(mixed_sent)
         down_sum = split_quads(down_part).astype(BF16)
         up_four = split_quads(up_part).astype(BF16)
-        up_x = by_x(up_x_sent(up_four))
         spread = jnp.zeros((groups, 2, VD, width), BF16)
         spread = put(spread, out_part.reshape(groups, 1, VD, width), core, 1)
         out_sum = lax.psum_scatter(
             spread.reshape(groups * 2 * VD, width), "seq", scatter_dimension=0, tiled=True
         )
-    up_sum = up_to_owners(up_four, up_x)
-    down_sum = lax.psum(after(down_sum, grad_heads), "grp")
-    gate_back = jax.vjp(gate_norm, retained, gate_pre, group_gain_f, group_bias_f)[1]
-    grad_retained, grad_gate, group_gain_part, group_bias_part = gate_back(grad_heads.astype(F32))
-    grad_retained = grad_retained.astype(BF16)
-    grad_gate = grad_gate.astype(BF16)
-    key_sums = jnp.zeros((3 * rows, KD), F32)
-    value_sums = jnp.zeros((3 * rows, VD), F32)
-    query_parts = []
-    for start in range(0, pair_rows, STRETCH):
-        mask = block_mask(start)
-        block_queries = queries[start : start + STRETCH]
-        block_keys, block_values = key_span(start), value_span(start)
-        block_grad = grad_retained[start : start + STRETCH]
-        weights = (dot(block_queries, block_keys, ((1,), (1,))) * mask).astype(BF16)
-        grad_scores = (dot(block_grad, block_values, ((1,), (1,))) * mask).astype(BF16)
-        value_sums = value_sums.at[start : start + span].add(dot(weights, block_grad, ((0,), (0,))))
-        key_sums = key_sums.at[start : start + span].add(dot(grad_scores, block_queries, ((0,), (0,))))
-        query_parts.append(dot(grad_scores, block_keys))
-    grad_queries = jnp.concatenate(query_parts, axis=0)
-    later = jnp.concatenate([key_sums[:rows], value_sums[:rows]], axis=1).astype(BF16)
+        low_sum, high_sum = jnp.split(out_sum, 2)
+    half = down_sum.shape[0] // 2
+    line = GroupLine(group_index, 6)
+    line.add(down_sum[:half], down_sum[half:])
+    line.add(low_sum, high_sum)
+
+    early_query, early_gate, later, early_own, early_gain, early_bias = retention_back(
+        early_place, *shared, early_keys, early_values, *gated, early_hat, early_scale, grad_heads, rows, *early_rows
+    )
+    late_query, late_gate, late_own, late_end, late_gain, late_bias = retention_back(
+        late_place, *shared, late_keys, late_values, *gated, late_hat, late_scale, grad_heads, rows, *late_rows
+    )
+    line.step(grad_heads)
+    line.step(late_gate)
+    group_gain_part, group_bias_part = early_gain + late_gain, early_bias + late_bias
+    later = later.astype(BF16)
     if small_mesh:
-        (later,) = stages.run((later, lambda v: hop(v, -2)))
-        low_x, high_y = stages.run(
-            (plus(low[1], low_y[1]).astype(BF16), by_x), (plus(high[2], high_x[1]).astype(BF16), by_y)
-        )
-        low_sum = plus(plus(low[0], low_y[0]), low_x)
-        high_sum = plus(plus(high[0], high_x[0]), high_y)
-        out_sum = jnp.concatenate([low_sum, high_sum], axis=0)
+        out_last = stages.last
+        (later,) = stages.run((later, lambda v: hop(v, -2)), chain=(high_x, low_y))
+        mixed_x, up_y = stages.run(
+            (mixed_sent, by_x), (pick(up_part, 1 - quad), by_y), chain=out_last, late=(late_gate,)
+        )
+        up_four = plus(pick(up_part, quad), up_y).astype(BF16)
     else:
         later = hop(later, -2)
-    up_sum = lax.psum(after(up_sum, down_sum), "grp")
-    out_sum = lax.psum(after(out_sum.astype(BF16), up_sum), "grp")
-    down_grad, up_grad, out_grad = down_sum.astype(F32), up_sum.astype(F32), out_sum.astype(F32)
-
-    own_keys = key_sums[rows:].at[rows:].add(later[:, :KD].astype(F32))
-    grad_values = value_sums[rows:].at[rows:].add(later[:, KD:].astype(F32)).astype(BF16)
-    grad_query = rotate_back(grad_queries, cosine, sine).astype(BF16)
-    grad_key = (rotate_back(own_keys, cosine, sine) * key_scale).astype(BF16)
-    grads = jnp.concatenate([grad_query, grad_key, grad_values, grad_gate], axis=1)
-
-    normed_part = pair_sum(dot(grads, head_weight, ((1,), (1,))), rows, BF16)
-    grad_normed = group_scatter(normed_part, group_index)
-    head_part = dot(pair_normed, grads, ((0,), (0,)))
-    product_part = jnp.sum(head_part * head_weight.astype(F32), axis=1)
+    chunk_shape = low_sum.shape
+    line.add(*(item.reshape(chunk_shape) for item in jnp.split(up_four.reshape(-1), 2)))
+
+    def projection_grads(query, own, gate, begin):
+        near = slice(begin, begin + rows)
+        turned = (cosine[near], sine[near])
+        return jnp.concatenate(
+            [
+                rotate_back(query, *turned).astype(BF16),
+                (rotate_back(own[:, :KD], *turned) * key_scale).astype(BF16),
+                own[:, KD:].astype(BF16),
+                gate,
+            ],
+            axis=1,
+        )
+
+    early_grads = projection_grads(early_query, early_own + late_own, early_gate, 0)
+    line.step(early_grads)
+    late_grads = projection_grads(late_query, late_end + later.astype(F32), late_gate, rows)
+    line.step(late_grads)
+    grads = jnp.concatenate([early_grads, late_grads])
+
+    theirs_part = dot(cut(grads, 1 - core, rows, 0), head_weight, ((1,), (1,))).astype(BF16)
+    normed_part = dot(cut(grads, core, rows, 0), head_weight, ((1,), (1,))) + by_core(theirs_part).astype(F32)
+    blocks = normed_part.astype(BF16).reshape(groups, own_rows, width)
+    own_block = pick(normed_part.reshape(groups, own_rows, width), group_index)
+    if small_mesh:
+        line.add_blocks(blocks)
+        for _ in range(5):
+            line.step()
+        from_groups = line.last()
+    else:
+        for _ in range(4):
+            line.step()
+        block_line = GroupLine(group_index, 0)
+        block_line.add_blocks(blocks)
+        for _ in range(groups - 1):
+            block_line.step()
+        from_groups = block_line.last()
+    grad_normed = own_block + from_groups
+    down_grad = jnp.concatenate([line.total(0), line.total(1)])
+    out_grad = jnp.concatenate([line.total(2), line.total(3)])
+    up_four = jnp.concatenate([line.total(4).reshape(-1), line.total(5).reshape(-1)]).astype(BF16)
+    up_four = up_four.reshape(4, part, ff_quarter)
+    head_part = dot(pair_normed, grads, ((0,), (0,))).astype(BF16)
+    product_part = jnp.sum(head_part.astype(F32) * head_weight.astype(F32), axis=1)
     bias_one_part = jnp.sum(head_weight.astype(F32) * jnp.sum(grads.astype(F32), axis=0)[None], axis=1)
     gain_one_part = (product_part - bias_one * bias_one_part) / gain_one
-    head_part = head_part.astype(BF16).reshape(chips, 2, part, columns)
+    head_part = head_part.reshape(chips, 2, part, columns)
     parts = {d: pick(head_part, chip ^ d) for d in range(chips)}
     if small_mesh:
         high_x, low_y = stages.run(
-            (jnp.stack([parts[1][1], parts[3][1]]), by_x), (jnp.stack([parts[2][0], parts[3][0]]), by_y)
+            (jnp.stack([parts[1][1], parts[3][1]]), by_x),
+            (jnp.stack([parts[2][0], parts[3][0]]), by_y),
+            late=(normed_part,),
         )
         low_x, high_y = stages.run(
             (plus(parts[1][0], low_y[1]).astype(BF16), by_x),
             (plus(parts[2][1], high_x[1]).astype(BF16), by_y),
         )
-        (mixed_x,) = stages.run((mixed_two[own_rows:].astype(BF16), by_x))
-        mixed_sum = plus(mixed_two[:own_rows], mixed_x)
         low_sum = plus(plus(parts[0][0], low_y[0]), low_x)
         high_sum = plus(plus(parts[0][1], high_x[0]), high_y)
     else:
         low_sum, high_sum = split_chips(parts)
-    mixed = (hidden + mixed_sum + down_bias_full).astype(BF16)
+    up_grad = up_to_owners(up_four, by_x(up_x_sent(up_four))).astype(F32)
+    mixed = (hidden + plus(pair_part(near_mixed), mixed_x) + down_bias_full).astype(BF16)
     own_head = jnp.where(core == 0, low_sum, high_sum)
     other_head = by_core(jnp.where(core == 0, high_sum, low_sum).astype(BF16)).astype(F32)
     first_head = jnp.where(core == 0, own_head, other_head)

time: 999 us -> 899 us (0.90)
  waiting for transfers between devices: 416 us -> 295 us
  matrix products: 163 us -> 98.5 us
  Pallas kernels: 0 us -> 64 us
  starting transfers between devices: 85 us -> 126 us
  local copies, waits for them, and re-layouts: 128 us -> 108 us
    dot_general x39 -> x12, matrix products: 163 us -> 98.5 us  [dot(): return lax.dot_general(a, b, (dims, ((), ())), preferred_element_type=F32)]
    ppermute x12 -> x18, waiting for transfers between devices: 112 us -> 47.6 us  [step(): self.came[way].append(lax.ppermute(block, 'grp', pairs))]
    pallas_call x0 -> x6, Pallas kernels: none -> 64 us  [the longest x2 28.7 us: feed(): pl.pallas_call(feed_kernel, out_shape=(jax.ShapeDtypeStruct((rows, hidden...]
    ppermute x2, waiting for transfers between devices: 53.3 us -> 1.09 us  [hop(): lax.ppermute(block, 'seq', [(i, i + by) for i in range(devices) if 0 <= i...]
    ppermute x37 -> x41, starting transfers between devices: 27.8 us -> 65.6 us  [flip(): return lax.ppermute(block, 'seq', [(i, i ^ bit) for i in range(devices)])]
    ppermute x37 -> x41, waiting for transfers between devices: 238 us -> 207 us  [flip(): return lax.ppermute(block, 'seq', [(i, i ^ bit) for i in range(devices)])]
    unnamed x430 -> x334, local copies, waits for them, and re-layouts: 54.8 us -> 31 us
    all_gather x1, waiting for transfers between devices: 0.01 us -> 16.8 us  [body(): gathered = lax.all_gather(normed, 'grp', axis=0, tiled=True)]
  transfers between devices with their start and end apart: 60 -> 69, of which waited for: 32 -> 36; matrix products, arithmetic and copies ran while one was open for 34% -> 34% of each run, Pallas kernels for 0% -> 7%
where the time goes in v2:
time: 899 us; the launch traced here: 892 us
  waiting for transfers between devices  295 us (33%)
  other arithmetic  172 us (19%)
  starting transfers between devices  126 us (14%)
  local copies, waits for them, and re-layouts  108 us (12%)
  matrix products  98.5 us (11%)
  Pallas kernels  64 us (7%)
  between operations  17.6 us (2%)
  blocking collectives  10.3 us (1%)
    ppermute x41, waiting for transfers between devices, flip(): return lax.ppermute(block, 'seq', [(i, i ^ bit) for i in range(devices)])  207 us
    dot_general x12, matrix products, dot(): return lax.dot_general(a, b, (dims, ((), ())), preferred_element_type=F32)  98.5 us
    ppermute x41, starting transfers between devices, flip(): return lax.ppermute(block, 'seq', [(i, i ^ bit) for i in range(devices)])  65.6 us
    ppermute x18, waiting for transfers between devices, step(): self.came[way].append(lax.ppermute(block, 'grp', pairs))  47.6 us
    ppermute x18, starting transfers between devices, step(): self.came[way].append(lax.ppermute(block, 'grp', pairs))  41.3 us
    unnamed x334, local copies, waits for them, and re-layouts  31 us
    pallas_call x2, Pallas kernels, feed(): pl.pallas_call(feed_kernel, out_shape=(jax.ShapeDtypeStruct((rows, hidden...  28.7 us
    pallas_call x2, Pallas kernels, retention_back(): pl.pallas_call(retention_back_kernel, out_shape=(jax.ShapeDtypeStruct((ro...  24.1 us
  transfers between devices with their start and end apart: 69, of which 36 were waited for; matrix products, arithmetic and copies ran while one was open for 34% of the time, Pallas kernels for 7%

profile of v2, /device:TPU:0, one launch (start us, length us, event | category | flops | bytes accessed | tf_op | source)
XLA Modules:
  0.0 891.6 jit_solution(15300787790355220265)
XLA Ops:
  16.1 10.3 %all-gather = bf16[8,1,2048]{2,1,0:T(2,128)(2,1)S(1)} all-gather(bf16[1,1,2048]{2,1,0:T(2,128)(2,1)S(1)} %bitcast.302), channel_id=1, replica_groups=mesh['seq'=8,'grp'=4] {'seq'}, dimensions={0}, use_global_device_ids=true | all-gather | bytes 36864 | tf_op jit(solution)/shard_map/all_gather | solution.py:496
  30.0 17.7 %collective-permute-done.1 = bf16[256,1536]{1,0:T(8,128)(2,1)S(1)} collective-permute-done((bf16[256,1536]{1,0:T(8,128)(2,1)S(1)}, bf16[256,1536]{1,0:T(8,128)(2,1)S(1)}, u32[]{:S(2)}, u32[]{:S(2)}) %collective-permute-start.1) | collective-permute-done | bytes 786464 | tf_op jit(solution)/shard_map/ppermute | solution.py:24
  58.4 5.7 multiply_sine_fusion
  64.1 23.3 %collective-permute-done.3 = bf16[2,256,1536]{2,1,0:T(8,128)(2,1)} collective-permute-done((bf16[2,256,1536]{2,1,0:T(8,128)(2,1)}, bf16[2,256,1536]{2,1,0:T(8,128)(2,1)}, u32[]{:S(2)}, u32[]{:S(2)}) %collective-permute-start.3) | collective-permute-done | bytes 1572896 | tf_op jit(solution)/shard_map/ppermute | solution.py:24
  92.3 16.8 %all-gather.3.cloned.1.call-done = bf16[1024,2048]{1,0:T(8,128)(2,1)} async-done(((bf16[256,2048]{1,0:T(8,128)(2,1)}), bf16[1024,2048]{1,0:T(8,128)(2,1)}) %all-gather.3.cloned.1.call-update) | async-done | bytes 4194320 | tf_op jit(solution)/shard_map/all_gather | solution.py:511
  115.1 18.9 %collective-permute-done.7 = bf16[2,256,2048]{2,1,0:T(8,128)(2,1)} collective-permute-done((bf16[2,256,2048]{2,1,0:T(8,128)(2,1)}, bf16[2,256,2048]{2,1,0:T(8,128)(2,1)}, u32[]{:S(2)}, u32[]{:S(2)}) %collective-permute-start.7) | collective-permute-done | bytes 2097184 | tf_op jit(solution)/shard_map/ppermute | solution.py:24
  146.0 7.6 convolution_convert_fusion.4.gate_ref
  153.6 7.0 convolution_convert_fusion.5.value_high_ref.value_low_ref
  167.6 5.6 fusion.84
  182.6 8.9 collective-permute-done.9
  196.9 5.6 shard_map.315
  203.5 33.7 %collective-permute-start.13 = (bf16[2,256,2048]{2,1,0:T(8,128)(2,1)}, bf16[2,256,2048]{2,1,0:T(8,128)(2,1)}, u32[]{:S(2)}, u32[]{:S(2)}) collective-permute-start(bf16[2,256,2048]{2,1,0:T(8,128)(2,1)} %pad_maximum_fusion.6), channel_id=1, source_target_pairs={{0,16},{4,20},{8,24},{12,28},{16,0},{20,4},{24,8},{28,12},{1,17},{... | collective-permute-start | bytes 6291464 | tf_op jit(solution)/shard_map/ppermute | solution.py:24
  240.6 5.6 shard_map.314
  248.7 5.2 all-to-all-start
  253.9 4.3 broadcast_in_dim.77
  259.7 10.3 %collective-permute-done.12 = bf16[2,256,2048]{2,1,0:T(8,128)(2,1)} collective-permute-done((bf16[2,256,2048]{2,1,0:T(8,128)(2,1)}, bf16[2,256,2048]{2,1,0:T(8,128)(2,1)}, u32[]{:S(2)}, u32[]{:S(2)}) %collective-permute-start.12) | collective-permute-done | bytes 2097184 | tf_op jit(solution)/shard_map/ppermute | solution.py:24
  278.0 10.2 %all-to-all-done = bf16[4,512,512]{2,1,0:T(8,128)(2,1)} async-done(((bf16[4,512,512]{2,1,0:T(8,128)(2,1)}), bf16[4,512,512]{2,1,0:T(8,128)(2,1)}, u32[]{:S(2)}, u32[]{:S(2)}) %all-to-all-start) | async-done | bytes 2097184 | tf_op jit(solution)/shard_map/all_to_all | solution.py:644
  289.8 7.8 fusion.97
  300.9 5.4 collective-permute-done.16
  323.2 35.4 %collective-permute-done.17 = bf16[4,256,1024]{2,1,0:T(8,128)(2,1)S(1)} collective-permute-done((bf16[4,256,1024]{2,1,0:T(8,128)(2,1)S(1)}, bf16[4,256,1024]{2,1,0:T(8,128)(2,1)S(1)}, u32[]{:S(2)}, u32[]{:S(2)}) %collective-permute-start.17) | collective-permute-done | bytes 2097184 | tf_op jit(solution)/shard_map/ppermute | solution.py:24
  363.7 14.3 %shard_map.316 = (bf16[512,1024]{1,0:T(8,128)(2,1)S(1)}, bf16[512,1024]{1,0:T(8,128)(2,1)S(1)}, bf16[512,2048]{1,0:T(8,128)(2,1)S(1)}, bf16[512,2048]{1,0:T(8,128)(2,1)}, f32[1,1024]{1,0:T(1,128)S(1)}) custom-call(bf16[512,2048]{1,0:T(8,128)(2,1)} %pad_maximum_fusion.14.normed_ref, bf16[512,2048]{1,0:T(8,128)(2,1)} %pad_maximum_fusion.15.cotangent_ref, ...), custom_call_target="tpu_custom_call" | custom-call | flops 1073741824 | bytes 1048576 | tf_op jit(solution)/shard_map/pallas_call | solution.py:420
  384.1 14.4 %shard_map.317 = (bf16[512,1024]{1,0:T(8,128)(2,1)S(1)}, bf16[512,1024]{1,0:T(8,128)(2,1)S(1)}, bf16[512,2048]{1,0:T(8,128)(2,1)S(1)}, bf16[512,2048]{1,0:T(8,128)(2,1)}, f32[1,1024]{1,0:T(1,128)S(1)}) custom-call(bf16[512,2048]{1,0:T(8,128)(2,1)} %pad_maximum_fusion.16.normed_ref, bf16[512,2048]{1,0:T(8,128)(2,1)} %pad_maximum_fusion.17.cotangent_ref, ...), custom_call_target="tpu_custom_call" | custom-call | flops 1073741824 | bytes 1048576 | tf_op jit(solution)/shard_map/pallas_call | solution.py:420
  401.2 6.2 fusion.21
  413.5 23.9 %collective-permute-done.25 = bf16[256,2048]{1,0:T(8,128)(2,1)S(1)} collective-permute-done((bf16[256,2048]{1,0:T(8,128)(2,1)S(1)}, bf16[256,2048]{1,0:T(8,128)(2,1)S(1)}, u32[]{:S(2)}, u32[]{:S(2)}) %collective-permute-start.25) | collective-permute-done | bytes 1048608 | tf_op jit(solution)/shard_map/ppermute | solution.py:24
  454.5 9.1 %convolution_convert_fusion.3 = bf16[512,2048]{1,0:T(8,128)(2,1)S(1)} fusion(bf16[2048,2048]{1,0:T(8,128)(2,1)} %bitcast.40, bf16[256,2048]{1,0:T(8,128)(2,1)S(1)} %get-tuple-element.300, bf16[256,2048]{1,0:T(8,128)(2,1)S(1)} %get-tuple-element.299), kind=kOutput, calls=%fused_computation.53 | convolution fusion | flops 4300210176 | bytes 12582912 | tf_op jit(solution)/shard_map/dot_general | solution.py:19
  463.6 7.2 convolution_convert_fusion
  472.6 4.5 all-to-all-start.1
  488.3 4.9 fusion.18
  499.8 4.4 fusion.16
  504.2 30.1 %collective-permute-done.27 = bf16[2,256,2048]{2,1,0:T(8,128)(2,1)} collective-permute-done((bf16[2,256,2048]{2,1,0:T(8,128)(2,1)}, bf16[2,256,2048]{2,1,0:T(8,128)(2,1)}, u32[]{:S(2)}, u32[]{:S(2)}) %collective-permute-start.27) | collective-permute-done | bytes 2097184 | tf_op jit(solution)/shard_map/ppermute | solution.py:24
  534.4 9.5 %collective-permute-done.28 = bf16[2,256,2048]{2,1,0:T(8,128)(2,1)} collective-permute-done((bf16[2,256,2048]{2,1,0:T(8,128)(2,1)}, bf16[2,256,2048]{2,1,0:T(8,128)(2,1)}, u32[]{:S(2)}, u32[]{:S(2)}) %collective-permute-start.28) | collective-permute-done | bytes 2097184 | tf_op jit(solution)/shard_map/ppermute | solution.py:24
  560.9 12.1 %shard_map.319 = (f32[1024,256]{1,0:T(8,128)S(1)}, bf16[1024,512]{1,0:T(8,128)(2,1)S(1)}, f32[1024,768]{1,0:T(8,128)}, f32[1024,768]{1,0:T(8,128)}, f32[1,512]{1,0:T(1,128)S(1)}, /*index=5*/f32[1,512]{1,0:T(1,128)S(1)}) custom-call(s32[2]{0:T(128)S(1)} %pad_add_fusion.place_ref, s32[3]{0:T(128)S(1)} %bitcast_subtract_fusion.starts_ref, f32[1]{0:T(128)} %bitcast.3.decay_ref, ...), custom_call_target="tpu_custom_call" | custom-call | flops 587202560 | bytes 2097152 | tf_op jit(solution)/shard_map/pallas_call | solution.py:353
  579.2 12.0 %shard_map.318 = (f32[1024,256]{1,0:T(8,128)S(1)}, bf16[1024,512]{1,0:T(8,128)(2,1)S(1)}, f32[1024,768]{1,0:T(8,128)}, f32[1024,768]{1,0:T(8,128)}, f32[1,512]{1,0:T(1,128)S(1)}, /*index=5*/f32[1,512]{1,0:T(1,128)S(1)}) custom-call(s32[2]{0:T(128)S(1)} %pad_add_fusion.1.place_ref, s32[3]{0:T(128)S(1)} %bitcast_subtract_fusion.starts_ref, ...), custom_call_target="tpu_custom_call" | custom-call | flops 587202560 | bytes 2097152 | tf_op jit(solution)/shard_map/pallas_call | solution.py:353
  602.6 4.5 add_convert_fusion.17
  623.8 20.7 %multiply_reduce_fusion.1 = (f32[2048]{0:T(1024)S(1)}, bf16[2048,1536]{1,0:T(8,128)(2,1)}) fusion(bf16[4,2,256,1536]{3,2,1,0:T(8,128)(2,1)} %copy-done.30, bf16[1024,1536]{1,0:T(8,128)(2,1)} %copy-done.75, bf16[1024,1536]{1,0:T(8,128)(2,1)} %constant_dynamic-update-slice_fusion, bf16[1024,2048]{1,0:T(8,128)(2,1)} %copy-done.54, bf16[1024,2048]{1,0:T(8,128)(2,1)} %copy-done.53), kind=kOutput, calls=%fused_computation.2 | convolution fusion | flops 12929988608 | bytes 27271168 | tf_op jit(solution)/shard_map/dot_general | solution.py:19
  650.9 10.7 %convolution_convert_fusion.2 = bf16[1024,2048]{1,0:T(8,128)(2,1)} fusion(bf16[2048,1536]{1,0:T(8,128)(2,1)} %bitcast.259, s32[]{:T(128)S(6)} %select_n.660, bf16[1024,1536]{1,0:T(8,128)(2,1)} %constant_dynamic-update-slice_fusion, bf16[1024,1536]{1,0:T(8,128)(2,1)S(1)} %copy-done.76), kind=kOutput, calls=%fused_computation.38 | convolution fusion | flops 6450839552 | bytes 16777220 | tf_op jit(solution)/shard_map/dot_general | solution.py:19
  664.4 4.4 collective-permute-done.40
  689.5 7.4 collective-permute-done.42
  696.9 5.1 collective-permute-done.43
  714.6 9.4 %collective-permute-done.44 = bf16[256,2048]{1,0:T(8,128)(2,1)S(1)} collective-permute-done((bf16[256,2048]{1,0:T(8,128)(2,1)S(1)}, bf16[256,2048]{1,0:T(8,128)(2,1)S(1)}, u32[]{:S(2)}, u32[]{:S(2)}) %collective-permute-start.44) | collective-permute-done | bytes 1048608 | tf_op jit(solution)/shard_map/ppermute | solution.py:126
  733.3 12.5 %fusion.140 = (bf16[1024,2048]{1,0:T(8,128)(2,1)}, f32[1024,2048]{1,0:T(8,128)}) fusion(bf16[1024,2048]{1,0:T(8,128)(2,1)} %collective-permute-done.34, bf16[2048,1536]{1,0:T(8,128)(2,1)S(1)} %bitcast.264, s32[]{:T(128)S(6)} %select_n.659, bf16[1024,1536]{1,0:T(8,128)(2,1)} %constant_dynamic-update-slice_fusion, bf16[1024,1536]{1,0:T(8,128)(2,1)} %copy-done.75), kind=kOutput, calls=%fused_computation.380 | convolution fusion | flops 6455033856 | bytes 29360132 | tf_op jit(solution)/shard_map/dot_general | solution.py:19
  753.0 4.7 collective-permute-start.48
  762.2 16.5 %collective-permute-done.59 = bf16[2,256,1536]{2,1,0:T(8,128)(2,1)S(1)} collective-permute-done((bf16[2,256,1536]{2,1,0:T(8,128)(2,1)}, bf16[2,256,1536]{2,1,0:T(8,128)(2,1)S(1)}, u32[]{:S(2)}, u32[]{:S(2)}) %collective-permute-start.59) | collective-permute-done | bytes 1572896 | tf_op jit(solution)/shard_map/ppermute | solution.py:24
  784.6 4.6 collective-permute-start.50
  790.8 4.4 convert_add_fusion.11
  801.4 4.5 collective-permute-done.51
  811.5 4.9 add_convert_fusion.3
  873.1 5.2 collective-permute-done.58
  (662 shorter events, 356.4 us)
Async XLA Ops:
  7.2 101.9 %all-gather.3.cloned.1.call-start = ((), (), s32[]{:S(2)}) async-start(), calls=%async_computation.2 | async-start | bytes 5242880 | tf_op jit(solution)/shard_map/all_gather | solution.py:511
  51.5 35.9 %collective-permute-start.3 = (bf16[2,256,1536]{2,1,0:T(8,128)(2,1)}, bf16[2,256,1536]{2,1,0:T(8,128)(2,1)}, u32[]{:S(2)}, u32[]{:S(2)}) collective-permute-start(bf16[2,256,1536]{2,1,0:T(8,128)(2,1)} %pad_maximum_fusion.24), channel_id=1, source_target_pairs={{0,8},{4,12},{8,0},{12,4},{16,24},{20,28},{24,16},{28,20},{1,9},{5... | collective-permute-start | bytes 4718600 | tf_op jit(solution)/shard_map/ppermute | solution.py:24
  52.1 35.8 %collective-permute-start.4 = (bf16[2,256,1536]{2,1,0:T(8,128)(2,1)}, bf16[2,256,1536]{2,1,0:T(8,128)(2,1)}, u32[]{:S(2)}, u32[]{:S(2)}) collective-permute-start(bf16[2,256,1536]{2,1,0:T(8,128)(2,1)} %pad_maximum_fusion.26), channel_id=1, source_target_pairs={{0,16},{4,20},{8,24},{12,28},{16,0},{20,4},{24,8},{28,12},{1,17},{... | collective-permute-start | bytes 4718600 | tf_op jit(solution)/shard_map/ppermute | solution.py:24
  87.9 46.1 %collective-permute-start.7 = (bf16[2,256,2048]{2,1,0:T(8,128)(2,1)}, bf16[2,256,2048]{2,1,0:T(8,128)(2,1)}, u32[]{:S(2)}, u32[]{:S(2)}) collective-permute-start(bf16[2,256,2048]{2,1,0:T(8,128)(2,1)} %pad_maximum_fusion.12), channel_id=1, source_target_pairs={{0,8},{4,12},{8,0},{12,4},{16,24},{20,28},{24,16},{28,20},{1,9},{5... | collective-permute-start | bytes 6291464 | tf_op jit(solution)/shard_map/ppermute | solution.py:24
  89.2 45.7 %collective-permute-start.8 = (bf16[512,2048]{1,0:T(8,128)(2,1)}, bf16[512,2048]{1,0:T(8,128)(2,1)}, u32[]{:S(2)}, u32[]{:S(2)}) collective-permute-start(bf16[512,2048]{1,0:T(8,128)(2,1)} %param.33), channel_id=1, source_target_pairs={{0,16},{4,20},{8,24},{12,28},{16,0},{20,4},{24,8},{28,12},{1,17},{... | collective-permute-start | bytes 6291464 | tf_op jit(solution)/shard_map/ppermute | solution.py:24
  109.1 33.5 %collective-permute-start.5 = (bf16[1024,2048]{1,0:T(8,128)(2,1)}, bf16[1024,2048]{1,0:T(8,128)(2,1)S(1)}, u32[]{:S(2)}, u32[]{:S(2)}) collective-permute-start(bf16[1024,2048]{1,0:T(8,128)(2,1)} %all-gather.3.cloned.1.call-done), channel_id=1, source_target_pairs={{0,4},{4,0},{8,12},{12,8},{16,20},{20,16},{24,28},{28,24},{1,5},{5... | collective-permute-start | bytes 12582920 | tf_op jit(solution)/shard_map/ppermute | solution.py:24
  165.5 26.0 %collective-permute-start.9 = (bf16[256,2048]{1,0:T(8,128)(2,1)S(1)}, bf16[256,2048]{1,0:T(8,128)(2,1)S(1)}, u32[]{:S(2)}, u32[]{:S(2)}) collective-permute-start(bf16[256,2048]{1,0:T(8,128)(2,1)S(1)} %copy-done.110), channel_id=1, source_target_pairs={{0,8},{4,12},{8,0},{12,4},{16,24},{20,28},{24,16},{28,20},{1,9},{5... | collective-permute-start | bytes 3145736 | tf_op jit(solution)/shard_map/ppermute | solution.py:24
  166.5 25.3 %collective-permute-start.10 = (bf16[256,2048]{1,0:T(8,128)(2,1)S(1)}, bf16[256,2048]{1,0:T(8,128)(2,1)S(1)}, u32[]{:S(2)}, u32[]{:S(2)}) collective-permute-start(bf16[256,2048]{1,0:T(8,128)(2,1)S(1)} %copy-done.109), channel_id=1, source_target_pairs={{0,16},{4,20},{8,24},{12,28},{16,0},{20,4},{24,8},{28,12},{1,17},{... | collective-permute-start | bytes 3145736 | tf_op jit(solution)/shard_map/ppermute | solution.py:24
  175.7 61.5 %collective-permute-start.6 = (bf16[1024,768]{1,0:T(8,128)(2,1)}, bf16[1024,768]{1,0:T(8,128)(2,1)}, u32[]{:S(2)}, u32[]{:S(2)}) collective-permute-start(bf16[1024,768]{1,0:T(8,128)(2,1)} %pad_maximum_fusion.27), channel_id=1, source_target_pairs={{0,8},{4,12},{8,16},{12,20},{16,24},{20,28},{1,9},{5,13},{9,17},{1... | collective-permute-start | bytes 4718600 | tf_op jit(solution)/shard_map/ppermute | solution.py:29
  195.1 74.9 %collective-permute-start.12 = (bf16[2,256,2048]{2,1,0:T(8,128)(2,1)}, bf16[2,256,2048]{2,1,0:T(8,128)(2,1)}, u32[]{:S(2)}, u32[]{:S(2)}) collective-permute-start(bf16[2,256,2048]{2,1,0:T(8,128)(2,1)} %pad_maximum_fusion.9), channel_id=1, source_target_pairs={{0,8},{4,12},{8,0},{12,4},{16,24},{20,28},{24,16},{28,20},{1,9},{5... | collective-permute-start | bytes 6291464 | tf_op jit(solution)/shard_map/ppermute | solution.py:24
  203.5 69.6 %collective-permute-start.13 = (bf16[2,256,2048]{2,1,0:T(8,128)(2,1)}, bf16[2,256,2048]{2,1,0:T(8,128)(2,1)}, u32[]{:S(2)}, u32[]{:S(2)}) collective-permute-start(bf16[2,256,2048]{2,1,0:T(8,128)(2,1)} %pad_maximum_fusion.6), channel_id=1, source_target_pairs={{0,16},{4,20},{8,24},{12,28},{16,0},{20,4},{24,8},{28,12},{1,17},{... | collective-permute-start | bytes 6291464 | tf_op jit(solution)/shard_map/ppermute | solution.py:24
  248.7 39.5 %all-to-all-start = ((bf16[4,512,512]{2,1,0:T(8,128)(2,1)}), bf16[4,512,512]{2,1,0:T(8,128)(2,1)}, u32[]{:S(2)}, u32[]{:S(2)}) async-start(bf16[4,512,512]{2,1,0:T(8,128)(2,1)} %pad_maximum_fusion.10), calls=%async_computation | async-start | bytes 4194304 | tf_op jit(solution)/shard_map/all_to_all | solution.py:644
  309.6 49.1 %collective-permute-start.17 = (bf16[4,256,1024]{2,1,0:T(8,128)(2,1)S(1)}, bf16[4,256,1024]{2,1,0:T(8,128)(2,1)S(1)}, u32[]{:S(2)}, u32[]{:S(2)}) collective-permute-start(bf16[4,256,1024]{2,1,0:T(8,128)(2,1)S(1)} %copy-done.94), channel_id=1, source_target_pairs={{0,16},{4,20},{8,24},{12,28},{16,0},{20,4},{24,8},{28,12},{1,17},{... | collective-permute-start | bytes 6291464 | tf_op jit(solution)/shard_map/ppermute | solution.py:24
  316.0 43.5 %collective-permute-start.19 = (bf16[256,2048]{1,0:T(8,128)(2,1)S(1)}, bf16[256,2048]{1,0:T(8,128)(2,1)S(1)}, u32[]{:S(2)}, u32[]{:S(2)}) collective-permute-start(bf16[256,2048]{1,0:T(8,128)(2,1)S(1)} %add_convert_fusion.22), channel_id=1, source_target_pairs={{0,8},{4,12},{8,0},{12,4},{16,24},{20,28},{24,16},{28,20},{1,9},{5... | collective-permute-start | bytes 3145736 | tf_op jit(solution)/shard_map/ppermute | solution.py:24
  321.6 40.5 %collective-permute-start.15 = (bf16[256,2048]{1,0:T(8,128)(2,1)S(1)}, bf16[256,2048]{1,0:T(8,128)(2,1)S(1)}, u32[]{:S(2)}, u32[]{:S(2)}) collective-permute-start(bf16[256,2048]{1,0:T(8,128)(2,1)S(1)} %add_convert_fusion.22), channel_id=1, source_target_pairs={{0,4},{4,0},{8,12},{12,8},{16,20},{20,16},{24,28},{28,24},{1,5},{5... | collective-permute-start | bytes 3145736 | tf_op jit(solution)/shard_map/ppermute | solution.py:24
  359.5 22.9 %collective-permute-start.20 = (bf16[256,2048]{1,0:T(8,128)(2,1)S(1)}, bf16[256,2048]{1,0:T(8,128)(2,1)S(1)}, u32[]{:S(2)}, u32[]{:S(2)}) collective-permute-start(bf16[256,2048]{1,0:T(8,128)(2,1)S(1)} %collective-permute-done.19), channel_id=1, source_target_pairs={{0,4},{4,0},{8,12},{12,8},{16,20},{20,16},{24,28},{28,24},{1,5},{5... | collective-permute-start | bytes 3145736 | tf_op jit(solution)/shard_map/ppermute | solution.py:24
  382.0 31.5 %collective-permute-start.23 = (bf16[256,2048]{1,0:T(8,128)(2,1)}, bf16[256,2048]{1,0:T(8,128)(2,1)}, u32[]{:S(2)}, u32[]{:S(2)}) collective-permute-start(bf16[256,2048]{1,0:T(8,128)(2,1)} %slice.450), channel_id=1, source_target_pairs={{0,4},{4,0},{8,12},{12,8},{16,20},{20,16},{24,28},{28,24},{1,5},{5... | collective-permute-start | bytes 3145736 | tf_op jit(solution)/shard_map/ppermute | solution.py:24
  412.2 25.3 %collective-permute-start.25 = (bf16[256,2048]{1,0:T(8,128)(2,1)S(1)}, bf16[256,2048]{1,0:T(8,128)(2,1)S(1)}, u32[]{:S(2)}, u32[]{:S(2)}) collective-permute-start(bf16[256,2048]{1,0:T(8,128)(2,1)S(1)} %add_convert_fusion.20), channel_id=1, source_target_pairs={{0,8},{4,12},{8,0},{12,4},{16,24},{20,28},{24,16},{28,20},{1,9},{5... | collective-permute-start | bytes 3145736 | tf_op jit(solution)/shard_map/ppermute | solution.py:24
  450.6 45.4 %collective-permute-start.22 = (bf16[256,2048]{1,0:T(8,128)(2,1)}, bf16[256,2048]{1,0:T(8,128)(2,1)}, u32[]{:S(2)}, u32[]{:S(2)}) collective-permute-start(bf16[256,2048]{1,0:T(8,128)(2,1)} %slice.448), channel_id=1, source_target_pairs={{0,4},{4,0},{8,12},{12,8},{16,20},{20,16},{24,28},{28,24},{1,5},{5... | collective-permute-start | bytes 3145736 | tf_op jit(solution)/shard_map/ppermute | solution.py:24
  451.0 48.8 %collective-permute-start.35 = (bf16[512,2048]{1,0:T(8,128)(2,1)}, bf16[512,2048]{1,0:T(8,128)(2,1)}, u32[]{:S(2)}, u32[]{:S(2)}) collective-permute-start(bf16[512,2048]{1,0:T(8,128)(2,1)} %dynamic-slice_bitcast_fusion), channel_id=1, source_target_pairs={{0,16},{4,20},{8,24},{12,28},{16,0},{20,4},{24,8},{28,12},{1,17},{... | collective-permute-start | bytes 6291464 | tf_op jit(solution)/shard_map/ppermute | solution.py:24
  472.6 77.1 %all-to-all-start.1 = ((bf16[4,512,512]{2,1,0:T(8,128)(2,1)}), bf16[4,512,512]{2,1,0:T(8,128)(2,1)}, u32[]{:S(2)}, u32[]{:S(2)}) async-start(bf16[4,512,512]{2,1,0:T(8,128)(2,1)} %pad_maximum_fusion.21), calls=%async_computation.1 | async-start | bytes 4194304 | tf_op jit(solution)/shard_map/all_to_all | solution.py:644
  486.7 47.7 %collective-permute-start.27 = (bf16[2,256,2048]{2,1,0:T(8,128)(2,1)}, bf16[2,256,2048]{2,1,0:T(8,128)(2,1)}, u32[]{:S(2)}, u32[]{:S(2)}) collective-permute-start(bf16[2,256,2048]{2,1,0:T(8,128)(2,1)} %pad_maximum_fusion.19), channel_id=1, source_target_pairs={{0,8},{4,12},{8,0},{12,4},{16,24},{20,28},{24,16},{28,20},{1,9},{5... | collective-permute-start | bytes 6291464 | tf_op jit(solution)/shard_map/ppermute | solution.py:24
  487.4 56.5 %collective-permute-start.28 = (bf16[2,256,2048]{2,1,0:T(8,128)(2,1)}, bf16[2,256,2048]{2,1,0:T(8,128)(2,1)}, u32[]{:S(2)}, u32[]{:S(2)}) collective-permute-start(bf16[2,256,2048]{2,1,0:T(8,128)(2,1)} %pad_maximum_fusion.20), channel_id=1, source_target_pairs={{0,16},{4,20},{8,24},{12,28},{16,0},{20,4},{24,8},{28,12},{1,17},{... | collective-permute-start | bytes 6291464 | tf_op jit(solution)/shard_map/ppermute | solution.py:24
  552.9 45.5 %collective-permute-start.29 = (bf16[256,2048]{1,0:T(8,128)(2,1)}, bf16[256,2048]{1,0:T(8,128)(2,1)}, u32[]{:S(2)}, u32[]{:S(2)}) collective-permute-start(bf16[256,2048]{1,0:T(8,128)(2,1)} %fusion.60), channel_id=1, source_target_pairs={{0,8},{4,12},{8,0},{12,4},{16,24},{20,28},{24,16},{28,20},{1,9},{5... | collective-permute-start | bytes 3145736 | tf_op jit(solution)/shard_map/ppermute | solution.py:24
  554.1 44.3 %collective-permute-start.30 = (bf16[256,2048]{1,0:T(8,128)(2,1)}, bf16[256,2048]{1,0:T(8,128)(2,1)}, u32[]{:S(2)}, u32[]{:S(2)}) collective-permute-start(bf16[256,2048]{1,0:T(8,128)(2,1)} %fusion.59), channel_id=1, source_target_pairs={{0,16},{4,20},{8,24},{12,28},{16,0},{20,4},{24,8},{28,12},{1,17},{... | collective-permute-start | bytes 3145736 | tf_op jit(solution)/shard_map/ppermute | solution.py:24
  556.8 45.7 %collective-permute-start.36 = (bf16[256,2048]{1,0:T(8,128)(2,1)}, bf16[256,2048]{1,0:T(8,128)(2,1)}, u32[]{:S(2)}, u32[]{:S(2)}) collective-permute-start(bf16[256,2048]{1,0:T(8,128)(2,1)} %get-tuple-element.186), channel_id=1, source_target_pairs={{0,1},{4,5},{8,9},{12,13},{16,17},{20,21},{24,25},{28,29}} | collective-permute-start | bytes 3145736 | tf_op jit(solution)/shard_map/ppermute | solution.py:126
  559.1 43.4 %collective-permute-start.37 = (bf16[256,2048]{1,0:T(8,128)(2,1)}, bf16[256,2048]{1,0:T(8,128)(2,1)}, u32[]{:S(2)}, u32[]{:S(2)}) collective-permute-start(bf16[256,2048]{1,0:T(8,128)(2,1)} %get-tuple-element.186), channel_id=1, source_target_pairs={{3,2},{7,6},{11,10},{15,14},{19,18},{23,22},{27,26},{31,30}} | collective-permute-start | bytes 3145736 | tf_op jit(solution)/shard_map/ppermute | solution.py:126
  577.6 39.5 %collective-permute-start.33 = (bf16[1024,768]{1,0:T(8,128)(2,1)}, bf16[1024,768]{1,0:T(8,128)(2,1)}, u32[]{:S(2)}, u32[]{:S(2)}) collective-permute-start(bf16[1024,768]{1,0:T(8,128)(2,1)} %convert_element_type.538), channel_id=1, source_target_pairs={{8,0},{12,4},{16,8},{20,12},{24,16},{28,20},{9,1},{13,5},{17,9},{2... | collective-permute-start | bytes 4718600 | tf_op jit(solution)/shard_map/ppermute | solution.py:29
  607.1 76.1 %collective-permute-start.31 = (bf16[256,2048]{1,0:T(8,128)(2,1)}, bf16[256,2048]{1,0:T(8,128)(2,1)}, u32[]{:S(2)}, u32[]{:S(2)}) collective-permute-start(bf16[256,2048]{1,0:T(8,128)(2,1)} %add_convert_fusion.21), channel_id=1, source_target_pairs={{0,8},{4,12},{8,0},{12,4},{16,24},{20,28},{24,16},{28,20},{1,9},{5... | collective-permute-start | bytes 3145736 | tf_op jit(solution)/shard_map/ppermute | solution.py:24
  609.8 34.7 %collective-permute-start.38 = (bf16[256,2048]{1,0:T(8,128)(2,1)}, bf16[256,2048]{1,0:T(8,128)(2,1)}, u32[]{:S(2)}, u32[]{:S(2)}) collective-permute-start(bf16[256,2048]{1,0:T(8,128)(2,1)} %get-tuple-element.188), channel_id=1, source_target_pairs={{0,1},{1,2},{4,5},{5,6},{8,9},{9,10},{12,13},{13,14},{16,17},{17,1... | collective-permute-start | bytes 3145736 | tf_op jit(solution)/shard_map/ppermute | solution.py:126
  612.0 32.5 %collective-permute-start.39 = (bf16[256,2048]{1,0:T(8,128)(2,1)}, bf16[256,2048]{1,0:T(8,128)(2,1)}, u32[]{:S(2)}, u32[]{:S(2)}) collective-permute-start(bf16[256,2048]{1,0:T(8,128)(2,1)} %get-tuple-element.189), channel_id=1, source_target_pairs={{3,2},{2,1},{7,6},{6,5},{11,10},{10,9},{15,14},{14,13},{19,18},{18... | collective-permute-start | bytes 3145736 | tf_op jit(solution)/shard_map/ppermute | solution.py:126
  614.0 69.2 %collective-permute-start.32 = (bf16[4,256,1024]{2,1,0:T(8,128)(2,1)}, bf16[4,256,1024]{2,1,0:T(8,128)(2,1)}, u32[]{:S(2)}, u32[]{:S(2)}) collective-permute-start(bf16[4,256,1024]{2,1,0:T(8,128)(2,1)} %dynamic-slice_bitcast_fusion.1), channel_id=1, source_target_pairs={{0,16},{4,20},{8,24},{12,28},{16,0},{20,4},{24,8},{28,12},{1,17},{... | collective-permute-start | bytes 6291464 | tf_op jit(solution)/shard_map/ppermute | solution.py:24
  647.6 21.2 %collective-permute-start.40 = (bf16[256,2048]{1,0:T(8,128)(2,1)S(1)}, bf16[256,2048]{1,0:T(8,128)(2,1)S(1)}, u32[]{:S(2)}, u32[]{:S(2)}) collective-permute-start(bf16[256,2048]{1,0:T(8,128)(2,1)S(1)} %get-tuple-element.190), channel_id=1, source_target_pairs={{0,1},{1,2},{2,3},{4,5},{5,6},{6,7},{8,9},{9,10},{10,11},{12,13},{... | collective-permute-start | bytes 3145736 | tf_op jit(solution)/shard_map/ppermute | solution.py:126
  649.2 23.9 %collective-permute-start.41 = (bf16[256,2048]{1,0:T(8,128)(2,1)S(1)}, bf16[256,2048]{1,0:T(8,128)(2,1)S(1)}, u32[]{:S(2)}, u32[]{:S(2)}) collective-permute-start(bf16[256,2048]{1,0:T(8,128)(2,1)S(1)} %get-tuple-element.191), channel_id=1, source_target_pairs={{3,2},{2,1},{1,0},{7,6},{6,5},{5,4},{11,10},{10,9},{9,8},{15,14},{... | collective-permute-start | bytes 3145736 | tf_op jit(solution)/shard_map/ppermute | solution.py:126
  661.5 71.8 %collective-permute-start.34 = (bf16[1024,2048]{1,0:T(8,128)(2,1)}, bf16[1024,2048]{1,0:T(8,128)(2,1)}, u32[]{:S(2)}, u32[]{:S(2)}) collective-permute-start(bf16[1024,2048]{1,0:T(8,128)(2,1)} %convolution_convert_fusion.2), channel_id=1, source_target_pairs={{0,4},{4,0},{8,12},{12,8},{16,20},{20,16},{24,28},{28,24},{1,5},{5... | collective-permute-start | bytes 12582920 | tf_op jit(solution)/shard_map/ppermute | solution.py:24
  675.5 21.4 %collective-permute-start.42 = (bf16[256,2048]{1,0:T(8,128)(2,1)}, bf16[256,2048]{1,0:T(8,128)(2,1)}, u32[]{:S(2)}, u32[]{:S(2)}) collective-permute-start(bf16[256,2048]{1,0:T(8,128)(2,1)} %get-tuple-element.192), channel_id=1, source_target_pairs={{0,1},{1,2},{2,3},{4,5},{5,6},{6,7},{8,9},{9,10},{10,11},{12,13},{... | collective-permute-start | bytes 3145736 | tf_op jit(solution)/shard_map/ppermute | solution.py:126
  679.4 22.6 %collective-permute-start.43 = (bf16[256,2048]{1,0:T(8,128)(2,1)}, bf16[256,2048]{1,0:T(8,128)(2,1)}, u32[]{:S(2)}, u32[]{:S(2)}) collective-permute-start(bf16[256,2048]{1,0:T(8,128)(2,1)} %get-tuple-element.193), channel_id=1, source_target_pairs={{3,2},{2,1},{1,0},{7,6},{6,5},{5,4},{11,10},{10,9},{9,8},{15,14},{... | collective-permute-start | bytes 3145736 | tf_op jit(solution)/shard_map/ppermute | solution.py:126
  683.2 75.8 %collective-permute-start.18 = (bf16[256,2048]{1,0:T(8,128)(2,1)}, bf16[256,2048]{1,0:T(8,128)(2,1)}, u32[]{:S(2)}, u32[]{:S(2)}) collective-permute-start(bf16[256,2048]{1,0:T(8,128)(2,1)} %slice.445), channel_id=1, source_target_pairs={{0,4},{4,0},{8,12},{12,8},{16,20},{20,16},{24,28},{28,24},{1,5},{5... | collective-permute-start | bytes 3145736 | tf_op jit(solution)/shard_map/ppermute | solution.py:24
  707.4 20.8 %collective-permute-start.45 = (bf16[256,2048]{1,0:T(8,128)(2,1)S(1)}, bf16[256,2048]{1,0:T(8,128)(2,1)S(1)}, u32[]{:S(2)}, u32[]{:S(2)}) collective-permute-start(bf16[256,2048]{1,0:T(8,128)(2,1)S(1)} %get-tuple-element.195), channel_id=1, source_target_pairs={{3,2},{2,1},{1,0},{7,6},{6,5},{5,4},{11,10},{10,9},{9,8},{15,14},{... | collective-permute-start | bytes 3145736 | tf_op jit(solution)/shard_map/ppermute | solution.py:126
  729.3 22.2 %collective-permute-start.46 = (bf16[256,2048]{1,0:T(8,128)(2,1)S(1)}, bf16[256,2048]{1,0:T(8,128)(2,1)S(1)}, u32[]{:S(2)}, u32[]{:S(2)}) collective-permute-start(bf16[256,2048]{1,0:T(8,128)(2,1)S(1)} %get-tuple-element.196), channel_id=1, source_target_pairs={{0,1},{1,2},{2,3},{4,5},{5,6},{6,7},{8,9},{9,10},{10,11},{12,13},{... | collective-permute-start | bytes 3145736 | tf_op jit(solution)/shard_map/ppermute | solution.py:126
  745.9 32.9 %collective-permute-start.59 = (bf16[2,256,1536]{2,1,0:T(8,128)(2,1)}, bf16[2,256,1536]{2,1,0:T(8,128)(2,1)S(1)}, u32[]{:S(2)}, u32[]{:S(2)}) collective-permute-start(bf16[2,256,1536]{2,1,0:T(8,128)(2,1)} %pad_maximum_fusion.28), channel_id=1, source_target_pairs={{0,8},{4,12},{8,0},{12,4},{16,24},{20,28},{24,16},{28,20},{1,9},{5... | collective-permute-start | bytes 4718600 | tf_op jit(solution)/shard_map/ppermute | solution.py:24
  748.3 32.7 %collective-permute-start.60 = (bf16[2,256,1536]{2,1,0:T(8,128)(2,1)}, bf16[2,256,1536]{2,1,0:T(8,128)(2,1)S(1)}, u32[]{:S(2)}, u32[]{:S(2)}) collective-permute-start(bf16[2,256,1536]{2,1,0:T(8,128)(2,1)} %pad_maximum_fusion.29), channel_id=1, source_target_pairs={{0,16},{4,20},{8,24},{12,28},{16,0},{20,4},{24,8},{28,12},{1,17},{... | collective-permute-start | bytes 4718600 | tf_op jit(solution)/shard_map/ppermute | solution.py:24
  753.0 29.9 %collective-permute-start.48 = (bf16[256,2048]{1,0:T(8,128)(2,1)S(1)}, bf16[256,2048]{1,0:T(8,128)(2,1)S(1)}, u32[]{:S(2)}, u32[]{:S(2)}) collective-permute-start(bf16[256,2048]{1,0:T(8,128)(2,1)S(1)} %get-tuple-element.199), channel_id=1, source_target_pairs={{0,1},{1,2},{2,3},{4,5},{5,6},{6,7},{8,9},{9,10},{10,11},{12,13},{... | collective-permute-start | bytes 3145736 | tf_op jit(solution)/shard_map/ppermute | solution.py:126
  757.7 25.2 %collective-permute-start.49 = (bf16[256,2048]{1,0:T(8,128)(2,1)S(1)}, bf16[256,2048]{1,0:T(8,128)(2,1)S(1)}, u32[]{:S(2)}, u32[]{:S(2)}) collective-permute-start(bf16[256,2048]{1,0:T(8,128)(2,1)S(1)} %get-tuple-element.200), channel_id=1, source_target_pairs={{3,2},{2,1},{1,0},{7,6},{6,5},{5,4},{11,10},{10,9},{9,8},{15,14},{... | collective-permute-start | bytes 3145736 | tf_op jit(solution)/shard_map/ppermute | solution.py:126
  799.1 32.3 %collective-permute-start.63 = (bf16[256,1536]{1,0:T(8,128)(2,1)}, bf16[256,1536]{1,0:T(8,128)(2,1)}, u32[]{:S(2)}, u32[]{:S(2)}) collective-permute-start(bf16[256,1536]{1,0:T(8,128)(2,1)} %select_convert_fusion), channel_id=1, source_target_pairs={{0,4},{4,0},{8,12},{12,8},{16,20},{20,16},{24,28},{28,24},{1,5},{5... | collective-permute-start | bytes 2359304 | tf_op jit(solution)/shard_map/ppermute | solution.py:24
  818.8 22.8 %collective-permute-start.52 = (bf16[256,2048]{1,0:T(8,128)(2,1)}, bf16[256,2048]{1,0:T(8,128)(2,1)S(1)}, u32[]{:S(2)}, u32[]{:S(2)}) collective-permute-start(bf16[256,2048]{1,0:T(8,128)(2,1)} %get-tuple-element.203), channel_id=1, source_target_pairs={{0,1},{1,2},{2,3},{4,5},{5,6},{6,7},{8,9},{9,10},{10,11},{12,13},{... | collective-permute-start | bytes 3145736 | tf_op jit(solution)/shard_map/ppermute | solution.py:126
  822.3 23.4 %collective-permute-start.53 = (bf16[256,2048]{1,0:T(8,128)(2,1)}, bf16[256,2048]{1,0:T(8,128)(2,1)S(1)}, u32[]{:S(2)}, u32[]{:S(2)}) collective-permute-start(bf16[256,2048]{1,0:T(8,128)(2,1)} %get-tuple-element.204), channel_id=1, source_target_pairs={{3,2},{2,1},{1,0},{7,6},{6,5},{5,4},{11,10},{10,9},{9,8},{15,14},{... | collective-permute-start | bytes 3145736 | tf_op jit(solution)/shard_map/ppermute | solution.py:126
  827.0 38.8 %collective-permute-start.64 = (bf16[2,256,1024]{2,1,0:T(8,128)(2,1)}, bf16[2,256,1024]{2,1,0:T(8,128)(2,1)S(1)}, u32[]{:S(2)}, u32[]{:S(2)}) collective-permute-start(bf16[2,256,1024]{2,1,0:T(8,128)(2,1)} %pad_maximum_fusion.36), channel_id=1, source_target_pairs={{0,8},{4,12},{8,0},{12,4},{16,24},{20,28},{24,16},{28,20},{1,9},{5... | collective-permute-start | bytes 3145736 | tf_op jit(solution)/shard_map/ppermute | solution.py:24
  (175 other events, 1705.8 us)
Sparse Core Ops, SparseCore 0:
  28.0 81.0 all-gather.2

commit v3 on v2

--- a/solution.py
+++ b/solution.py
@@ -139,11 +139,15 @@
 
 
 def small_sum(block):
-    for axis in ("seq", "grp"):
-        devices, bit = lax.axis_size(axis), 1
-        while bit < devices:
-            block = block + lax.ppermute(block, axis, [(i, i ^ bit) for i in range(devices)])
-            bit *= 2
+    bit = lax.axis_size("seq") // 2
+    while bit:
+        mine = lax.axis_index("seq") // bit % 2
+        block = cut(block, mine, bit, 0) + flip(cut(block, 1 - mine, bit, 0), bit)
+        bit //= 2
+    groups, bit = lax.axis_size("grp"), 1
+    while bit < groups:
+        block = block + lax.ppermute(block, "grp", [(i, i ^ bit) for i in range(groups)])
+        bit *= 2
     return block
 
 
@@ -880,7 +884,7 @@
         )
     ]
     sums = small_sum(jnp.concatenate(pieces, axis=1))
-    sums = pick(sums, seq_index)
+    sums = sums[0]
     first_back = jax.vjp(lambda v: layer_norm(v, gain_one, bias_one), inputs)[1]
     tokens_grad = (grad_hidden + first_back(after(grad_normed, sums))[0]).astype(BF16)
     taken, start = [], 0

time: 899 us -> 896 us (level)
  starting transfers between devices: 126 us -> 95.1 us
  waiting for transfers between devices: 295 us -> 322 us
    ppermute x41 -> x44, waiting for transfers between devices: 207 us -> 240 us  [flip(): return lax.ppermute(block, 'seq', [(i, i ^ bit) for i in range(devices)])]
    ppermute x41 -> x44, starting transfers between devices: 65.6 us -> 38.1 us  [flip(): return lax.ppermute(block, 'seq', [(i, i ^ bit) for i in range(devices)])]
  transfers between devices with their start and end apart: 69 -> 69, of which waited for: 36 -> 35; matrix products, arithmetic and copies ran while one was open for 34% -> 34% of each run, Pallas kernels for 7% -> 7%
where the time goes in v3:
time: 896 us; the launch traced here: 888 us
  waiting for transfers between devices  322 us (36%)
  other arithmetic  172 us (19%)
  local copies, waits for them, and re-layouts  109 us (12%)
  matrix products  98.5 us (11%)
  starting transfers between devices  95.1 us (11%)
  Pallas kernels  64.1 us (7%)
  between operations  17.7 us (2%)
  blocking collectives  10.3 us (1%)
    ppermute x44, waiting for transfers between devices, flip(): return lax.ppermute(block, 'seq', [(i, i ^ bit) for i in range(devices)])  240 us
    dot_general x12, matrix products, dot(): return lax.dot_general(a, b, (dims, ((), ())), preferred_element_type=F32)  98.5 us
    ppermute x18, waiting for transfers between devices, step(): self.came[way].append(lax.ppermute(block, 'grp', pairs))  47.5 us
    ppermute x18, starting transfers between devices, step(): self.came[way].append(lax.ppermute(block, 'grp', pairs))  41.5 us
    ppermute x44, starting transfers between devices, flip(): return lax.ppermute(block, 'seq', [(i, i ^ bit) for i in range(devices)])  38.1 us
    unnamed x334, local copies, waits for them, and re-layouts  31 us
    pallas_call x2, Pallas kernels, feed(): pl.pallas_call(feed_kernel, out_shape=(jax.ShapeDtypeStruct((rows, hidden...  28.7 us
    pallas_call x2, Pallas kernels, retention_back(): pl.pallas_call(retention_back_kernel, out_shape=(jax.ShapeDtypeStruct((ro...  24.1 us
  transfers between devices with their start and end apart: 69, of which 35 were waited for; matrix products, arithmetic and copies ran while one was open for 34% of the time, Pallas kernels for 7%

profile of v3, /device:TPU:0, one launch (start us, length us, event | category | flops | bytes accessed | tf_op | source)
XLA Modules:
  0.0 888.4 jit_solution(8691512855563190789)
XLA Ops:
  16.1 10.3 %all-gather = bf16[8,1,2048]{2,1,0:T(2,128)(2,1)S(1)} all-gather(bf16[1,1,2048]{2,1,0:T(2,128)(2,1)S(1)} %bitcast.302), channel_id=1, replica_groups=mesh['seq'=8,'grp'=4] {'seq'}, dimensions={0}, use_global_device_ids=true | all-gather | bytes 36864 | tf_op jit(solution)/shard_map/all_gather | solution.py:500
  30.0 17.7 %collective-permute-done.1 = bf16[256,1536]{1,0:T(8,128)(2,1)S(1)} collective-permute-done((bf16[256,1536]{1,0:T(8,128)(2,1)S(1)}, bf16[256,1536]{1,0:T(8,128)(2,1)S(1)}, u32[]{:S(2)}, u32[]{:S(2)}) %collective-permute-start.1) | collective-permute-done | bytes 786464 | tf_op jit(solution)/shard_map/ppermute | solution.py:24
  58.4 5.7 multiply_sine_fusion
  64.1 23.3 %collective-permute-done.3 = bf16[2,256,1536]{2,1,0:T(8,128)(2,1)} collective-permute-done((bf16[2,256,1536]{2,1,0:T(8,128)(2,1)}, bf16[2,256,1536]{2,1,0:T(8,128)(2,1)}, u32[]{:S(2)}, u32[]{:S(2)}) %collective-permute-start.3) | collective-permute-done | bytes 1572896 | tf_op jit(solution)/shard_map/ppermute | solution.py:24
  92.3 16.8 %all-gather.3.cloned.1.call-done = bf16[1024,2048]{1,0:T(8,128)(2,1)} async-done(((bf16[256,2048]{1,0:T(8,128)(2,1)}), bf16[1024,2048]{1,0:T(8,128)(2,1)}) %all-gather.3.cloned.1.call-update) | async-done | bytes 4194320 | tf_op jit(solution)/shard_map/all_gather | solution.py:515
  115.1 18.9 %collective-permute-done.7 = bf16[2,256,2048]{2,1,0:T(8,128)(2,1)} collective-permute-done((bf16[2,256,2048]{2,1,0:T(8,128)(2,1)}, bf16[2,256,2048]{2,1,0:T(8,128)(2,1)}, u32[]{:S(2)}, u32[]{:S(2)}) %collective-permute-start.7) | collective-permute-done | bytes 2097184 | tf_op jit(solution)/shard_map/ppermute | solution.py:24
  146.0 7.6 convolution_convert_fusion.4.gate_ref
  153.6 7.0 convolution_convert_fusion.5.value_high_ref.value_low_ref
  167.6 5.6 fusion.84
  182.7 8.9 %collective-permute-done.9 = bf16[256,2048]{1,0:T(8,128)(2,1)S(1)} collective-permute-done((bf16[256,2048]{1,0:T(8,128)(2,1)S(1)}, bf16[256,2048]{1,0:T(8,128)(2,1)S(1)}, u32[]{:S(2)}, u32[]{:S(2)}) %collective-permute-start.9) | collective-permute-done | bytes 1048608 | tf_op jit(solution)/shard_map/ppermute | solution.py:24
  191.6 32.3 %collective-permute-done.10 = bf16[256,2048]{1,0:T(8,128)(2,1)S(1)} collective-permute-done((bf16[256,2048]{1,0:T(8,128)(2,1)S(1)}, bf16[256,2048]{1,0:T(8,128)(2,1)S(1)}, u32[]{:S(2)}, u32[]{:S(2)}) %collective-permute-start.10) | collective-permute-done | bytes 1048608 | tf_op jit(solution)/shard_map/ppermute | solution.py:24
  227.8 5.6 shard_map.315
  240.7 5.6 shard_map.314
  248.8 5.0 all-to-all-start
  253.8 4.3 broadcast_in_dim.77
  259.7 10.3 %collective-permute-done.12 = bf16[2,256,2048]{2,1,0:T(8,128)(2,1)} collective-permute-done((bf16[2,256,2048]{2,1,0:T(8,128)(2,1)}, bf16[2,256,2048]{2,1,0:T(8,128)(2,1)}, u32[]{:S(2)}, u32[]{:S(2)}) %collective-permute-start.12) | collective-permute-done | bytes 2097184 | tf_op jit(solution)/shard_map/ppermute | solution.py:24
  277.9 10.0 %all-to-all-done = bf16[4,512,512]{2,1,0:T(8,128)(2,1)} async-done(((bf16[4,512,512]{2,1,0:T(8,128)(2,1)}), bf16[4,512,512]{2,1,0:T(8,128)(2,1)}, u32[]{:S(2)}, u32[]{:S(2)}) %all-to-all-start) | async-done | bytes 2097184 | tf_op jit(solution)/shard_map/all_to_all | solution.py:648
  289.7 7.8 fusion.97
  300.7 5.4 collective-permute-done.16
  323.2 35.4 %collective-permute-done.17 = bf16[4,256,1024]{2,1,0:T(8,128)(2,1)S(1)} collective-permute-done((bf16[4,256,1024]{2,1,0:T(8,128)(2,1)S(1)}, bf16[4,256,1024]{2,1,0:T(8,128)(2,1)S(1)}, u32[]{:S(2)}, u32[]{:S(2)}) %collective-permute-start.17) | collective-permute-done | bytes 2097184 | tf_op jit(solution)/shard_map/ppermute | solution.py:24
  363.7 14.3 %shard_map.316 = (bf16[512,1024]{1,0:T(8,128)(2,1)S(1)}, bf16[512,1024]{1,0:T(8,128)(2,1)S(1)}, bf16[512,2048]{1,0:T(8,128)(2,1)S(1)}, bf16[512,2048]{1,0:T(8,128)(2,1)}, f32[1,1024]{1,0:T(1,128)S(1)}) custom-call(bf16[512,2048]{1,0:T(8,128)(2,1)} %pad_maximum_fusion.14.normed_ref, bf16[512,2048]{1,0:T(8,128)(2,1)} %pad_maximum_fusion.15.cotangent_ref, ...), custom_call_target="tpu_custom_call" | custom-call | flops 1073741824 | bytes 1048576 | tf_op jit(solution)/shard_map/pallas_call | solution.py:424
  384.0 14.4 %shard_map.317 = (bf16[512,1024]{1,0:T(8,128)(2,1)S(1)}, bf16[512,1024]{1,0:T(8,128)(2,1)S(1)}, bf16[512,2048]{1,0:T(8,128)(2,1)S(1)}, bf16[512,2048]{1,0:T(8,128)(2,1)}, f32[1,1024]{1,0:T(1,128)S(1)}) custom-call(bf16[512,2048]{1,0:T(8,128)(2,1)} %pad_maximum_fusion.16.normed_ref, bf16[512,2048]{1,0:T(8,128)(2,1)} %pad_maximum_fusion.17.cotangent_ref, ...), custom_call_target="tpu_custom_call" | custom-call | flops 1073741824 | bytes 1048576 | tf_op jit(solution)/shard_map/pallas_call | solution.py:424
  401.1 6.2 fusion.21
  413.4 24.0 %collective-permute-done.25 = bf16[256,2048]{1,0:T(8,128)(2,1)S(1)} collective-permute-done((bf16[256,2048]{1,0:T(8,128)(2,1)S(1)}, bf16[256,2048]{1,0:T(8,128)(2,1)S(1)}, u32[]{:S(2)}, u32[]{:S(2)}) %collective-permute-start.25) | collective-permute-done | bytes 1048608 | tf_op jit(solution)/shard_map/ppermute | solution.py:24
  454.5 9.1 %convolution_convert_fusion.3 = bf16[512,2048]{1,0:T(8,128)(2,1)S(1)} fusion(bf16[2048,2048]{1,0:T(8,128)(2,1)} %bitcast.40, bf16[256,2048]{1,0:T(8,128)(2,1)S(1)} %get-tuple-element.300, bf16[256,2048]{1,0:T(8,128)(2,1)S(1)} %get-tuple-element.299), kind=kOutput, calls=%fused_computation.53 | convolution fusion | flops 4300210176 | bytes 12582912 | tf_op jit(solution)/shard_map/dot_general | solution.py:19
  463.6 7.2 convolution_convert_fusion
  472.6 4.5 all-to-all-start.1
  488.2 4.9 fusion.18
  499.8 4.4 fusion.16
  504.2 30.2 %collective-permute-done.27 = bf16[2,256,2048]{2,1,0:T(8,128)(2,1)} collective-permute-done((bf16[2,256,2048]{2,1,0:T(8,128)(2,1)}, bf16[2,256,2048]{2,1,0:T(8,128)(2,1)}, u32[]{:S(2)}, u32[]{:S(2)}) %collective-permute-start.27) | collective-permute-done | bytes 2097184 | tf_op jit(solution)/shard_map/ppermute | solution.py:24
  534.4 9.6 %collective-permute-done.28 = bf16[2,256,2048]{2,1,0:T(8,128)(2,1)} collective-permute-done((bf16[2,256,2048]{2,1,0:T(8,128)(2,1)}, bf16[2,256,2048]{2,1,0:T(8,128)(2,1)}, u32[]{:S(2)}, u32[]{:S(2)}) %collective-permute-start.28) | collective-permute-done | bytes 2097184 | tf_op jit(solution)/shard_map/ppermute | solution.py:24
  560.9 12.1 %shard_map.319 = (f32[1024,256]{1,0:T(8,128)S(1)}, bf16[1024,512]{1,0:T(8,128)(2,1)S(1)}, f32[1024,768]{1,0:T(8,128)}, f32[1024,768]{1,0:T(8,128)}, f32[1,512]{1,0:T(1,128)S(1)}, /*index=5*/f32[1,512]{1,0:T(1,128)S(1)}) custom-call(s32[2]{0:T(128)S(1)} %pad_add_fusion.place_ref, s32[3]{0:T(128)S(1)} %bitcast_subtract_fusion.starts_ref, f32[1]{0:T(128)} %bitcast.3.decay_ref, ...), custom_call_target="tpu_custom_call" | custom-call | flops 587202560 | bytes 2097152 | tf_op jit(solution)/shard_map/pallas_call | solution.py:357
  579.2 12.0 %shard_map.318 = (f32[1024,256]{1,0:T(8,128)S(1)}, bf16[1024,512]{1,0:T(8,128)(2,1)S(1)}, f32[1024,768]{1,0:T(8,128)}, f32[1024,768]{1,0:T(8,128)}, f32[1,512]{1,0:T(1,128)S(1)}, /*index=5*/f32[1,512]{1,0:T(1,128)S(1)}) custom-call(s32[2]{0:T(128)S(1)} %pad_add_fusion.1.place_ref, s32[3]{0:T(128)S(1)} %bitcast_subtract_fusion.starts_ref, ...), custom_call_target="tpu_custom_call" | custom-call | flops 587202560 | bytes 2097152 | tf_op jit(solution)/shard_map/pallas_call | solution.py:357
  602.6 4.5 add_convert_fusion.17
  623.8 20.7 %multiply_reduce_fusion.1 = (f32[2048]{0:T(1024)S(1)}, bf16[2048,1536]{1,0:T(8,128)(2,1)}) fusion(bf16[4,2,256,1536]{3,2,1,0:T(8,128)(2,1)} %copy-done.30, bf16[1024,1536]{1,0:T(8,128)(2,1)} %copy-done.75, bf16[1024,1536]{1,0:T(8,128)(2,1)} %constant_dynamic-update-slice_fusion, bf16[1024,2048]{1,0:T(8,128)(2,1)} %copy-done.54, bf16[1024,2048]{1,0:T(8,128)(2,1)} %copy-done.53), kind=kOutput, calls=%fused_computation.2 | convolution fusion | flops 12929988608 | bytes 27271168 | tf_op jit(solution)/shard_map/dot_general | solution.py:19
  650.9 10.7 %convolution_convert_fusion.2 = bf16[1024,2048]{1,0:T(8,128)(2,1)} fusion(bf16[2048,1536]{1,0:T(8,128)(2,1)} %bitcast.259, s32[]{:T(128)S(6)} %select_n.687, bf16[1024,1536]{1,0:T(8,128)(2,1)} %constant_dynamic-update-slice_fusion, bf16[1024,1536]{1,0:T(8,128)(2,1)S(1)} %copy-done.76), kind=kOutput, calls=%fused_computation.38 | convolution fusion | flops 6450839552 | bytes 16777220 | tf_op jit(solution)/shard_map/dot_general | solution.py:19
  664.4 4.4 collective-permute-done.40
  668.8 4.3 collective-permute-done.41
  689.6 7.4 collective-permute-done.42
  696.9 5.1 collective-permute-done.43
  714.7 9.4 %collective-permute-done.44 = bf16[256,2048]{1,0:T(8,128)(2,1)S(1)} collective-permute-done((bf16[256,2048]{1,0:T(8,128)(2,1)S(1)}, bf16[256,2048]{1,0:T(8,128)(2,1)S(1)}, u32[]{:S(2)}, u32[]{:S(2)}) %collective-permute-start.44) | collective-permute-done | bytes 1048608 | tf_op jit(solution)/shard_map/ppermute | solution.py:126
  733.4 12.5 %fusion.140 = (bf16[1024,2048]{1,0:T(8,128)(2,1)}, f32[1024,2048]{1,0:T(8,128)}) fusion(bf16[1024,2048]{1,0:T(8,128)(2,1)} %collective-permute-done.34, bf16[2048,1536]{1,0:T(8,128)(2,1)S(1)} %bitcast.264, s32[]{:T(128)S(6)} %select_n.686, bf16[1024,1536]{1,0:T(8,128)(2,1)} %constant_dynamic-update-slice_fusion, bf16[1024,1536]{1,0:T(8,128)(2,1)} %copy-done.75), kind=kOutput, calls=%fused_computation.384 | convolution fusion | flops 6455033856 | bytes 29360132 | tf_op jit(solution)/shard_map/dot_general | solution.py:19
  753.2 4.9 collective-permute-start.48
  762.6 16.1 %collective-permute-done.59 = bf16[2,256,1536]{2,1,0:T(8,128)(2,1)S(1)} collective-permute-done((bf16[2,256,1536]{2,1,0:T(8,128)(2,1)}, bf16[2,256,1536]{2,1,0:T(8,128)(2,1)S(1)}, u32[]{:S(2)}, u32[]{:S(2)}) %collective-permute-start.59) | collective-permute-done | bytes 1572896 | tf_op jit(solution)/shard_map/ppermute | solution.py:24
  785.1 4.6 collective-permute-start.50
  791.4 4.4 convert_add_fusion.11
  802.0 4.5 collective-permute-done.51
  812.1 4.9 add_convert_fusion.3
  (665 shorter events, 355.8 us)
Async XLA Ops:
  7.2 101.9 %all-gather.3.cloned.1.call-start = ((), (), s32[]{:S(2)}) async-start(), calls=%async_computation.2 | async-start | bytes 5242880 | tf_op jit(solution)/shard_map/all_gather | solution.py:515
  51.5 35.9 %collective-permute-start.3 = (bf16[2,256,1536]{2,1,0:T(8,128)(2,1)}, bf16[2,256,1536]{2,1,0:T(8,128)(2,1)}, u32[]{:S(2)}, u32[]{:S(2)}) collective-permute-start(bf16[2,256,1536]{2,1,0:T(8,128)(2,1)} %pad_maximum_fusion.24), channel_id=1, source_target_pairs={{0,8},{4,12},{8,0},{12,4},{16,24},{20,28},{24,16},{28,20},{1,9},{5... | collective-permute-start | bytes 4718600 | tf_op jit(solution)/shard_map/ppermute | solution.py:24
  52.1 35.8 %collective-permute-start.4 = (bf16[2,256,1536]{2,1,0:T(8,128)(2,1)}, bf16[2,256,1536]{2,1,0:T(8,128)(2,1)}, u32[]{:S(2)}, u32[]{:S(2)}) collective-permute-start(bf16[2,256,1536]{2,1,0:T(8,128)(2,1)} %pad_maximum_fusion.26), channel_id=1, source_target_pairs={{0,16},{4,20},{8,24},{12,28},{16,0},{20,4},{24,8},{28,12},{1,17},{... | collective-permute-start | bytes 4718600 | tf_op jit(solution)/shard_map/ppermute | solution.py:24
  87.9 46.1 %collective-permute-start.7 = (bf16[2,256,2048]{2,1,0:T(8,128)(2,1)}, bf16[2,256,2048]{2,1,0:T(8,128)(2,1)}, u32[]{:S(2)}, u32[]{:S(2)}) collective-permute-start(bf16[2,256,2048]{2,1,0:T(8,128)(2,1)} %pad_maximum_fusion.12), channel_id=1, source_target_pairs={{0,8},{4,12},{8,0},{12,4},{16,24},{20,28},{24,16},{28,20},{1,9},{5... | collective-permute-start | bytes 6291464 | tf_op jit(solution)/shard_map/ppermute | solution.py:24
  89.2 45.7 %collective-permute-start.8 = (bf16[512,2048]{1,0:T(8,128)(2,1)}, bf16[512,2048]{1,0:T(8,128)(2,1)}, u32[]{:S(2)}, u32[]{:S(2)}) collective-permute-start(bf16[512,2048]{1,0:T(8,128)(2,1)} %param.33), channel_id=1, source_target_pairs={{0,16},{4,20},{8,24},{12,28},{16,0},{20,4},{24,8},{28,12},{1,17},{... | collective-permute-start | bytes 6291464 | tf_op jit(solution)/shard_map/ppermute | solution.py:24
  109.1 33.5 %collective-permute-start.5 = (bf16[1024,2048]{1,0:T(8,128)(2,1)}, bf16[1024,2048]{1,0:T(8,128)(2,1)S(1)}, u32[]{:S(2)}, u32[]{:S(2)}) collective-permute-start(bf16[1024,2048]{1,0:T(8,128)(2,1)} %all-gather.3.cloned.1.call-done), channel_id=1, source_target_pairs={{0,4},{4,0},{8,12},{12,8},{16,20},{20,16},{24,28},{28,24},{1,5},{5... | collective-permute-start | bytes 12582920 | tf_op jit(solution)/shard_map/ppermute | solution.py:24
  165.5 26.0 %collective-permute-start.9 = (bf16[256,2048]{1,0:T(8,128)(2,1)S(1)}, bf16[256,2048]{1,0:T(8,128)(2,1)S(1)}, u32[]{:S(2)}, u32[]{:S(2)}) collective-permute-start(bf16[256,2048]{1,0:T(8,128)(2,1)S(1)} %copy-done.110), channel_id=1, source_target_pairs={{0,8},{4,12},{8,0},{12,4},{16,24},{20,28},{24,16},{28,20},{1,9},{5... | collective-permute-start | bytes 3145736 | tf_op jit(solution)/shard_map/ppermute | solution.py:24
  166.5 57.4 %collective-permute-start.10 = (bf16[256,2048]{1,0:T(8,128)(2,1)S(1)}, bf16[256,2048]{1,0:T(8,128)(2,1)S(1)}, u32[]{:S(2)}, u32[]{:S(2)}) collective-permute-start(bf16[256,2048]{1,0:T(8,128)(2,1)S(1)} %copy-done.109), channel_id=1, source_target_pairs={{0,16},{4,20},{8,24},{12,28},{16,0},{20,4},{24,8},{28,12},{1,17},{... | collective-permute-start | bytes 3145736 | tf_op jit(solution)/shard_map/ppermute | solution.py:24
  175.7 61.7 %collective-permute-start.6 = (bf16[1024,768]{1,0:T(8,128)(2,1)}, bf16[1024,768]{1,0:T(8,128)(2,1)}, u32[]{:S(2)}, u32[]{:S(2)}) collective-permute-start(bf16[1024,768]{1,0:T(8,128)(2,1)} %pad_maximum_fusion.27), channel_id=1, source_target_pairs={{0,8},{4,12},{8,16},{12,20},{16,24},{20,28},{1,9},{5,13},{9,17},{1... | collective-permute-start | bytes 4718600 | tf_op jit(solution)/shard_map/ppermute | solution.py:29
  227.1 42.9 %collective-permute-start.12 = (bf16[2,256,2048]{2,1,0:T(8,128)(2,1)}, bf16[2,256,2048]{2,1,0:T(8,128)(2,1)}, u32[]{:S(2)}, u32[]{:S(2)}) collective-permute-start(bf16[2,256,2048]{2,1,0:T(8,128)(2,1)} %pad_maximum_fusion.9), channel_id=1, source_target_pairs={{0,8},{4,12},{8,0},{12,4},{16,24},{20,28},{24,16},{28,20},{1,9},{5... | collective-permute-start | bytes 6291464 | tf_op jit(solution)/shard_map/ppermute | solution.py:24
  234.5 38.7 %collective-permute-start.13 = (bf16[2,256,2048]{2,1,0:T(8,128)(2,1)}, bf16[2,256,2048]{2,1,0:T(8,128)(2,1)}, u32[]{:S(2)}, u32[]{:S(2)}) collective-permute-start(bf16[2,256,2048]{2,1,0:T(8,128)(2,1)} %pad_maximum_fusion.6), channel_id=1, source_target_pairs={{0,16},{4,20},{8,24},{12,28},{16,0},{20,4},{24,8},{28,12},{1,17},{... | collective-permute-start | bytes 6291464 | tf_op jit(solution)/shard_map/ppermute | solution.py:24
  248.8 39.2 %all-to-all-start = ((bf16[4,512,512]{2,1,0:T(8,128)(2,1)}), bf16[4,512,512]{2,1,0:T(8,128)(2,1)}, u32[]{:S(2)}, u32[]{:S(2)}) async-start(bf16[4,512,512]{2,1,0:T(8,128)(2,1)} %pad_maximum_fusion.10), calls=%async_computation | async-start | bytes 4194304 | tf_op jit(solution)/shard_map/all_to_all | solution.py:648
  309.4 49.2 %collective-permute-start.17 = (bf16[4,256,1024]{2,1,0:T(8,128)(2,1)S(1)}, bf16[4,256,1024]{2,1,0:T(8,128)(2,1)S(1)}, u32[]{:S(2)}, u32[]{:S(2)}) collective-permute-start(bf16[4,256,1024]{2,1,0:T(8,128)(2,1)S(1)} %copy-done.94), channel_id=1, source_target_pairs={{0,16},{4,20},{8,24},{12,28},{16,0},{20,4},{24,8},{28,12},{1,17},{... | collective-permute-start | bytes 6291464 | tf_op jit(solution)/shard_map/ppermute | solution.py:24
  316.0 43.5 %collective-permute-start.19 = (bf16[256,2048]{1,0:T(8,128)(2,1)S(1)}, bf16[256,2048]{1,0:T(8,128)(2,1)S(1)}, u32[]{:S(2)}, u32[]{:S(2)}) collective-permute-start(bf16[256,2048]{1,0:T(8,128)(2,1)S(1)} %add_convert_fusion.22), channel_id=1, source_target_pairs={{0,8},{4,12},{8,0},{12,4},{16,24},{20,28},{24,16},{28,20},{1,9},{5... | collective-permute-start | bytes 3145736 | tf_op jit(solution)/shard_map/ppermute | solution.py:24
  321.5 40.5 %collective-permute-start.15 = (bf16[256,2048]{1,0:T(8,128)(2,1)S(1)}, bf16[256,2048]{1,0:T(8,128)(2,1)S(1)}, u32[]{:S(2)}, u32[]{:S(2)}) collective-permute-start(bf16[256,2048]{1,0:T(8,128)(2,1)S(1)} %add_convert_fusion.22), channel_id=1, source_target_pairs={{0,4},{4,0},{8,12},{12,8},{16,20},{20,16},{24,28},{28,24},{1,5},{5... | collective-permute-start | bytes 3145736 | tf_op jit(solution)/shard_map/ppermute | solution.py:24
  359.4 22.9 %collective-permute-start.20 = (bf16[256,2048]{1,0:T(8,128)(2,1)S(1)}, bf16[256,2048]{1,0:T(8,128)(2,1)S(1)}, u32[]{:S(2)}, u32[]{:S(2)}) collective-permute-start(bf16[256,2048]{1,0:T(8,128)(2,1)S(1)} %collective-permute-done.19), channel_id=1, source_target_pairs={{0,4},{4,0},{8,12},{12,8},{16,20},{20,16},{24,28},{28,24},{1,5},{5... | collective-permute-start | bytes 3145736 | tf_op jit(solution)/shard_map/ppermute | solution.py:24
  381.9 31.4 %collective-permute-start.23 = (bf16[256,2048]{1,0:T(8,128)(2,1)}, bf16[256,2048]{1,0:T(8,128)(2,1)}, u32[]{:S(2)}, u32[]{:S(2)}) collective-permute-start(bf16[256,2048]{1,0:T(8,128)(2,1)} %slice.450), channel_id=1, source_target_pairs={{0,4},{4,0},{8,12},{12,8},{16,20},{20,16},{24,28},{28,24},{1,5},{5... | collective-permute-start | bytes 3145736 | tf_op jit(solution)/shard_map/ppermute | solution.py:24
  412.1 25.3 %collective-permute-start.25 = (bf16[256,2048]{1,0:T(8,128)(2,1)S(1)}, bf16[256,2048]{1,0:T(8,128)(2,1)S(1)}, u32[]{:S(2)}, u32[]{:S(2)}) collective-permute-start(bf16[256,2048]{1,0:T(8,128)(2,1)S(1)} %add_convert_fusion.20), channel_id=1, source_target_pairs={{0,8},{4,12},{8,0},{12,4},{16,24},{20,28},{24,16},{28,20},{1,9},{5... | collective-permute-start | bytes 3145736 | tf_op jit(solution)/shard_map/ppermute | solution.py:24
  450.6 45.3 %collective-permute-start.22 = (bf16[256,2048]{1,0:T(8,128)(2,1)}, bf16[256,2048]{1,0:T(8,128)(2,1)}, u32[]{:S(2)}, u32[]{:S(2)}) collective-permute-start(bf16[256,2048]{1,0:T(8,128)(2,1)} %slice.448), channel_id=1, source_target_pairs={{0,4},{4,0},{8,12},{12,8},{16,20},{20,16},{24,28},{28,24},{1,5},{5... | collective-permute-start | bytes 3145736 | tf_op jit(solution)/shard_map/ppermute | solution.py:24
  451.0 48.8 %collective-permute-start.35 = (bf16[512,2048]{1,0:T(8,128)(2,1)}, bf16[512,2048]{1,0:T(8,128)(2,1)}, u32[]{:S(2)}, u32[]{:S(2)}) collective-permute-start(bf16[512,2048]{1,0:T(8,128)(2,1)} %dynamic-slice_bitcast_fusion), channel_id=1, source_target_pairs={{0,16},{4,20},{8,24},{12,28},{16,0},{20,4},{24,8},{28,12},{1,17},{... | collective-permute-start | bytes 6291464 | tf_op jit(solution)/shard_map/ppermute | solution.py:24
  472.6 77.2 %all-to-all-start.1 = ((bf16[4,512,512]{2,1,0:T(8,128)(2,1)}), bf16[4,512,512]{2,1,0:T(8,128)(2,1)}, u32[]{:S(2)}, u32[]{:S(2)}) async-start(bf16[4,512,512]{2,1,0:T(8,128)(2,1)} %pad_maximum_fusion.21), calls=%async_computation.1 | async-start | bytes 4194304 | tf_op jit(solution)/shard_map/all_to_all | solution.py:648
  486.6 47.7 %collective-permute-start.27 = (bf16[2,256,2048]{2,1,0:T(8,128)(2,1)}, bf16[2,256,2048]{2,1,0:T(8,128)(2,1)}, u32[]{:S(2)}, u32[]{:S(2)}) collective-permute-start(bf16[2,256,2048]{2,1,0:T(8,128)(2,1)} %pad_maximum_fusion.19), channel_id=1, source_target_pairs={{0,8},{4,12},{8,0},{12,4},{16,24},{20,28},{24,16},{28,20},{1,9},{5... | collective-permute-start | bytes 6291464 | tf_op jit(solution)/shard_map/ppermute | solution.py:24
  487.3 56.6 %collective-permute-start.28 = (bf16[2,256,2048]{2,1,0:T(8,128)(2,1)}, bf16[2,256,2048]{2,1,0:T(8,128)(2,1)}, u32[]{:S(2)}, u32[]{:S(2)}) collective-permute-start(bf16[2,256,2048]{2,1,0:T(8,128)(2,1)} %pad_maximum_fusion.20), channel_id=1, source_target_pairs={{0,16},{4,20},{8,24},{12,28},{16,0},{20,4},{24,8},{28,12},{1,17},{... | collective-permute-start | bytes 6291464 | tf_op jit(solution)/shard_map/ppermute | solution.py:24
  552.9 45.5 %collective-permute-start.29 = (bf16[256,2048]{1,0:T(8,128)(2,1)}, bf16[256,2048]{1,0:T(8,128)(2,1)}, u32[]{:S(2)}, u32[]{:S(2)}) collective-permute-start(bf16[256,2048]{1,0:T(8,128)(2,1)} %fusion.60), channel_id=1, source_target_pairs={{0,8},{4,12},{8,0},{12,4},{16,24},{20,28},{24,16},{28,20},{1,9},{5... | collective-permute-start | bytes 3145736 | tf_op jit(solution)/shard_map/ppermute | solution.py:24
  554.1 44.4 %collective-permute-start.30 = (bf16[256,2048]{1,0:T(8,128)(2,1)}, bf16[256,2048]{1,0:T(8,128)(2,1)}, u32[]{:S(2)}, u32[]{:S(2)}) collective-permute-start(bf16[256,2048]{1,0:T(8,128)(2,1)} %fusion.59), channel_id=1, source_target_pairs={{0,16},{4,20},{8,24},{12,28},{16,0},{20,4},{24,8},{28,12},{1,17},{... | collective-permute-start | bytes 3145736 | tf_op jit(solution)/shard_map/ppermute | solution.py:24
  556.9 45.7 %collective-permute-start.36 = (bf16[256,2048]{1,0:T(8,128)(2,1)}, bf16[256,2048]{1,0:T(8,128)(2,1)}, u32[]{:S(2)}, u32[]{:S(2)}) collective-permute-start(bf16[256,2048]{1,0:T(8,128)(2,1)} %get-tuple-element.186), channel_id=1, source_target_pairs={{0,1},{4,5},{8,9},{12,13},{16,17},{20,21},{24,25},{28,29}} | collective-permute-start | bytes 3145736 | tf_op jit(solution)/shard_map/ppermute | solution.py:126
  559.1 43.4 %collective-permute-start.37 = (bf16[256,2048]{1,0:T(8,128)(2,1)}, bf16[256,2048]{1,0:T(8,128)(2,1)}, u32[]{:S(2)}, u32[]{:S(2)}) collective-permute-start(bf16[256,2048]{1,0:T(8,128)(2,1)} %get-tuple-element.186), channel_id=1, source_target_pairs={{3,2},{7,6},{11,10},{15,14},{19,18},{23,22},{27,26},{31,30}} | collective-permute-start | bytes 3145736 | tf_op jit(solution)/shard_map/ppermute | solution.py:126
  577.7 39.5 %collective-permute-start.33 = (bf16[1024,768]{1,0:T(8,128)(2,1)}, bf16[1024,768]{1,0:T(8,128)(2,1)}, u32[]{:S(2)}, u32[]{:S(2)}) collective-permute-start(bf16[1024,768]{1,0:T(8,128)(2,1)} %convert_element_type.538), channel_id=1, source_target_pairs={{8,0},{12,4},{16,8},{20,12},{24,16},{28,20},{9,1},{13,5},{17,9},{2... | collective-permute-start | bytes 4718600 | tf_op jit(solution)/shard_map/ppermute | solution.py:29
  607.1 76.1 %collective-permute-start.31 = (bf16[256,2048]{1,0:T(8,128)(2,1)}, bf16[256,2048]{1,0:T(8,128)(2,1)}, u32[]{:S(2)}, u32[]{:S(2)}) collective-permute-start(bf16[256,2048]{1,0:T(8,128)(2,1)} %add_convert_fusion.21), channel_id=1, source_target_pairs={{0,8},{4,12},{8,0},{12,4},{16,24},{20,28},{24,16},{28,20},{1,9},{5... | collective-permute-start | bytes 3145736 | tf_op jit(solution)/shard_map/ppermute | solution.py:24
  609.8 34.7 %collective-permute-start.38 = (bf16[256,2048]{1,0:T(8,128)(2,1)}, bf16[256,2048]{1,0:T(8,128)(2,1)}, u32[]{:S(2)}, u32[]{:S(2)}) collective-permute-start(bf16[256,2048]{1,0:T(8,128)(2,1)} %get-tuple-element.188), channel_id=1, source_target_pairs={{0,1},{1,2},{4,5},{5,6},{8,9},{9,10},{12,13},{13,14},{16,17},{17,1... | collective-permute-start | bytes 3145736 | tf_op jit(solution)/shard_map/ppermute | solution.py:126
  612.0 32.5 %collective-permute-start.39 = (bf16[256,2048]{1,0:T(8,128)(2,1)}, bf16[256,2048]{1,0:T(8,128)(2,1)}, u32[]{:S(2)}, u32[]{:S(2)}) collective-permute-start(bf16[256,2048]{1,0:T(8,128)(2,1)} %get-tuple-element.189), channel_id=1, source_target_pairs={{3,2},{2,1},{7,6},{6,5},{11,10},{10,9},{15,14},{14,13},{19,18},{18... | collective-permute-start | bytes 3145736 | tf_op jit(solution)/shard_map/ppermute | solution.py:126
  614.1 69.2 %collective-permute-start.32 = (bf16[4,256,1024]{2,1,0:T(8,128)(2,1)}, bf16[4,256,1024]{2,1,0:T(8,128)(2,1)}, u32[]{:S(2)}, u32[]{:S(2)}) collective-permute-start(bf16[4,256,1024]{2,1,0:T(8,128)(2,1)} %dynamic-slice_bitcast_fusion.1), channel_id=1, source_target_pairs={{0,16},{4,20},{8,24},{12,28},{16,0},{20,4},{24,8},{28,12},{1,17},{... | collective-permute-start | bytes 6291464 | tf_op jit(solution)/shard_map/ppermute | solution.py:24
  647.6 21.1 %collective-permute-start.40 = (bf16[256,2048]{1,0:T(8,128)(2,1)S(1)}, bf16[256,2048]{1,0:T(8,128)(2,1)S(1)}, u32[]{:S(2)}, u32[]{:S(2)}) collective-permute-start(bf16[256,2048]{1,0:T(8,128)(2,1)S(1)} %get-tuple-element.190), channel_id=1, source_target_pairs={{0,1},{1,2},{2,3},{4,5},{5,6},{6,7},{8,9},{9,10},{10,11},{12,13},{... | collective-permute-start | bytes 3145736 | tf_op jit(solution)/shard_map/ppermute | solution.py:126
  649.3 23.8 %collective-permute-start.41 = (bf16[256,2048]{1,0:T(8,128)(2,1)S(1)}, bf16[256,2048]{1,0:T(8,128)(2,1)S(1)}, u32[]{:S(2)}, u32[]{:S(2)}) collective-permute-start(bf16[256,2048]{1,0:T(8,128)(2,1)S(1)} %get-tuple-element.191), channel_id=1, source_target_pairs={{3,2},{2,1},{1,0},{7,6},{6,5},{5,4},{11,10},{10,9},{9,8},{15,14},{... | collective-permute-start | bytes 3145736 | tf_op jit(solution)/shard_map/ppermute | solution.py:126
  661.6 71.8 %collective-permute-start.34 = (bf16[1024,2048]{1,0:T(8,128)(2,1)}, bf16[1024,2048]{1,0:T(8,128)(2,1)}, u32[]{:S(2)}, u32[]{:S(2)}) collective-permute-start(bf16[1024,2048]{1,0:T(8,128)(2,1)} %convolution_convert_fusion.2), channel_id=1, source_target_pairs={{0,4},{4,0},{8,12},{12,8},{16,20},{20,16},{24,28},{28,24},{1,5},{5... | collective-permute-start | bytes 12582920 | tf_op jit(solution)/shard_map/ppermute | solution.py:24
  675.5 21.4 %collective-permute-start.42 = (bf16[256,2048]{1,0:T(8,128)(2,1)}, bf16[256,2048]{1,0:T(8,128)(2,1)}, u32[]{:S(2)}, u32[]{:S(2)}) collective-permute-start(bf16[256,2048]{1,0:T(8,128)(2,1)} %get-tuple-element.192), channel_id=1, source_target_pairs={{0,1},{1,2},{2,3},{4,5},{5,6},{6,7},{8,9},{9,10},{10,11},{12,13},{... | collective-permute-start | bytes 3145736 | tf_op jit(solution)/shard_map/ppermute | solution.py:126
  679.4 22.6 %collective-permute-start.43 = (bf16[256,2048]{1,0:T(8,128)(2,1)}, bf16[256,2048]{1,0:T(8,128)(2,1)}, u32[]{:S(2)}, u32[]{:S(2)}) collective-permute-start(bf16[256,2048]{1,0:T(8,128)(2,1)} %get-tuple-element.193), channel_id=1, source_target_pairs={{3,2},{2,1},{1,0},{7,6},{6,5},{5,4},{11,10},{10,9},{9,8},{15,14},{... | collective-permute-start | bytes 3145736 | tf_op jit(solution)/shard_map/ppermute | solution.py:126
  683.3 76.2 %collective-permute-start.18 = (bf16[256,2048]{1,0:T(8,128)(2,1)}, bf16[256,2048]{1,0:T(8,128)(2,1)}, u32[]{:S(2)}, u32[]{:S(2)}) collective-permute-start(bf16[256,2048]{1,0:T(8,128)(2,1)} %slice.445), channel_id=1, source_target_pairs={{0,4},{4,0},{8,12},{12,8},{16,20},{20,16},{24,28},{28,24},{1,5},{5... | collective-permute-start | bytes 3145736 | tf_op jit(solution)/shard_map/ppermute | solution.py:24
  707.4 20.8 %collective-permute-start.45 = (bf16[256,2048]{1,0:T(8,128)(2,1)S(1)}, bf16[256,2048]{1,0:T(8,128)(2,1)S(1)}, u32[]{:S(2)}, u32[]{:S(2)}) collective-permute-start(bf16[256,2048]{1,0:T(8,128)(2,1)S(1)} %get-tuple-element.195), channel_id=1, source_target_pairs={{3,2},{2,1},{1,0},{7,6},{6,5},{5,4},{11,10},{10,9},{9,8},{15,14},{... | collective-permute-start | bytes 3145736 | tf_op jit(solution)/shard_map/ppermute | solution.py:126
  729.4 22.5 %collective-permute-start.46 = (bf16[256,2048]{1,0:T(8,128)(2,1)S(1)}, bf16[256,2048]{1,0:T(8,128)(2,1)S(1)}, u32[]{:S(2)}, u32[]{:S(2)}) collective-permute-start(bf16[256,2048]{1,0:T(8,128)(2,1)S(1)} %get-tuple-element.196), channel_id=1, source_target_pairs={{0,1},{1,2},{2,3},{4,5},{5,6},{6,7},{8,9},{9,10},{10,11},{12,13},{... | collective-permute-start | bytes 3145736 | tf_op jit(solution)/shard_map/ppermute | solution.py:126
  745.9 32.7 %collective-permute-start.59 = (bf16[2,256,1536]{2,1,0:T(8,128)(2,1)}, bf16[2,256,1536]{2,1,0:T(8,128)(2,1)S(1)}, u32[]{:S(2)}, u32[]{:S(2)}) collective-permute-start(bf16[2,256,1536]{2,1,0:T(8,128)(2,1)} %pad_maximum_fusion.28), channel_id=1, source_target_pairs={{0,8},{4,12},{8,0},{12,4},{16,24},{20,28},{24,16},{28,20},{1,9},{5... | collective-permute-start | bytes 4718600 | tf_op jit(solution)/shard_map/ppermute | solution.py:24
  748.3 32.7 %collective-permute-start.60 = (bf16[2,256,1536]{2,1,0:T(8,128)(2,1)}, bf16[2,256,1536]{2,1,0:T(8,128)(2,1)S(1)}, u32[]{:S(2)}, u32[]{:S(2)}) collective-permute-start(bf16[2,256,1536]{2,1,0:T(8,128)(2,1)} %pad_maximum_fusion.29), channel_id=1, source_target_pairs={{0,16},{4,20},{8,24},{12,28},{16,0},{20,4},{24,8},{28,12},{1,17},{... | collective-permute-start | bytes 4718600 | tf_op jit(solution)/shard_map/ppermute | solution.py:24
  753.2 30.3 %collective-permute-start.48 = (bf16[256,2048]{1,0:T(8,128)(2,1)S(1)}, bf16[256,2048]{1,0:T(8,128)(2,1)S(1)}, u32[]{:S(2)}, u32[]{:S(2)}) collective-permute-start(bf16[256,2048]{1,0:T(8,128)(2,1)S(1)} %get-tuple-element.199), channel_id=1, source_target_pairs={{0,1},{1,2},{2,3},{4,5},{5,6},{6,7},{8,9},{9,10},{10,11},{12,13},{... | collective-permute-start | bytes 3145736 | tf_op jit(solution)/shard_map/ppermute | solution.py:126
  758.1 25.4 %collective-permute-start.49 = (bf16[256,2048]{1,0:T(8,128)(2,1)S(1)}, bf16[256,2048]{1,0:T(8,128)(2,1)S(1)}, u32[]{:S(2)}, u32[]{:S(2)}) collective-permute-start(bf16[256,2048]{1,0:T(8,128)(2,1)S(1)} %get-tuple-element.200), channel_id=1, source_target_pairs={{3,2},{2,1},{1,0},{7,6},{6,5},{5,4},{11,10},{10,9},{9,8},{15,14},{... | collective-permute-start | bytes 3145736 | tf_op jit(solution)/shard_map/ppermute | solution.py:126
  799.7 32.2 %collective-permute-start.63 = (bf16[256,1536]{1,0:T(8,128)(2,1)}, bf16[256,1536]{1,0:T(8,128)(2,1)}, u32[]{:S(2)}, u32[]{:S(2)}) collective-permute-start(bf16[256,1536]{1,0:T(8,128)(2,1)} %select_convert_fusion), channel_id=1, source_target_pairs={{0,4},{4,0},{8,12},{12,8},{16,20},{20,16},{24,28},{28,24},{1,5},{5... | collective-permute-start | bytes 2359304 | tf_op jit(solution)/shard_map/ppermute | solution.py:24
  819.4 22.8 %collective-permute-start.52 = (bf16[256,2048]{1,0:T(8,128)(2,1)}, bf16[256,2048]{1,0:T(8,128)(2,1)S(1)}, u32[]{:S(2)}, u32[]{:S(2)}) collective-permute-start(bf16[256,2048]{1,0:T(8,128)(2,1)} %get-tuple-element.203), channel_id=1, source_target_pairs={{0,1},{1,2},{2,3},{4,5},{5,6},{6,7},{8,9},{9,10},{10,11},{12,13},{... | collective-permute-start | bytes 3145736 | tf_op jit(solution)/shard_map/ppermute | solution.py:126
  822.9 23.4 %collective-permute-start.53 = (bf16[256,2048]{1,0:T(8,128)(2,1)}, bf16[256,2048]{1,0:T(8,128)(2,1)S(1)}, u32[]{:S(2)}, u32[]{:S(2)}) collective-permute-start(bf16[256,2048]{1,0:T(8,128)(2,1)} %get-tuple-element.204), channel_id=1, source_target_pairs={{3,2},{2,1},{1,0},{7,6},{6,5},{5,4},{11,10},{10,9},{9,8},{15,14},{... | collective-permute-start | bytes 3145736 | tf_op jit(solution)/shard_map/ppermute | solution.py:126
  827.5 36.4 %collective-permute-start.64 = (bf16[2,256,1024]{2,1,0:T(8,128)(2,1)}, bf16[2,256,1024]{2,1,0:T(8,128)(2,1)S(1)}, u32[]{:S(2)}, u32[]{:S(2)}) collective-permute-start(bf16[2,256,1024]{2,1,0:T(8,128)(2,1)} %pad_maximum_fusion.36), channel_id=1, source_target_pairs={{0,8},{4,12},{8,0},{12,4},{16,24},{20,28},{24,16},{28,20},{1,9},{5... | collective-permute-start | bytes 3145736 | tf_op jit(solution)/shard_map/ppermute | solution.py:24
  (175 other events, 1758.9 us)
Sparse Core Ops, SparseCore 0:
  28.0 81.0 all-gather.2

commit v4 on v3

--- a/solution.py
+++ b/solution.py
@@ -333,7 +333,7 @@
 
 
 def retention(place, starts, decay, queries, keys, values, gate, gain, bias, rows, low, high):
-    cost = pl.CostEstimate(flops=rows * 1280 * 192, bytes_accessed=rows * 1024, transcendentals=0)
+    cost = pl.CostEstimate(flops=rows * 1966080, bytes_accessed=rows * 8192, transcendentals=0)
     return pl.pallas_call(
         retention_kernel,
         out_shape=(
@@ -352,7 +352,7 @@
 def retention_back(
     place, starts, decay, queries, keys, values, gate, gain, bias, hat, scale, grad, rows, low, high
 ):
-    cost = pl.CostEstimate(flops=rows * 1280 * 448, bytes_accessed=rows * 2048, transcendentals=0)
+    cost = pl.CostEstimate(flops=rows * 4587520, bytes_accessed=rows * 16384, transcendentals=0)
     part = pl.BlockSpec((rows, VD), lambda _: (high[1], 0))
     return pl.pallas_call(
         retention_back_kernel,
@@ -419,7 +419,7 @@
         return pl.BlockSpec((TILE, columns), lambda i: (i, 0))
 
     cost = pl.CostEstimate(
-        flops=rows * width * hidden, bytes_accessed=rows * width, transcendentals=0
+        flops=rows * width * hidden * 8, bytes_accessed=rows * width * 8, transcendentals=0
     )
     return pl.pallas_call(
         feed_kernel,

time: 896 us -> 887 us (0.990)
  waiting for transfers between devices: 322 us -> 289 us
  starting transfers between devices: 95.1 us -> 121 us
    ppermute x44, waiting for transfers between devices: 240 us -> 206 us  [flip(): return lax.ppermute(block, 'seq', [(i, i ^ bit) for i in range(devices)])]
    ppermute x44, starting transfers between devices: 38.1 us -> 65.9 us  [flip(): return lax.ppermute(block, 'seq', [(i, i ^ bit) for i in range(devices)])]
    unnamed x334 -> x350, local copies, waits for them, and re-layouts: 31 us -> 27.1 us
  transfers between devices with their start and end apart: 69 -> 69, of which waited for: 35 -> 33; matrix products, arithmetic and copies ran while one was open for 34% -> 35% of each run, Pallas kernels for 7% -> 7%
where the time goes in v4:
time: 887 us; the launch traced here: 879 us
  waiting for transfers between devices  289 us (33%)
  other arithmetic  168 us (19%)
  starting transfers between devices  121 us (14%)
  local copies, waits for them, and re-layouts  108 us (12%)
  matrix products  99.2 us (11%)
  Pallas kernels  64.7 us (7%)
  between operations  17.9 us (2%)
  blocking collectives  10.4 us (1%)
    ppermute x44, waiting for transfers between devices, flip(): return lax.ppermute(block, 'seq', [(i, i ^ bit) for i in range(devices)])  206 us
    dot_general x12, matrix products, dot(): return lax.dot_general(a, b, (dims, ((), ())), preferred_element_type=F32)  99.2 us
    ppermute x44, starting transfers between devices, flip(): return lax.ppermute(block, 'seq', [(i, i ^ bit) for i in range(devices)])  65.9 us
    ppermute x18, waiting for transfers between devices, step(): self.came[way].append(lax.ppermute(block, 'grp', pairs))  49.9 us
    ppermute x18, starting transfers between devices, step(): self.came[way].append(lax.ppermute(block, 'grp', pairs))  39.7 us
    pallas_call x2, Pallas kernels, feed(): pl.pallas_call(feed_kernel, out_shape=(jax.ShapeDtypeStruct((rows, hidden...  28.7 us
    unnamed x350, local copies, waits for them, and re-layouts  27.1 us
    pallas_call x2, Pallas kernels, retention_back(): pl.pallas_call(retention_back_kernel, out_shape=(jax.ShapeDtypeStruct((ro...  24.7 us
  transfers between devices with their start and end apart: 69, of which 33 were waited for; matrix products, arithmetic and copies ran while one was open for 35% of the time, Pallas kernels for 7%

profile of v4, /device:TPU:0, one launch (start us, length us, event | category | flops | bytes accessed | tf_op | source)
XLA Modules:
  0.0 879.3 jit_solution(2829678216561741117)
XLA Ops:
  16.1 10.4 %all-gather = bf16[8,1,2048]{2,1,0:T(2,128)(2,1)S(1)} all-gather(bf16[1,1,2048]{2,1,0:T(2,128)(2,1)S(1)} %bitcast.301), channel_id=1, replica_groups=mesh['seq'=8,'grp'=4] {'seq'}, dimensions={0}, use_global_device_ids=true | all-gather | bytes 36864 | tf_op jit(solution)/shard_map/all_gather | solution.py:500
  31.1 16.9 %collective-permute-done.1 = bf16[256,1536]{1,0:T(8,128)(2,1)} collective-permute-done((bf16[256,1536]{1,0:T(8,128)(2,1)S(1)}, bf16[256,1536]{1,0:T(8,128)(2,1)}, u32[]{:S(2)}, u32[]{:S(2)}) %collective-permute-start.1) | collective-permute-done | bytes 786464 | tf_op jit(solution)/shard_map/ppermute | solution.py:24
  61.9 27.2 %collective-permute-done.3 = bf16[2,256,1536]{2,1,0:T(8,128)(2,1)} collective-permute-done((bf16[2,256,1536]{2,1,0:T(8,128)(2,1)}, bf16[2,256,1536]{2,1,0:T(8,128)(2,1)}, u32[]{:S(2)}, u32[]{:S(2)}) %collective-permute-start.3) | collective-permute-done | bytes 1572896 | tf_op jit(solution)/shard_map/ppermute | solution.py:24
  91.5 5.7 multiply_sine_fusion
  97.2 12.1 %all-gather.3.cloned.1.call-done = bf16[1024,2048]{1,0:T(8,128)(2,1)} async-done(((bf16[256,2048]{1,0:T(8,128)(2,1)}), bf16[1024,2048]{1,0:T(8,128)(2,1)}) %all-gather.3.cloned.1.call-update) | async-done | bytes 4194320 | tf_op jit(solution)/shard_map/all_gather | solution.py:515
  117.4 18.1 %collective-permute-done.7 = bf16[2,256,2048]{2,1,0:T(8,128)(2,1)} collective-permute-done((bf16[2,256,2048]{2,1,0:T(8,128)(2,1)}, bf16[2,256,2048]{2,1,0:T(8,128)(2,1)}, u32[]{:S(2)}, u32[]{:S(2)}) %collective-permute-start.7) | collective-permute-done | bytes 2097184 | tf_op jit(solution)/shard_map/ppermute | solution.py:24
  147.5 7.6 convolution_convert_fusion.4.gate_ref
  155.1 6.8 convolution_convert_fusion.5.value_high_ref.value_low_ref
  168.8 5.6 fusion.84
  176.9 4.3 collective-permute-start.6
  183.9 8.9 %collective-permute-done.9 = bf16[256,2048]{1,0:T(8,128)(2,1)S(1)} collective-permute-done((bf16[256,2048]{1,0:T(8,128)(2,1)S(1)}, bf16[256,2048]{1,0:T(8,128)(2,1)S(1)}, u32[]{:S(2)}, u32[]{:S(2)}) %collective-permute-start.9) | collective-permute-done | bytes 1048608 | tf_op jit(solution)/shard_map/ppermute | solution.py:24
  197.7 5.6 shard_map.315
  204.2 33.7 %collective-permute-start.13 = (bf16[2,256,2048]{2,1,0:T(8,128)(2,1)}, bf16[2,256,2048]{2,1,0:T(8,128)(2,1)}, u32[]{:S(2)}, u32[]{:S(2)}) collective-permute-start(bf16[2,256,2048]{2,1,0:T(8,128)(2,1)} %pad_maximum_fusion.6), channel_id=1, source_target_pairs={{0,16},{4,20},{8,24},{12,28},{16,0},{20,4},{24,8},{28,12},{1,17},{... | collective-permute-start | bytes 6291464 | tf_op jit(solution)/shard_map/ppermute | solution.py:24
  241.5 5.6 shard_map.314
  250.4 5.2 all-to-all-start
  255.7 4.3 broadcast_in_dim.77
  261.5 9.6 %collective-permute-done.12 = bf16[2,256,2048]{2,1,0:T(8,128)(2,1)} collective-permute-done((bf16[2,256,2048]{2,1,0:T(8,128)(2,1)}, bf16[2,256,2048]{2,1,0:T(8,128)(2,1)}, u32[]{:S(2)}, u32[]{:S(2)}) %collective-permute-start.12) | collective-permute-done | bytes 2097184 | tf_op jit(solution)/shard_map/ppermute | solution.py:24
  279.1 11.0 %all-to-all-done = bf16[4,512,512]{2,1,0:T(8,128)(2,1)} async-done(((bf16[4,512,512]{2,1,0:T(8,128)(2,1)}), bf16[4,512,512]{2,1,0:T(8,128)(2,1)}, u32[]{:S(2)}, u32[]{:S(2)}) %all-to-all-start) | async-done | bytes 2097184 | tf_op jit(solution)/shard_map/all_to_all | solution.py:648
  291.8 7.8 fusion.97
  321.0 36.7 %collective-permute-done.17 = bf16[4,256,1024]{2,1,0:T(8,128)(2,1)S(1)} collective-permute-done((bf16[4,256,1024]{2,1,0:T(8,128)(2,1)S(1)}, bf16[4,256,1024]{2,1,0:T(8,128)(2,1)S(1)}, u32[]{:S(2)}, u32[]{:S(2)}) %collective-permute-start.17) | collective-permute-done | bytes 2097184 | tf_op jit(solution)/shard_map/ppermute | solution.py:24
  362.8 14.3 %shard_map.316 = (bf16[512,1024]{1,0:T(8,128)(2,1)S(1)}, bf16[512,1024]{1,0:T(8,128)(2,1)S(1)}, bf16[512,2048]{1,0:T(8,128)(2,1)S(1)}, bf16[512,2048]{1,0:T(8,128)(2,1)}, f32[1,1024]{1,0:T(1,128)S(1)}) custom-call(bf16[512,2048]{1,0:T(8,128)(2,1)} %pad_maximum_fusion.14.normed_ref, bf16[512,2048]{1,0:T(8,128)(2,1)} %pad_maximum_fusion.15.cotangent_ref, ...), custom_call_target="tpu_custom_call" | custom-call | flops 8589934592 | bytes 8388608 | tf_op jit(solution)/shard_map/pallas_call | solution.py:424
  383.2 14.4 %shard_map.317 = (bf16[512,1024]{1,0:T(8,128)(2,1)S(1)}, bf16[512,1024]{1,0:T(8,128)(2,1)S(1)}, bf16[512,2048]{1,0:T(8,128)(2,1)S(1)}, bf16[512,2048]{1,0:T(8,128)(2,1)}, f32[1,1024]{1,0:T(1,128)S(1)}) custom-call(bf16[512,2048]{1,0:T(8,128)(2,1)} %pad_maximum_fusion.16.normed_ref, bf16[512,2048]{1,0:T(8,128)(2,1)} %pad_maximum_fusion.17.cotangent_ref, ...), custom_call_target="tpu_custom_call" | custom-call | flops 8589934592 | bytes 8388608 | tf_op jit(solution)/shard_map/pallas_call | solution.py:424
  400.3 5.9 fusion.21
  410.8 24.3 %collective-permute-done.25 = bf16[256,2048]{1,0:T(8,128)(2,1)S(1)} collective-permute-done((bf16[256,2048]{1,0:T(8,128)(2,1)S(1)}, bf16[256,2048]{1,0:T(8,128)(2,1)S(1)}, u32[]{:S(2)}, u32[]{:S(2)}) %collective-permute-start.25) | collective-permute-done | bytes 1048608 | tf_op jit(solution)/shard_map/ppermute | solution.py:24
  448.3 9.1 %convolution_convert_fusion.3 = bf16[512,2048]{1,0:T(8,128)(2,1)S(1)} fusion(bf16[2048,2048]{1,0:T(8,128)(2,1)} %bitcast.40, bf16[256,2048]{1,0:T(8,128)(2,1)S(1)} %get-tuple-element.300, bf16[256,2048]{1,0:T(8,128)(2,1)S(1)} %get-tuple-element.299), kind=kOutput, calls=%fused_computation.53 | convolution fusion | flops 4300210176 | bytes 12582912 | tf_op jit(solution)/shard_map/dot_general | solution.py:19
  457.5 7.2 convolution_convert_fusion
  466.5 4.4 all-to-all-start.1
  482.1 6.2 fusion.18
  498.7 29.5 %collective-permute-done.27 = bf16[2,256,2048]{2,1,0:T(8,128)(2,1)} collective-permute-done((bf16[2,256,2048]{2,1,0:T(8,128)(2,1)}, bf16[2,256,2048]{2,1,0:T(8,128)(2,1)}, u32[]{:S(2)}, u32[]{:S(2)}) %collective-permute-start.27) | collective-permute-done | bytes 2097184 | tf_op jit(solution)/shard_map/ppermute | solution.py:24
  528.2 9.9 %collective-permute-done.28 = bf16[2,256,2048]{2,1,0:T(8,128)(2,1)} collective-permute-done((bf16[2,256,2048]{2,1,0:T(8,128)(2,1)}, bf16[2,256,2048]{2,1,0:T(8,128)(2,1)}, u32[]{:S(2)}, u32[]{:S(2)}) %collective-permute-start.28) | collective-permute-done | bytes 2097184 | tf_op jit(solution)/shard_map/ppermute | solution.py:24
  553.6 12.4 %shard_map.319 = (f32[1024,256]{1,0:T(8,128)S(1)}, bf16[1024,512]{1,0:T(8,128)(2,1)S(1)}, f32[1024,768]{1,0:T(8,128)}, f32[1024,768]{1,0:T(8,128)}, f32[1,512]{1,0:T(1,128)S(1)}, /*index=5*/f32[1,512]{1,0:T(1,128)S(1)}) custom-call(s32[2]{0:T(128)S(1)} %pad_add_fusion.place_ref, s32[3]{0:T(128)S(1)} %bitcast_subtract_fusion.starts_ref, f32[1]{0:T(128)} %bitcast.3.decay_ref, ...), custom_call_target="tpu_custom_call" | custom-call | flops 4697620480 | bytes 16777216 | tf_op jit(solution)/shard_map/pallas_call | solution.py:357
  571.2 12.3 %shard_map.318 = (f32[1024,256]{1,0:T(8,128)S(1)}, bf16[1024,512]{1,0:T(8,128)(2,1)S(1)}, f32[1024,768]{1,0:T(8,128)}, f32[1024,768]{1,0:T(8,128)}, f32[1,512]{1,0:T(1,128)S(1)}, /*index=5*/f32[1,512]{1,0:T(1,128)S(1)}) custom-call(s32[2]{0:T(128)S(1)} %pad_add_fusion.1.place_ref, s32[3]{0:T(128)S(1)} %bitcast_subtract_fusion.starts_ref, ...), custom_call_target="tpu_custom_call" | custom-call | flops 4697620480 | bytes 16777216 | tf_op jit(solution)/shard_map/pallas_call | solution.py:357
  591.0 4.1 fusion.56
  595.2 4.5 add_convert_fusion.17
  618.1 20.7 %multiply_reduce_fusion.1 = (f32[2048]{0:T(1024)S(1)}, bf16[2048,1536]{1,0:T(8,128)(2,1)}) fusion(bf16[4,2,256,1536]{3,2,1,0:T(8,128)(2,1)} %copy-done.34, bf16[1024,1536]{1,0:T(8,128)(2,1)} %copy-done.86, bf16[1024,1536]{1,0:T(8,128)(2,1)} %constant_dynamic-update-slice_fusion, bf16[1024,2048]{1,0:T(8,128)(2,1)} %copy-done.62, bf16[1024,2048]{1,0:T(8,128)(2,1)} %copy-done.61), kind=kOutput, calls=%fused_computation.2 | convolution fusion | flops 12929988608 | bytes 27271168 | tf_op jit(solution)/shard_map/dot_general | solution.py:19
  645.1 10.7 %convolution_convert_fusion.2 = bf16[1024,2048]{1,0:T(8,128)(2,1)} fusion(bf16[2048,1536]{1,0:T(8,128)(2,1)} %bitcast.257, s32[]{:T(128)S(6)} %select_n.687, bf16[1024,1536]{1,0:T(8,128)(2,1)} %constant_dynamic-update-slice_fusion, bf16[1024,1536]{1,0:T(8,128)(2,1)S(1)} %copy-done.87), kind=kOutput, calls=%fused_computation.38 | convolution fusion | flops 6450839552 | bytes 16777220 | tf_op jit(solution)/shard_map/dot_general | solution.py:19
  658.6 4.3 collective-permute-done.40
  662.9 4.3 collective-permute-done.41
  683.1 7.4 collective-permute-done.42
  690.6 5.1 collective-permute-done.43
  707.2 10.2 %collective-permute-done.44 = bf16[256,2048]{1,0:T(8,128)(2,1)S(1)} collective-permute-done((bf16[256,2048]{1,0:T(8,128)(2,1)S(1)}, bf16[256,2048]{1,0:T(8,128)(2,1)S(1)}, u32[]{:S(2)}, u32[]{:S(2)}) %collective-permute-start.44) | collective-permute-done | bytes 1048608 | tf_op jit(solution)/shard_map/ppermute | solution.py:126
  717.4 4.2 collective-permute-done.45
  726.7 12.5 %fusion.140 = (bf16[1024,2048]{1,0:T(8,128)(2,1)}, f32[1024,2048]{1,0:T(8,128)}) fusion(bf16[1024,2048]{1,0:T(8,128)(2,1)} %collective-permute-done.34, bf16[2048,1536]{1,0:T(8,128)(2,1)S(1)} %bitcast.262, s32[]{:T(128)S(6)} %select_n.686, bf16[1024,1536]{1,0:T(8,128)(2,1)} %constant_dynamic-update-slice_fusion, bf16[1024,1536]{1,0:T(8,128)(2,1)} %copy-done.86), kind=kOutput, calls=%fused_computation.384 | convolution fusion | flops 6455033856 | bytes 29360132 | tf_op jit(solution)/shard_map/dot_general | solution.py:19
  754.7 16.6 %collective-permute-done.59 = bf16[2,256,1536]{2,1,0:T(8,128)(2,1)S(1)} collective-permute-done((bf16[2,256,1536]{2,1,0:T(8,128)(2,1)}, bf16[2,256,1536]{2,1,0:T(8,128)(2,1)S(1)}, u32[]{:S(2)}, u32[]{:S(2)}) %collective-permute-start.59) | collective-permute-done | bytes 1572896 | tf_op jit(solution)/shard_map/ppermute | solution.py:24
  778.6 4.6 collective-permute-start.50
  784.8 4.2 convert_add_fusion.11
  795.5 4.5 collective-permute-done.51
  805.6 4.9 add_convert_fusion.3
  (681 shorter events, 345.5 us)
Async XLA Ops:
  7.2 102.1 %all-gather.3.cloned.1.call-start = ((), (), s32[]{:S(2)}) async-start(), calls=%async_computation.2 | async-start | bytes 5242880 | tf_op jit(solution)/shard_map/all_gather | solution.py:515
  53.2 35.9 %collective-permute-start.3 = (bf16[2,256,1536]{2,1,0:T(8,128)(2,1)}, bf16[2,256,1536]{2,1,0:T(8,128)(2,1)}, u32[]{:S(2)}, u32[]{:S(2)}) collective-permute-start(bf16[2,256,1536]{2,1,0:T(8,128)(2,1)} %pad_maximum_fusion.24), channel_id=1, source_target_pairs={{0,8},{4,12},{8,0},{12,4},{16,24},{20,28},{24,16},{28,20},{1,9},{5... | collective-permute-start | bytes 4718600 | tf_op jit(solution)/shard_map/ppermute | solution.py:24
  53.7 35.7 %collective-permute-start.4 = (bf16[2,256,1536]{2,1,0:T(8,128)(2,1)}, bf16[2,256,1536]{2,1,0:T(8,128)(2,1)}, u32[]{:S(2)}, u32[]{:S(2)}) collective-permute-start(bf16[2,256,1536]{2,1,0:T(8,128)(2,1)} %pad_maximum_fusion.26), channel_id=1, source_target_pairs={{0,16},{4,20},{8,24},{12,28},{16,0},{20,4},{24,8},{28,12},{1,17},{... | collective-permute-start | bytes 4718600 | tf_op jit(solution)/shard_map/ppermute | solution.py:24
  89.4 46.0 %collective-permute-start.7 = (bf16[2,256,2048]{2,1,0:T(8,128)(2,1)}, bf16[2,256,2048]{2,1,0:T(8,128)(2,1)}, u32[]{:S(2)}, u32[]{:S(2)}) collective-permute-start(bf16[2,256,2048]{2,1,0:T(8,128)(2,1)} %pad_maximum_fusion.12), channel_id=1, source_target_pairs={{0,8},{4,12},{8,0},{12,4},{16,24},{20,28},{24,16},{28,20},{1,9},{5... | collective-permute-start | bytes 6291464 | tf_op jit(solution)/shard_map/ppermute | solution.py:24
  90.9 45.7 %collective-permute-start.8 = (bf16[512,2048]{1,0:T(8,128)(2,1)}, bf16[512,2048]{1,0:T(8,128)(2,1)}, u32[]{:S(2)}, u32[]{:S(2)}) collective-permute-start(bf16[512,2048]{1,0:T(8,128)(2,1)} %param.33), channel_id=1, source_target_pairs={{0,16},{4,20},{8,24},{12,28},{16,0},{20,4},{24,8},{28,12},{1,17},{... | collective-permute-start | bytes 6291464 | tf_op jit(solution)/shard_map/ppermute | solution.py:24
  109.3 35.4 %collective-permute-start.5 = (bf16[1024,2048]{1,0:T(8,128)(2,1)}, bf16[1024,2048]{1,0:T(8,128)(2,1)S(1)}, u32[]{:S(2)}, u32[]{:S(2)}) collective-permute-start(bf16[1024,2048]{1,0:T(8,128)(2,1)} %all-gather.3.cloned.1.call-done), channel_id=1, source_target_pairs={{0,4},{4,0},{8,12},{12,8},{16,20},{20,16},{24,28},{28,24},{1,5},{5... | collective-permute-start | bytes 12582920 | tf_op jit(solution)/shard_map/ppermute | solution.py:24
  166.7 26.0 %collective-permute-start.9 = (bf16[256,2048]{1,0:T(8,128)(2,1)S(1)}, bf16[256,2048]{1,0:T(8,128)(2,1)S(1)}, u32[]{:S(2)}, u32[]{:S(2)}) collective-permute-start(bf16[256,2048]{1,0:T(8,128)(2,1)S(1)} %copy-done.119), channel_id=1, source_target_pairs={{0,8},{4,12},{8,0},{12,4},{16,24},{20,28},{24,16},{28,20},{1,9},{5... | collective-permute-start | bytes 3145736 | tf_op jit(solution)/shard_map/ppermute | solution.py:24
  167.5 25.2 %collective-permute-start.10 = (bf16[256,2048]{1,0:T(8,128)(2,1)S(1)}, bf16[256,2048]{1,0:T(8,128)(2,1)S(1)}, u32[]{:S(2)}, u32[]{:S(2)}) collective-permute-start(bf16[256,2048]{1,0:T(8,128)(2,1)S(1)} %copy-done.118), channel_id=1, source_target_pairs={{0,16},{4,20},{8,24},{12,28},{16,0},{20,4},{24,8},{28,12},{1,17},{... | collective-permute-start | bytes 3145736 | tf_op jit(solution)/shard_map/ppermute | solution.py:24
  176.9 61.0 %collective-permute-start.6 = (bf16[1024,768]{1,0:T(8,128)(2,1)}, bf16[1024,768]{1,0:T(8,128)(2,1)}, u32[]{:S(2)}, u32[]{:S(2)}) collective-permute-start(bf16[1024,768]{1,0:T(8,128)(2,1)} %pad_maximum_fusion.27), channel_id=1, source_target_pairs={{0,8},{4,12},{8,16},{12,20},{16,24},{20,28},{1,9},{5,13},{9,17},{1... | collective-permute-start | bytes 4718600 | tf_op jit(solution)/shard_map/ppermute | solution.py:29
  196.2 74.9 %collective-permute-start.12 = (bf16[2,256,2048]{2,1,0:T(8,128)(2,1)}, bf16[2,256,2048]{2,1,0:T(8,128)(2,1)}, u32[]{:S(2)}, u32[]{:S(2)}) collective-permute-start(bf16[2,256,2048]{2,1,0:T(8,128)(2,1)} %pad_maximum_fusion.9), channel_id=1, source_target_pairs={{0,8},{4,12},{8,0},{12,4},{16,24},{20,28},{24,16},{28,20},{1,9},{5... | collective-permute-start | bytes 6291464 | tf_op jit(solution)/shard_map/ppermute | solution.py:24
  204.2 70.1 %collective-permute-start.13 = (bf16[2,256,2048]{2,1,0:T(8,128)(2,1)}, bf16[2,256,2048]{2,1,0:T(8,128)(2,1)}, u32[]{:S(2)}, u32[]{:S(2)}) collective-permute-start(bf16[2,256,2048]{2,1,0:T(8,128)(2,1)} %pad_maximum_fusion.6), channel_id=1, source_target_pairs={{0,16},{4,20},{8,24},{12,28},{16,0},{20,4},{24,8},{28,12},{1,17},{... | collective-permute-start | bytes 6291464 | tf_op jit(solution)/shard_map/ppermute | solution.py:24
  250.4 39.7 %all-to-all-start = ((bf16[4,512,512]{2,1,0:T(8,128)(2,1)}), bf16[4,512,512]{2,1,0:T(8,128)(2,1)}, u32[]{:S(2)}, u32[]{:S(2)}) async-start(bf16[4,512,512]{2,1,0:T(8,128)(2,1)} %pad_maximum_fusion.10), calls=%async_computation | async-start | bytes 4194304 | tf_op jit(solution)/shard_map/all_to_all | solution.py:648
  255.6 46.8 %collective-permute-start.16 = (bf16[256,2048]{1,0:T(8,128)(2,1)S(1)}, bf16[256,2048]{1,0:T(8,128)(2,1)}, u32[]{:S(2)}, u32[]{:S(2)}) collective-permute-start(bf16[256,2048]{1,0:T(8,128)(2,1)S(1)} %copy-done.40), channel_id=1, source_target_pairs={{0,4},{4,0},{8,12},{12,8},{16,20},{20,16},{24,28},{28,24},{1,5},{5... | collective-permute-start | bytes 3145736 | tf_op jit(solution)/shard_map/ppermute | solution.py:24
  308.4 49.3 %collective-permute-start.17 = (bf16[4,256,1024]{2,1,0:T(8,128)(2,1)S(1)}, bf16[4,256,1024]{2,1,0:T(8,128)(2,1)S(1)}, u32[]{:S(2)}, u32[]{:S(2)}) collective-permute-start(bf16[4,256,1024]{2,1,0:T(8,128)(2,1)S(1)} %copy-done.104), channel_id=1, source_target_pairs={{0,16},{4,20},{8,24},{12,28},{16,0},{20,4},{24,8},{28,12},{1,17},{... | collective-permute-start | bytes 6291464 | tf_op jit(solution)/shard_map/ppermute | solution.py:24
  318.7 42.3 %collective-permute-start.19 = (bf16[256,2048]{1,0:T(8,128)(2,1)S(1)}, bf16[256,2048]{1,0:T(8,128)(2,1)S(1)}, u32[]{:S(2)}, u32[]{:S(2)}) collective-permute-start(bf16[256,2048]{1,0:T(8,128)(2,1)S(1)} %add_convert_fusion.22), channel_id=1, source_target_pairs={{0,8},{4,12},{8,0},{12,4},{16,24},{20,28},{24,16},{28,20},{1,9},{5... | collective-permute-start | bytes 3145736 | tf_op jit(solution)/shard_map/ppermute | solution.py:24
  319.3 41.7 %collective-permute-start.15 = (bf16[256,2048]{1,0:T(8,128)(2,1)S(1)}, bf16[256,2048]{1,0:T(8,128)(2,1)S(1)}, u32[]{:S(2)}, u32[]{:S(2)}) collective-permute-start(bf16[256,2048]{1,0:T(8,128)(2,1)S(1)} %add_convert_fusion.22), channel_id=1, source_target_pairs={{0,4},{4,0},{8,12},{12,8},{16,20},{20,16},{24,28},{28,24},{1,5},{5... | collective-permute-start | bytes 3145736 | tf_op jit(solution)/shard_map/ppermute | solution.py:24
  381.1 29.6 %collective-permute-start.23 = (bf16[256,2048]{1,0:T(8,128)(2,1)}, bf16[256,2048]{1,0:T(8,128)(2,1)}, u32[]{:S(2)}, u32[]{:S(2)}) collective-permute-start(bf16[256,2048]{1,0:T(8,128)(2,1)} %slice.450), channel_id=1, source_target_pairs={{0,4},{4,0},{8,12},{12,8},{16,20},{20,16},{24,28},{28,24},{1,5},{5... | collective-permute-start | bytes 3145736 | tf_op jit(solution)/shard_map/ppermute | solution.py:24
  409.8 25.3 %collective-permute-start.25 = (bf16[256,2048]{1,0:T(8,128)(2,1)S(1)}, bf16[256,2048]{1,0:T(8,128)(2,1)S(1)}, u32[]{:S(2)}, u32[]{:S(2)}) collective-permute-start(bf16[256,2048]{1,0:T(8,128)(2,1)S(1)} %add_convert_fusion.20), channel_id=1, source_target_pairs={{0,8},{4,12},{8,0},{12,4},{16,24},{20,28},{24,16},{28,20},{1,9},{5... | collective-permute-start | bytes 3145736 | tf_op jit(solution)/shard_map/ppermute | solution.py:24
  444.8 46.9 %collective-permute-start.22 = (bf16[256,2048]{1,0:T(8,128)(2,1)}, bf16[256,2048]{1,0:T(8,128)(2,1)}, u32[]{:S(2)}, u32[]{:S(2)}) collective-permute-start(bf16[256,2048]{1,0:T(8,128)(2,1)} %slice.448), channel_id=1, source_target_pairs={{0,4},{4,0},{8,12},{12,8},{16,20},{20,16},{24,28},{28,24},{1,5},{5... | collective-permute-start | bytes 3145736 | tf_op jit(solution)/shard_map/ppermute | solution.py:24
  445.2 49.1 %collective-permute-start.35 = (bf16[512,2048]{1,0:T(8,128)(2,1)}, bf16[512,2048]{1,0:T(8,128)(2,1)}, u32[]{:S(2)}, u32[]{:S(2)}) collective-permute-start(bf16[512,2048]{1,0:T(8,128)(2,1)} %dynamic-slice_bitcast_fusion), channel_id=1, source_target_pairs={{0,16},{4,20},{8,24},{12,28},{16,0},{20,4},{24,8},{28,12},{1,17},{... | collective-permute-start | bytes 6291464 | tf_op jit(solution)/shard_map/ppermute | solution.py:24
  466.5 77.5 %all-to-all-start.1 = ((bf16[4,512,512]{2,1,0:T(8,128)(2,1)}), bf16[4,512,512]{2,1,0:T(8,128)(2,1)}, u32[]{:S(2)}, u32[]{:S(2)}) async-start(bf16[4,512,512]{2,1,0:T(8,128)(2,1)} %pad_maximum_fusion.21), calls=%async_computation.1 | async-start | bytes 4194304 | tf_op jit(solution)/shard_map/all_to_all | solution.py:648
  480.5 47.7 %collective-permute-start.27 = (bf16[2,256,2048]{2,1,0:T(8,128)(2,1)}, bf16[2,256,2048]{2,1,0:T(8,128)(2,1)}, u32[]{:S(2)}, u32[]{:S(2)}) collective-permute-start(bf16[2,256,2048]{2,1,0:T(8,128)(2,1)} %pad_maximum_fusion.19), channel_id=1, source_target_pairs={{0,8},{4,12},{8,0},{12,4},{16,24},{20,28},{24,16},{28,20},{1,9},{5... | collective-permute-start | bytes 6291464 | tf_op jit(solution)/shard_map/ppermute | solution.py:24
  481.0 57.1 %collective-permute-start.28 = (bf16[2,256,2048]{2,1,0:T(8,128)(2,1)}, bf16[2,256,2048]{2,1,0:T(8,128)(2,1)}, u32[]{:S(2)}, u32[]{:S(2)}) collective-permute-start(bf16[2,256,2048]{2,1,0:T(8,128)(2,1)} %pad_maximum_fusion.20), channel_id=1, source_target_pairs={{0,16},{4,20},{8,24},{12,28},{16,0},{20,4},{24,8},{28,12},{1,17},{... | collective-permute-start | bytes 6291464 | tf_op jit(solution)/shard_map/ppermute | solution.py:24
  547.2 48.0 %collective-permute-start.36 = (bf16[256,2048]{1,0:T(8,128)(2,1)}, bf16[256,2048]{1,0:T(8,128)(2,1)}, u32[]{:S(2)}, u32[]{:S(2)}) collective-permute-start(bf16[256,2048]{1,0:T(8,128)(2,1)} %get-tuple-element.186), channel_id=1, source_target_pairs={{0,1},{4,5},{8,9},{12,13},{16,17},{20,21},{24,25},{28,29}} | collective-permute-start | bytes 3145736 | tf_op jit(solution)/shard_map/ppermute | solution.py:126
  549.5 45.7 %collective-permute-start.37 = (bf16[256,2048]{1,0:T(8,128)(2,1)}, bf16[256,2048]{1,0:T(8,128)(2,1)}, u32[]{:S(2)}, u32[]{:S(2)}) collective-permute-start(bf16[256,2048]{1,0:T(8,128)(2,1)} %get-tuple-element.186), channel_id=1, source_target_pairs={{3,2},{7,6},{11,10},{15,14},{19,18},{23,22},{27,26},{31,30}} | collective-permute-start | bytes 3145736 | tf_op jit(solution)/shard_map/ppermute | solution.py:126
  551.3 39.8 %collective-permute-start.29 = (bf16[256,2048]{1,0:T(8,128)(2,1)}, bf16[256,2048]{1,0:T(8,128)(2,1)}, u32[]{:S(2)}, u32[]{:S(2)}) collective-permute-start(bf16[256,2048]{1,0:T(8,128)(2,1)} %fusion.60), channel_id=1, source_target_pairs={{0,8},{4,12},{8,0},{12,4},{16,24},{20,28},{24,16},{28,20},{1,9},{5... | collective-permute-start | bytes 3145736 | tf_op jit(solution)/shard_map/ppermute | solution.py:24
  552.2 38.8 %collective-permute-start.30 = (bf16[256,2048]{1,0:T(8,128)(2,1)}, bf16[256,2048]{1,0:T(8,128)(2,1)}, u32[]{:S(2)}, u32[]{:S(2)}) collective-permute-start(bf16[256,2048]{1,0:T(8,128)(2,1)} %fusion.59), channel_id=1, source_target_pairs={{0,16},{4,20},{8,24},{12,28},{16,0},{20,4},{24,8},{28,12},{1,17},{... | collective-permute-start | bytes 3145736 | tf_op jit(solution)/shard_map/ppermute | solution.py:24
  569.7 41.8 %collective-permute-start.33 = (bf16[1024,768]{1,0:T(8,128)(2,1)}, bf16[1024,768]{1,0:T(8,128)(2,1)}, u32[]{:S(2)}, u32[]{:S(2)}) collective-permute-start(bf16[1024,768]{1,0:T(8,128)(2,1)} %convert_element_type.538), channel_id=1, source_target_pairs={{8,0},{12,4},{16,8},{20,12},{24,16},{28,20},{9,1},{13,5},{17,9},{2... | collective-permute-start | bytes 4718600 | tf_op jit(solution)/shard_map/ppermute | solution.py:29
  599.8 77.0 %collective-permute-start.31 = (bf16[256,2048]{1,0:T(8,128)(2,1)}, bf16[256,2048]{1,0:T(8,128)(2,1)}, u32[]{:S(2)}, u32[]{:S(2)}) collective-permute-start(bf16[256,2048]{1,0:T(8,128)(2,1)} %add_convert_fusion.21), channel_id=1, source_target_pairs={{0,8},{4,12},{8,0},{12,4},{16,24},{20,28},{24,16},{28,20},{1,9},{5... | collective-permute-start | bytes 3145736 | tf_op jit(solution)/shard_map/ppermute | solution.py:24
  602.4 36.4 %collective-permute-start.38 = (bf16[256,2048]{1,0:T(8,128)(2,1)}, bf16[256,2048]{1,0:T(8,128)(2,1)S(1)}, u32[]{:S(2)}, u32[]{:S(2)}) collective-permute-start(bf16[256,2048]{1,0:T(8,128)(2,1)} %get-tuple-element.188), channel_id=1, source_target_pairs={{0,1},{1,2},{4,5},{5,6},{8,9},{9,10},{12,13},{13,14},{16,17},{17,1... | collective-permute-start | bytes 3145736 | tf_op jit(solution)/shard_map/ppermute | solution.py:126
  603.8 35.0 %collective-permute-start.39 = (bf16[256,2048]{1,0:T(8,128)(2,1)}, bf16[256,2048]{1,0:T(8,128)(2,1)}, u32[]{:S(2)}, u32[]{:S(2)}) collective-permute-start(bf16[256,2048]{1,0:T(8,128)(2,1)} %get-tuple-element.189), channel_id=1, source_target_pairs={{3,2},{2,1},{7,6},{6,5},{11,10},{10,9},{15,14},{14,13},{19,18},{18... | collective-permute-start | bytes 3145736 | tf_op jit(solution)/shard_map/ppermute | solution.py:126
  605.8 71.0 %collective-permute-start.32 = (bf16[4,256,1024]{2,1,0:T(8,128)(2,1)}, bf16[4,256,1024]{2,1,0:T(8,128)(2,1)}, u32[]{:S(2)}, u32[]{:S(2)}) collective-permute-start(bf16[4,256,1024]{2,1,0:T(8,128)(2,1)} %dynamic-slice_bitcast_fusion.1), channel_id=1, source_target_pairs={{0,16},{4,20},{8,24},{12,28},{16,0},{20,4},{24,8},{28,12},{1,17},{... | collective-permute-start | bytes 6291464 | tf_op jit(solution)/shard_map/ppermute | solution.py:24
  641.9 21.0 %collective-permute-start.40 = (bf16[256,2048]{1,0:T(8,128)(2,1)S(1)}, bf16[256,2048]{1,0:T(8,128)(2,1)S(1)}, u32[]{:S(2)}, u32[]{:S(2)}) collective-permute-start(bf16[256,2048]{1,0:T(8,128)(2,1)S(1)} %get-tuple-element.190), channel_id=1, source_target_pairs={{0,1},{1,2},{2,3},{4,5},{5,6},{6,7},{8,9},{9,10},{10,11},{12,13},{... | collective-permute-start | bytes 3145736 | tf_op jit(solution)/shard_map/ppermute | solution.py:126
  643.5 23.7 %collective-permute-start.41 = (bf16[256,2048]{1,0:T(8,128)(2,1)S(1)}, bf16[256,2048]{1,0:T(8,128)(2,1)S(1)}, u32[]{:S(2)}, u32[]{:S(2)}) collective-permute-start(bf16[256,2048]{1,0:T(8,128)(2,1)S(1)} %get-tuple-element.191), channel_id=1, source_target_pairs={{3,2},{2,1},{1,0},{7,6},{6,5},{5,4},{11,10},{10,9},{9,8},{15,14},{... | collective-permute-start | bytes 3145736 | tf_op jit(solution)/shard_map/ppermute | solution.py:126
  655.8 70.9 %collective-permute-start.34 = (bf16[1024,2048]{1,0:T(8,128)(2,1)}, bf16[1024,2048]{1,0:T(8,128)(2,1)}, u32[]{:S(2)}, u32[]{:S(2)}) collective-permute-start(bf16[1024,2048]{1,0:T(8,128)(2,1)} %convolution_convert_fusion.2), channel_id=1, source_target_pairs={{0,4},{4,0},{8,12},{12,8},{16,20},{20,16},{24,28},{28,24},{1,5},{5... | collective-permute-start | bytes 12582920 | tf_op jit(solution)/shard_map/ppermute | solution.py:24
  669.6 20.9 %collective-permute-start.42 = (bf16[256,2048]{1,0:T(8,128)(2,1)}, bf16[256,2048]{1,0:T(8,128)(2,1)}, u32[]{:S(2)}, u32[]{:S(2)}) collective-permute-start(bf16[256,2048]{1,0:T(8,128)(2,1)} %get-tuple-element.192), channel_id=1, source_target_pairs={{0,1},{1,2},{2,3},{4,5},{5,6},{6,7},{8,9},{9,10},{10,11},{12,13},{... | collective-permute-start | bytes 3145736 | tf_op jit(solution)/shard_map/ppermute | solution.py:126
  673.3 22.3 %collective-permute-start.43 = (bf16[256,2048]{1,0:T(8,128)(2,1)}, bf16[256,2048]{1,0:T(8,128)(2,1)}, u32[]{:S(2)}, u32[]{:S(2)}) collective-permute-start(bf16[256,2048]{1,0:T(8,128)(2,1)} %get-tuple-element.193), channel_id=1, source_target_pairs={{3,2},{2,1},{1,0},{7,6},{6,5},{5,4},{11,10},{10,9},{9,8},{15,14},{... | collective-permute-start | bytes 3145736 | tf_op jit(solution)/shard_map/ppermute | solution.py:126
  676.7 74.7 %collective-permute-start.18 = (bf16[256,2048]{1,0:T(8,128)(2,1)}, bf16[256,2048]{1,0:T(8,128)(2,1)}, u32[]{:S(2)}, u32[]{:S(2)}) collective-permute-start(bf16[256,2048]{1,0:T(8,128)(2,1)} %slice.445), channel_id=1, source_target_pairs={{0,4},{4,0},{8,12},{12,8},{16,20},{20,16},{24,28},{28,24},{1,5},{5... | collective-permute-start | bytes 3145736 | tf_op jit(solution)/shard_map/ppermute | solution.py:24
  701.0 20.5 %collective-permute-start.45 = (bf16[256,2048]{1,0:T(8,128)(2,1)S(1)}, bf16[256,2048]{1,0:T(8,128)(2,1)S(1)}, u32[]{:S(2)}, u32[]{:S(2)}) collective-permute-start(bf16[256,2048]{1,0:T(8,128)(2,1)S(1)} %get-tuple-element.195), channel_id=1, source_target_pairs={{3,2},{2,1},{1,0},{7,6},{6,5},{5,4},{11,10},{10,9},{9,8},{15,14},{... | collective-permute-start | bytes 3145736 | tf_op jit(solution)/shard_map/ppermute | solution.py:126
  722.7 21.3 %collective-permute-start.46 = (bf16[256,2048]{1,0:T(8,128)(2,1)S(1)}, bf16[256,2048]{1,0:T(8,128)(2,1)S(1)}, u32[]{:S(2)}, u32[]{:S(2)}) collective-permute-start(bf16[256,2048]{1,0:T(8,128)(2,1)S(1)} %get-tuple-element.196), channel_id=1, source_target_pairs={{0,1},{1,2},{2,3},{4,5},{5,6},{6,7},{8,9},{9,10},{10,11},{12,13},{... | collective-permute-start | bytes 3145736 | tf_op jit(solution)/shard_map/ppermute | solution.py:126
  739.2 32.0 %collective-permute-start.59 = (bf16[2,256,1536]{2,1,0:T(8,128)(2,1)}, bf16[2,256,1536]{2,1,0:T(8,128)(2,1)S(1)}, u32[]{:S(2)}, u32[]{:S(2)}) collective-permute-start(bf16[2,256,1536]{2,1,0:T(8,128)(2,1)} %pad_maximum_fusion.28), channel_id=1, source_target_pairs={{0,8},{4,12},{8,0},{12,4},{16,24},{20,28},{24,16},{28,20},{1,9},{5... | collective-permute-start | bytes 4718600 | tf_op jit(solution)/shard_map/ppermute | solution.py:24
  741.0 32.3 %collective-permute-start.60 = (bf16[2,256,1536]{2,1,0:T(8,128)(2,1)}, bf16[2,256,1536]{2,1,0:T(8,128)(2,1)S(1)}, u32[]{:S(2)}, u32[]{:S(2)}) collective-permute-start(bf16[2,256,1536]{2,1,0:T(8,128)(2,1)} %pad_maximum_fusion.29), channel_id=1, source_target_pairs={{0,16},{4,20},{8,24},{12,28},{16,0},{20,4},{24,8},{28,12},{1,17},{... | collective-permute-start | bytes 4718600 | tf_op jit(solution)/shard_map/ppermute | solution.py:24
  746.1 30.9 %collective-permute-start.48 = (bf16[256,2048]{1,0:T(8,128)(2,1)S(1)}, bf16[256,2048]{1,0:T(8,128)(2,1)S(1)}, u32[]{:S(2)}, u32[]{:S(2)}) collective-permute-start(bf16[256,2048]{1,0:T(8,128)(2,1)S(1)} %get-tuple-element.199), channel_id=1, source_target_pairs={{0,1},{1,2},{2,3},{4,5},{5,6},{6,7},{8,9},{9,10},{10,11},{12,13},{... | collective-permute-start | bytes 3145736 | tf_op jit(solution)/shard_map/ppermute | solution.py:126
  750.2 26.8 %collective-permute-start.49 = (bf16[256,2048]{1,0:T(8,128)(2,1)S(1)}, bf16[256,2048]{1,0:T(8,128)(2,1)S(1)}, u32[]{:S(2)}, u32[]{:S(2)}) collective-permute-start(bf16[256,2048]{1,0:T(8,128)(2,1)S(1)} %get-tuple-element.200), channel_id=1, source_target_pairs={{3,2},{2,1},{1,0},{7,6},{6,5},{5,4},{11,10},{10,9},{9,8},{15,14},{... | collective-permute-start | bytes 3145736 | tf_op jit(solution)/shard_map/ppermute | solution.py:126
  793.0 31.4 %collective-permute-start.63 = (bf16[256,1536]{1,0:T(8,128)(2,1)}, bf16[256,1536]{1,0:T(8,128)(2,1)}, u32[]{:S(2)}, u32[]{:S(2)}) collective-permute-start(bf16[256,1536]{1,0:T(8,128)(2,1)} %select_convert_fusion), channel_id=1, source_target_pairs={{0,4},{4,0},{8,12},{12,8},{16,20},{20,16},{24,28},{28,24},{1,5},{5... | collective-permute-start | bytes 2359304 | tf_op jit(solution)/shard_map/ppermute | solution.py:24
  812.9 22.6 %collective-permute-start.52 = (bf16[256,2048]{1,0:T(8,128)(2,1)}, bf16[256,2048]{1,0:T(8,128)(2,1)S(1)}, u32[]{:S(2)}, u32[]{:S(2)}) collective-permute-start(bf16[256,2048]{1,0:T(8,128)(2,1)} %get-tuple-element.203), channel_id=1, source_target_pairs={{0,1},{1,2},{2,3},{4,5},{5,6},{6,7},{8,9},{9,10},{10,11},{12,13},{... | collective-permute-start | bytes 3145736 | tf_op jit(solution)/shard_map/ppermute | solution.py:126
  816.4 23.2 %collective-permute-start.53 = (bf16[256,2048]{1,0:T(8,128)(2,1)}, bf16[256,2048]{1,0:T(8,128)(2,1)S(1)}, u32[]{:S(2)}, u32[]{:S(2)}) collective-permute-start(bf16[256,2048]{1,0:T(8,128)(2,1)} %get-tuple-element.204), channel_id=1, source_target_pairs={{3,2},{2,1},{1,0},{7,6},{6,5},{5,4},{11,10},{10,9},{9,8},{15,14},{... | collective-permute-start | bytes 3145736 | tf_op jit(solution)/shard_map/ppermute | solution.py:126
  821.0 32.6 %collective-permute-start.64 = (bf16[2,256,1024]{2,1,0:T(8,128)(2,1)}, bf16[2,256,1024]{2,1,0:T(8,128)(2,1)S(1)}, u32[]{:S(2)}, u32[]{:S(2)}) collective-permute-start(bf16[2,256,1024]{2,1,0:T(8,128)(2,1)} %pad_maximum_fusion.36), channel_id=1, source_target_pairs={{0,8},{4,12},{8,0},{12,4},{16,24},{20,28},{24,16},{28,20},{1,9},{5... | collective-permute-start | bytes 3145736 | tf_op jit(solution)/shard_map/ppermute | solution.py:24
  (183 other events, 2073.5 us)
Sparse Core Ops, SparseCore 0:
  28.2 81.0 all-gather.2
